TPU v7x, 512 devices: a whole 4x8x8 slice. The times are simulated.
512 devices in a mesh: dp: 16 (over y, core), tensor: 32 (over x, z).
Axes of the slice: x: 4, y: 8, z: 8, core: 2. Of those that a mesh axis runs over, the one named last changes fastest.
Arguments:
- residual: bfloat16 [4096, 4608], P('tensor', 'dp'), may hold values from -6 to 6
- picked: int32 [512], P('tensor'), may hold values from 0 to 4095, as said below
- enc_weight: bfloat16 [4608, 32768], P('dp', 'tensor'), may hold values from -0.09375 to 0.09375
- enc_bias: float32 [32768], P('tensor'), may hold values from -3 to 3
- dec_weight: bfloat16 [32768, 4608], P('tensor', 'dp'), may hold values from -0.0234375 to 0.0234375
- dec_bias: float32 [4608], P('dp'), may hold values from -3 to 3
Outputs:
- enc_grad: float32 [4608, 32768], P('dp', 'tensor')
- bias_grad: float32 [32768], P('tensor')
- dec_grad: float32 [32768, 4608], P('tensor', 'dp')
Inputs may be any that keep to these rules, and one draw needn't show every extreme that they name: The entries of the aligned block k of 16 rows of picked are distinct tokens of k * 128 to (k + 1) * 128 - 1.
All inputs are finite; a program needn't handle non-finite values.
Results may differ from a plain program's by a relative error of at most 0.0039.
Values may be sent and summed in bfloat16 or wider, within the bound.
No kernel may reach another device: no remote copies, remote signals or barrier semaphores. Data moves between devices by JAX's collectives and lax.ppermute only.
A program may use at most 64 MiB of HBM per device.

v0:
```python
import jax
import jax.numpy as jnp
from jax import lax
from jax.sharding import PartitionSpec as P

ROWS = 512


def body(residual, picked, enc_weight, enc_bias, dec_weight, dec_bias):
    sharpness = 8.0
    sparsity_weight = 1.0
    row_total = ROWS
    row_share = row_total // lax.axis_size("dp")
    first_token = lax.axis_index("tensor") * residual.shape[0]
    local_rows = jnp.take(residual, picked - first_token, axis=0)
    sampled = lax.all_gather(local_rows, "tensor", axis=0, tiled=True)
    centered = (sampled.astype(jnp.float32) - dec_bias).astype(jnp.bfloat16)
    dec_float = dec_weight.astype(jnp.float32)
    squares = lax.psum(jnp.sum(dec_float * dec_float, axis=1), "dp")
    row_norms = jnp.sqrt(squares + 1e-06)
    unit_rows = (dec_float / row_norms[:, None]).astype(jnp.bfloat16)
    row_offset = lax.axis_index("dp") * row_share
    partial_pre = jnp.dot(centered, enc_weight, preferred_element_type=jnp.float32)
    pre_acts = lax.psum(partial_pre, "dp") + enc_bias
    active = (jax.nn.softplus(sharpness * pre_acts) / sharpness).astype(jnp.bfloat16)
    pre_share = lax.dynamic_slice_in_dim(pre_acts, row_offset, row_share, 0)
    partial_rebuilt = jnp.dot(active, unit_rows, preferred_element_type=jnp.float32)
    rebuilt = lax.psum(partial_rebuilt, "tensor") + dec_bias
    err_grad = (2.0 / row_total * (rebuilt - sampled.astype(jnp.float32))).astype(jnp.bfloat16)
    raw_share = lax.psum_scatter(
        lax.dot_general(
            err_grad, unit_rows, (((1,), (1,)), ((), ())), preferred_element_type=jnp.float32
        ),
        "dp",
        scatter_dimension=0,
        tiled=True,
    )
    latent_share = raw_share + sparsity_weight / row_total
    grad_share = (latent_share * jax.nn.sigmoid(sharpness * pre_share)).astype(jnp.bfloat16)
    pre_grad = lax.all_gather(grad_share, "dp", axis=0, tiled=True)
    enc_grad = lax.dot_general(
        centered, pre_grad, (((0,), (0,)), ((), ())), preferred_element_type=jnp.float32
    )
    bias_grad = jnp.sum(pre_grad.astype(jnp.float32), axis=0)
    unit_grad = lax.dot_general(
        active, err_grad, (((0,), (0,)), ((), ())), preferred_element_type=jnp.float32
    )
    local_dots = jnp.sum(unit_grad * unit_rows.astype(jnp.float32), axis=1)
    dot_sums = lax.psum(local_dots, "dp")
    dec_grad = (unit_grad - unit_rows.astype(jnp.float32) * dot_sums[:, None]) / row_norms[:, None]
    return (enc_grad, bias_grad, dec_grad)


def solution(mesh):
    return jax.shard_map(
        body,
        mesh=mesh,
        in_specs=(
            P("tensor", "dp"),
            P("tensor"),
            P("dp", "tensor"),
            P("tensor"),
            P("tensor", "dp"),
            P("dp"),
        ),
        out_specs=(P("dp", "tensor"), P("tensor"), P("tensor", "dp")),
        check_vma=False,
    )
```

profile of v0, /device:TPU:1, one launch (start us, length us, event | category | flops | bytes accessed | tf_op | source)
XLA Modules:
  0.0 466.1 jit_solution(8462125067208819731)
XLA Ops:
  7.2 0.0 all-reduce.3.cloned.1.call-start
  7.2 0.7 compare_and_fusion
  8.0 1.0 copy.11
  9.0 0.6 gather_fusion
  9.6 0.1 broadcast_select_fusion
  9.6 44.2 %all_gather.6 = bf16[512,288]{1,0:T(8,128)(2,1)S(1)} all-gather(bf16[16,288]{1,0:T(8,128)(2,1)S(1)} %broadcast_select_fusion), channel_id=1, replica_groups=mesh['dp'=16,'tensor'=32] {'tensor'}, dimensions={0}, use_global_device_ids=true | all-gather | bytes 304128 | tf_op jit(solution)/shard_map/all_gather | solution.py:16
  53.9 0.2 copy.12
  54.1 2.1 fusion.12
  56.2 0.0 all-reduce.3.cloned.1.call-update
  56.2 0.0 all-reduce.5.cloned.1.call-start
  56.3 1.0 copy-done.2
  57.3 0.1 fusion.2
  57.4 36.4 %psum.29 = f32[1024]{0:T(1024)S(1)} all-reduce(f32[1024]{0:T(1024)S(1)} %fusion.2), channel_id=1, replica_groups=mesh['dp'=16,'tensor'=32] {'dp'}, use_global_device_ids=true, to_apply=%region_2.3 | all-reduce | flops 1024 | bytes 8192 | tf_op jit(solution)/shard_map/psum | solution.py:19
  93.8 91.3 %all-reduce.3.cloned.1.call-done = f32[512,1024]{1,0:T(8,128)} async-done(((f32[512,1024]{1,0:T(8,128)}), f32[512,1024]{1,0:T(8,128)}) %all-reduce.3.cloned.1.call-update) | async-done | bytes 2097168 | tf_op jit(solution)/shard_map/psum | solution.py:24
  185.1 3.1 fusion.1
  188.2 1.0 copy-done.6
  189.2 1.3 fusion.16
  190.5 0.0 all-reduce.5.cloned.1.call-update
  190.6 0.0 reduce-scatter.2.cloned.1.call-start
  190.6 155.7 %all-reduce.5.cloned.1.call-done = f32[512,288]{0,1:T(8,128)} async-done(((f32[512,288]{0,1:T(8,128)}), f32[512,288]{0,1:T(8,128)}) %all-reduce.5.cloned.1.call-update) | async-done | bytes 589840 | tf_op jit(solution)/shard_map/psum | solution.py:28
  346.3 1.3 fusion.9
  347.6 2.1 fusion.14
  349.7 0.0 reduce-scatter.2.cloned.1.call-update
  349.7 0.0 all-gather.2.cloned.1.call-start
  349.7 61.5 %reduce-scatter.2.cloned.1.call-done = f32[32,1024]{1,0:T(8,128)} async-done(((f32[512,1024]{1,0:T(8,128)}), f32[32,1024]{1,0:T(8,128)}) %reduce-scatter.2.cloned.1.call-update) | async-done | bytes 131088 | tf_op jit(solution)/shard_map/reduce_scatter | solution.py:30
  411.3 1.6 multiply_convert_fusion
  412.9 1.9 fusion.4
  414.8 25.7 %psum.31 = f32[1024]{0:T(1024)S(1)} all-reduce(f32[1024]{0:T(1024)S(1)} %get-tuple-element.7), channel_id=1, replica_groups=mesh['dp'=16,'tensor'=32] {'dp'}, use_global_device_ids=true, to_apply=%region_7.8 | all-reduce | flops 1024 | bytes 8192 | tf_op jit(solution)/shard_map/psum | solution.py:49
  440.5 1.3 fusion.6
  441.8 14.1 %all-gather.2.cloned.1.call-done = bf16[512,1024]{1,0:T(8,128)(2,1)} async-done(((bf16[32,1024]{1,0:T(8,128)(2,1)}), bf16[512,1024]{1,0:T(8,128)(2,1)}) %all-gather.2.cloned.1.call-update) | async-done | bytes 1048592 | tf_op jit(solution)/shard_map/all_gather | solution.py:40
  455.9 2.1 convert_reduce_fusion
  458.0 1.5 fusion.10
  (19 shorter events, 0.1 us)
Async XLA Ops:
  7.2 46.9 %copy-start = (bf16[288,1024]{1,0:T(8,128)(2,1)S(1)}, bf16[288,1024]{1,0:T(8,128)(2,1)}, u32[]{:S(2)}) copy-start(bf16[288,1024]{1,0:T(8,128)(2,1)} %param.8) | copy-start | bytes 1769476
  7.2 46.9 %copy-start.7 = (f32[288]{0:T(512)S(1)}, f32[288]{0:T(512)}, u32[]{:S(2)}) copy-start(f32[288]{0:T(512)} %param.11) | copy-start | bytes 3460
  7.2 178.0 %all-reduce.3.cloned.1.call-start = ((), (), s32[]{:S(2)}) async-start(), calls=%async_computation.1 | async-start | bytes 4194304 | tf_op jit(solution)/shard_map/psum | solution.py:24
  56.2 1.1 copy-start.2
  56.2 129.0 %copy-start.8 = (f32[1024]{0:T(1024)S(1)}, f32[1024]{0:T(1024)}, u32[]{:S(2)}) copy-start(f32[1024]{0:T(1024)} %param.9) | copy-start | bytes 12292
  56.2 290.1 %all-reduce.5.cloned.1.call-start = ((), (), s32[]{:S(2)}) async-start(), calls=%async_computation.2 | async-start | bytes 1179648 | tf_op jit(solution)/shard_map/psum | solution.py:28
  185.1 4.1 copy-start.3
  188.2 1.0 copy-start.6
  190.6 220.7 %reduce-scatter.2.cloned.1.call-start = ((), (), s32[]{:S(2)}) async-start(), calls=%async_computation.3 | async-start | bytes 2228224 | tf_op jit(solution)/shard_map/reduce_scatter | solution.py:30
  346.3 1.3 copy-start.4
  349.7 106.2 %all-gather.2.cloned.1.call-start = ((), (), s32[]{:S(2)}) async-start(), calls=%async_computation.4 | async-start | bytes 1114112 | tf_op jit(solution)/shard_map/all_gather | solution.py:40
  412.9 27.7 %copy-start.5 = (bf16[1024,288]{0,1:T(8,128)(2,1)S(1)}, bf16[1024,288]{0,1:T(8,128)(2,1)}, u32[]{:S(2)}) copy-start(bf16[1024,288]{0,1:T(8,128)(2,1)} %param.10) | copy-start | bytes 1769476
  455.9 2.1 copy-start.1
Sparse Core Ops, SparseCore 0:
  56.3 128.7 all-reduce.2
  190.7 155.5 all-reduce.4
  349.8 61.3 reduce-scatter.1
  414.0 41.8 all-gather.1
where the time goes:
time: 466 us
  waiting for transfers between devices  323 us (69%)
  blocking collectives  106 us (23%)
  between operations  13.9 us (3%)
  other arithmetic  10.2 us (2%)
  matrix products  9.01 us (2%)
    psum x1, waiting for transfers between devices, body(): rebuilt = lax.psum(partial_rebuilt, 'tensor') + dec_bias  156 us
    psum x1, waiting for transfers between devices, body(): pre_acts = lax.psum(partial_pre, 'dp') + enc_bias  91.3 us
    reduce_scatter x1, waiting for transfers between devices, body(): lax.psum_scatter(lax.dot_general(err_grad, unit_rows, (((1,), (1,)), ((),...  61.5 us
    all_gather x1, blocking collectives, body(): sampled = lax.all_gather(local_rows, 'tensor', axis=0, tiled=True)  44.2 us
    psum x1, blocking collectives, body(): squares = lax.psum(jnp.sum(dec_float * dec_float, axis=1), 'dp')  36.4 us
    psum x1, blocking collectives, body(): dot_sums = lax.psum(local_dots, 'dp')  25.7 us
    all_gather x1, waiting for transfers between devices, body(): pre_grad = lax.all_gather(grad_share, 'dp', axis=0, tiled=True)  14.1 us
  transfers between devices with their start and end apart: 4, of which 4 were waited for; matrix products, arithmetic and copies ran while one was open for 1% of the time, Pallas kernels for 0%

commit v1 on v0

v1 whole, which is shorter than its diff:
```python
import jax
import jax.numpy as jnp
from jax import lax
from jax.sharding import Mesh
from jax.sharding import PartitionSpec as P

ROWS = 512
TENSOR = ("x", "z")
F32 = jnp.float32
BF16 = jnp.bfloat16


def exchange(blocks, axis):
    return lax.all_to_all(blocks, axis, 0, 0, tiled=False)


def gather(block, axis):
    count = lax.axis_size(axis)
    return exchange(jnp.broadcast_to(block[None], (count,) + block.shape), axis)


def swap(block):
    return lax.ppermute(block, "core", [(0, 1), (1, 0)])


def split(value):
    high = lax.reduce_precision(value, 8, 7)
    return jnp.stack([high, value - high]).astype(BF16)


def rows_of(value):
    return jnp.pad(split(value), ((0, 6), (0, 0)))


def merge(rows):
    return rows[..., 0, :].astype(F32) + rows[..., 1, :].astype(F32)


def body(residual, picked, enc_weight, enc_bias, dec_weight, dec_bias):
    sharpness = 8.0
    first = lax.axis_index("core") == 0
    half = enc_weight.shape[1] // 2
    count_y = lax.axis_size("y")
    share = ROWS // count_y

    def mine(value):
        return jnp.where(first, value[..., :half], value[..., half:])

    def other(value):
        return jnp.where(first, value[..., half:], value[..., :half])

    def join(own, its):
        low = jnp.where(first, own, its)
        high = jnp.where(first, its, own)
        return jnp.concatenate([low, high], axis=-1)

    first_token = lax.axis_index(TENSOR) * residual.shape[0]
    local_rows = jnp.take(residual, picked - first_token, axis=0)
    sampled = gather(local_rows, TENSOR).reshape(ROWS, -1)
    centered = (sampled.astype(F32) - dec_bias).astype(BF16)
    dec_float = dec_weight.astype(F32)
    squares = jnp.sum(dec_float * dec_float, axis=1)

    def reduce_rows(partial, extra):
        sent = other(partial).astype(BF16)
        if extra is not None:
            sent = jnp.concatenate([sent, rows_of(other(extra))])
        got = swap(sent)
        total = (mine(partial) + got[:ROWS].astype(F32)).astype(BF16)
        total = total.reshape(count_y, share, half)
        if extra is not None:
            extra = mine(extra) + merge(got[ROWS:])
            rows = jnp.broadcast_to(rows_of(extra)[None], (count_y, 8, half))
            total = jnp.concatenate([total, rows], axis=1)
        blocks = exchange(total, "y")
        result = jnp.sum(blocks[:, :share].astype(F32), axis=0)
        if extra is None:
            return result, None
        return result, jnp.sum(merge(blocks[:, share:]), axis=0)

    partial_pre = jnp.dot(centered, enc_weight, preferred_element_type=F32)
    pre_share, squares = reduce_rows(partial_pre, squares)
    pre_share = pre_share + mine(enc_bias)
    norms_half = jnp.sqrt(squares + 1e-06)
    active_share = (jax.nn.softplus(sharpness * pre_share) / sharpness).astype(BF16)
    active_half = gather(active_share, "y").reshape(ROWS, half)
    got = swap(jnp.concatenate([active_half, rows_of(norms_half)]))
    active = join(active_half, got[:ROWS])
    row_norms = join(norms_half, merge(got[ROWS:]))
    unit_rows = (dec_float / row_norms[:, None]).astype(BF16)
    partial_rebuilt = jnp.dot(active, unit_rows, preferred_element_type=F32)
    count_t = lax.axis_size(TENSOR)
    blocks = exchange(
        partial_rebuilt.astype(BF16).reshape(count_t, ROWS // count_t, -1), TENSOR
    )
    rebuilt_share = jnp.sum(blocks.astype(F32), axis=0) + dec_bias
    err_share = (2.0 / ROWS * (rebuilt_share - local_rows.astype(F32))).astype(BF16)
    err_grad = gather(err_share, TENSOR).reshape(ROWS, -1)
    partial_raw = lax.dot_general(
        err_grad, unit_rows, (((1,), (1,)), ((), ())), preferred_element_type=F32
    )
    raw_share, _ = reduce_rows(partial_raw, None)
    grad_share = ((raw_share + 1.0 / ROWS) * jax.nn.sigmoid(sharpness * pre_share)).astype(BF16)
    dots_share = jnp.sum(active_share.astype(F32) * raw_share, axis=0)
    blocks = gather(jnp.concatenate([grad_share, rows_of(dots_share)]), "y")
    grad_half = blocks[:, :share].reshape(ROWS, half)
    dots_half = jnp.sum(merge(blocks[:, share:]), axis=0)
    got = swap(jnp.concatenate([grad_half, rows_of(dots_half)]))
    pre_grad = join(grad_half, got[:ROWS])
    dot_sums = join(dots_half, merge(got[ROWS:]))
    enc_grad = lax.dot_general(
        centered, pre_grad, (((0,), (0,)), ((), ())), preferred_element_type=F32
    )
    bias_grad = jnp.sum(pre_grad.astype(F32), axis=0)
    unit_grad = lax.dot_general(
        active, err_grad, (((0,), (0,)), ((), ())), preferred_element_type=F32
    )
    dec_grad = (unit_grad - unit_rows.astype(F32) * dot_sums[:, None]) / row_norms[:, None]
    return (enc_grad, bias_grad, dec_grad)


def solution(mesh):
    grid = Mesh(mesh.devices.reshape(8, 2, 4, 8), ("y", "core", "x", "z"))
    dp = ("y", "core")
    return jax.shard_map(
        body,
        mesh=grid,
        in_specs=(
            P(TENSOR, dp),
            P(TENSOR),
            P(dp, TENSOR),
            P(TENSOR),
            P(TENSOR, dp),
            P(dp),
        ),
        out_specs=(P(dp, TENSOR), P(TENSOR), P(TENSOR, dp)),
        check_vma=False,
    )
```

time: 466 us -> 188 us (0.40)
  waiting for transfers between devices: 323 us -> 54.6 us
  starting transfers between devices: 0.16 us -> 41.8 us
  blocking collectives: 106 us -> 76.1 us
  between operations: 13.9 us -> 1.01 us
  other arithmetic: 10.2 us -> 4.69 us
    psum x2 -> x0, waiting for transfers between devices: 247 us -> none  [the longest x1 156 us: body(): rebuilt = lax.psum(partial_rebuilt, 'tensor') + dec_bias]
    all_to_all x0 -> x4, blocking collectives: none -> 76.1 us  [exchange(): return lax.all_to_all(blocks, axis, 0, 0, tiled=False)]
    psum x2 -> x0, blocking collectives: 62.1 us -> none  [the longest x1 36.4 us: body(): squares = lax.psum(jnp.sum(dec_float * dec_float, axis=1), 'dp')]
    reduce_scatter x1 -> x0, waiting for transfers between devices: 61.5 us -> none  [body(): lax.psum_scatter(lax.dot_general(err_grad, unit_rows, (((1,), (1,)), ((),...]
    all_to_all x0 -> x3, waiting for transfers between devices: none -> 48.6 us  [exchange(): return lax.all_to_all(blocks, axis, 0, 0, tiled=False)]
    all_gather x1 -> x0, blocking collectives: 44.2 us -> none  [body(): sampled = lax.all_gather(local_rows, 'tensor', axis=0, tiled=True)]
    all_to_all x0 -> x3, starting transfers between devices: none -> 24 us  [exchange(): return lax.all_to_all(blocks, axis, 0, 0, tiled=False)]
    ppermute x0 -> x4, starting transfers between devices: none -> 17.7 us  [swap(): return lax.ppermute(block, 'core', [(0, 1), (1, 0)])]
  transfers between devices with their start and end apart: 4 -> 7, of which waited for: 4 -> 7; matrix products, arithmetic and copies ran while one was open for 1% -> 0% of each run, Pallas kernels for 0% -> 0%
where the time goes in v1:
time: 188 us
  blocking collectives  76.1 us (40%)
  waiting for transfers between devices  54.6 us (29%)
  starting transfers between devices  41.8 us (22%)
  matrix products  4.98 us (3%)
  other arithmetic  4.69 us (2%)
  local copies, waits for them, and re-layouts  4.39 us (2%)
    all_to_all x4, blocking collectives, exchange(): return lax.all_to_all(blocks, axis, 0, 0, tiled=False)  76.1 us
    all_to_all x3, waiting for transfers between devices, exchange(): return lax.all_to_all(blocks, axis, 0, 0, tiled=False)  48.6 us
    all_to_all x3, starting transfers between devices, exchange(): return lax.all_to_all(blocks, axis, 0, 0, tiled=False)  24 us
    ppermute x4, starting transfers between devices, swap(): return lax.ppermute(block, 'core', [(0, 1), (1, 0)])  17.7 us
    ppermute x4, waiting for transfers between devices, swap(): return lax.ppermute(block, 'core', [(0, 1), (1, 0)])  6.09 us
  transfers between devices with their start and end apart: 7, of which 7 were waited for; matrix products, arithmetic and copies ran while one was open for 0% of the time, Pallas kernels for 0%

profile of v1, /device:TPU:1, one launch (start us, length us, event | category | flops | bytes accessed | tf_op | source)
XLA Modules:
  0.0 187.6 jit_solution(3500636520376028390)
XLA Ops:
  0.7 0.8 compare_and_fusion
  1.4 1.0 copy.10
  2.4 0.6 gather_fusion
  3.1 0.8 broadcast_in_dim.25
  3.9 13.7 %all-to-all-start = ((bf16[32,16,288]{2,1,0:T(8,128)(2,1)}), bf16[32,16,288]{2,1,0:T(8,128)(2,1)S(1)}, u32[]{:S(2)}, u32[]{:S(2)}) async-start(bf16[32,16,288]{2,1,0:T(8,128)(2,1)} %broadcast_in_dim.25), calls=%async_computation | async-start | bytes 786432 | tf_op jit(solution)/shard_map/all_to_all | solution.py:14
  17.8 11.4 %all-to-all-done = bf16[32,16,288]{2,1,0:T(8,128)(2,1)S(1)} async-done(((bf16[32,16,288]{2,1,0:T(8,128)(2,1)}), bf16[32,16,288]{2,1,0:T(8,128)(2,1)S(1)}, u32[]{:S(2)}, u32[]{:S(2)}) %all-to-all-start) | async-done | bytes 294944 | tf_op jit(solution)/shard_map/all_to_all | solution.py:14
  29.4 0.7 fusion.40
  30.3 5.7 %collective-permute-start = (bf16[520,512]{1,0:T(8,128)(2,1)S(1)}, bf16[520,512]{1,0:T(8,128)(2,1)S(1)}, u32[]{:S(2)}, u32[]{:S(2)}) collective-permute-start(bf16[520,512]{1,0:T(8,128)(2,1)S(1)} %pad_maximum_fusion.6), channel_id=1, source_target_pairs={{0,32},{32,0},{1,33},{33,1},{2,34},{34,2},{3,35},{35,3},{4,36},{36... | collective-permute-start | bytes 1597448 | tf_op jit(solution)/shard_map/ppermute | solution.py:23
  36.0 1.5 collective-permute-done
  37.9 0.9 pad_maximum_fusion.5
  38.8 6.8 %all-to-all-start.1 = ((bf16[8,72,512]{2,1,0:T(8,128)(2,1)}), bf16[8,72,512]{2,1,0:T(8,128)(2,1)S(1)}, u32[]{:S(2)}, u32[]{:S(2)}) async-start(bf16[8,72,512]{2,1,0:T(8,128)(2,1)} %pad_maximum_fusion.5), calls=%async_computation.1 | async-start | bytes 1179648 | tf_op jit(solution)/shard_map/all_to_all | solution.py:14
  45.6 19.3 %all-to-all-done.1 = bf16[8,72,512]{2,1,0:T(8,128)(2,1)S(1)} async-done(((bf16[8,72,512]{2,1,0:T(8,128)(2,1)}), bf16[8,72,512]{2,1,0:T(8,128)(2,1)S(1)}, u32[]{:S(2)}, u32[]{:S(2)}) %all-to-all-start.1) | async-done | bytes 589856 | tf_op jit(solution)/shard_map/all_to_all | solution.py:14
  65.2 0.8 broadcast_in_dim.27
  66.0 3.5 %all-to-all-start.2 = ((bf16[8,64,512]{2,1,0:T(8,128)(2,1)}), bf16[8,64,512]{2,1,0:T(8,128)(2,1)S(1)}, u32[]{:S(2)}, u32[]{:S(2)}) async-start(bf16[8,64,512]{2,1,0:T(8,128)(2,1)} %broadcast_in_dim.27), calls=%async_computation.2 | async-start | bytes 1048576 | tf_op jit(solution)/shard_map/all_to_all | solution.py:14
  69.6 17.8 %all-to-all-done.2 = bf16[8,64,512]{2,1,0:T(8,128)(2,1)S(1)} async-done(((bf16[8,64,512]{2,1,0:T(8,128)(2,1)}), bf16[8,64,512]{2,1,0:T(8,128)(2,1)S(1)}, u32[]{:S(2)}, u32[]{:S(2)}) %all-to-all-start.2) | async-done | bytes 524320 | tf_op jit(solution)/shard_map/all_to_all | solution.py:14
  87.4 2.4 %collective-permute-start.1 = (bf16[520,512]{1,0:T(8,128)(2,1)S(1)}, bf16[520,512]{1,0:T(8,128)(2,1)S(1)}, u32[]{:S(2)}, u32[]{:S(2)}) collective-permute-start(bf16[520,512]{1,0:T(8,128)(2,1)S(1)} %pad_maximum_fusion.7), channel_id=1, source_target_pairs={{0,32},{32,0},{1,33},{33,1},{2,34},{34,2},{3,35},{35,3},{4,36},{36... | collective-permute-start | bytes 1597448 | tf_op jit(solution)/shard_map/ppermute | solution.py:23
  89.8 1.5 collective-permute-done.1
  91.5 0.8 copy-done.2
  92.3 0.5 convolution_convert_fusion
  93.0 16.4 %all_to_all.35 = bf16[32,16,288]{2,1,0:T(8,128)(2,1)S(1)} all-to-all(bf16[32,16,288]{2,1,0:T(8,128)(2,1)S(1)} %bitcast.28), channel_id=1, replica_groups=mesh['y'=8,'core'=2,'x'=4,'z'=8] {'x','z'}, dimensions={0} | all-to-all | bytes 589824 | tf_op jit(solution)/shard_map/all_to_all | solution.py:14
  109.7 18.2 %all_to_all.36 = bf16[32,16,288]{2,1,0:T(8,128)(2,1)S(1)} all-to-all(bf16[32,16,288]{2,1,0:T(8,128)(2,1)S(1)} %broadcast_in_dim.28), channel_id=1, replica_groups=mesh['y'=8,'core'=2,'x'=4,'z'=8] {'x','z'}, dimensions={0} | all-to-all | bytes 589824 | tf_op jit(solution)/shard_map/all_to_all | solution.py:14
  127.8 0.7 fusion.37
  128.7 6.5 %collective-permute-start.2 = (bf16[512,512]{1,0:T(8,128)(2,1)S(1)}, bf16[512,512]{1,0:T(8,128)(2,1)S(1)}, u32[]{:S(2)}, u32[]{:S(2)}) collective-permute-start(bf16[512,512]{1,0:T(8,128)(2,1)S(1)} %select_convert_fusion), channel_id=1, source_target_pairs={{0,32},{32,0},{1,33},{33,1},{2,34},{34,2},{3,35},{35,3},{4,36},{36... | collective-permute-start | bytes 1572872 | tf_op jit(solution)/shard_map/ppermute | solution.py:23
  135.2 1.5 collective-permute-done.2
  136.7 0.3 add_convert_fusion
  137.1 20.4 %all_to_all.37 = bf16[8,64,512]{2,1,0:T(8,128)(2,1)S(1)} all-to-all(bf16[8,64,512]{2,1,0:T(8,128)(2,1)S(1)} %bitcast.27), channel_id=1, replica_groups=mesh['y'=8,'core'=2,'x'=4,'z'=8] {'y'}, dimensions={0} | all-to-all | bytes 1048576 | tf_op jit(solution)/shard_map/all_to_all | solution.py:14
  157.7 21.1 %all_to_all.38 = bf16[8,72,512]{2,1,0:T(8,128)(2,1)S(1)} all-to-all(bf16[8,72,512]{2,1,0:T(8,128)(2,1)S(1)} %broadcast_in_dim.29), channel_id=1, replica_groups=mesh['y'=8,'core'=2,'x'=4,'z'=8] {'y'}, dimensions={0} | all-to-all | bytes 1179648 | tf_op jit(solution)/shard_map/all_to_all | solution.py:14
  179.0 3.1 %collective-permute-start.3 = (bf16[520,512]{1,0:T(8,128)(2,1)S(1)}, bf16[520,512]{1,0:T(8,128)(2,1)S(1)}, u32[]{:S(2)}, u32[]{:S(2)}) collective-permute-start(bf16[520,512]{1,0:T(8,128)(2,1)S(1)} %pad_maximum_fusion.8), channel_id=1, source_target_pairs={{0,32},{32,0},{1,33},{33,1},{2,34},{34,2},{3,35},{35,3},{4,36},{36... | collective-permute-start | bytes 1597448 | tf_op jit(solution)/shard_map/ppermute | solution.py:23
  182.1 1.5 collective-permute-done.3
  183.7 0.8 convert_reduce_fusion
  184.5 1.5 fusion.4
  186.0 1.6 fusion
  (61 shorter events, 2.4 us)
Async XLA Ops:
  0.6 28.8 %copy-start = (bf16[288,1024]{1,0:T(8,128)(2,1)S(1)}, bf16[288,1024]{1,0:T(8,128)(2,1)}, u32[]{:S(2)}) copy-start(bf16[288,1024]{1,0:T(8,128)(2,1)} %param.8) | copy-start | bytes 1769476
  0.6 17.0 %copy-start.1 = (bf16[1024,288]{0,1:T(8,128)(2,1)S(1)}, bf16[1024,288]{0,1:T(8,128)(2,1)}, u32[]{:S(2)}) copy-start(bf16[1024,288]{0,1:T(8,128)(2,1)} %param.10) | copy-start | bytes 1769476
  0.7 28.6 %copy-start.4 = (f32[288]{0:T(512)S(1)}, f32[288]{0:T(512)}, u32[]{:S(2)}) copy-start(f32[288]{0:T(512)} %param.11) | copy-start | bytes 3460
  3.9 25.4 %all-to-all-start = ((bf16[32,16,288]{2,1,0:T(8,128)(2,1)}), bf16[32,16,288]{2,1,0:T(8,128)(2,1)S(1)}, u32[]{:S(2)}, u32[]{:S(2)}) async-start(bf16[32,16,288]{2,1,0:T(8,128)(2,1)} %broadcast_in_dim.25), calls=%async_computation | async-start | bytes 786432 | tf_op jit(solution)/shard_map/all_to_all | solution.py:14
  30.3 7.3 %collective-permute-start = (bf16[520,512]{1,0:T(8,128)(2,1)S(1)}, bf16[520,512]{1,0:T(8,128)(2,1)S(1)}, u32[]{:S(2)}, u32[]{:S(2)}) collective-permute-start(bf16[520,512]{1,0:T(8,128)(2,1)S(1)} %pad_maximum_fusion.6), channel_id=1, source_target_pairs={{0,32},{32,0},{1,33},{33,1},{2,34},{34,2},{3,35},{35,3},{4,36},{36... | collective-permute-start | bytes 1597448 | tf_op jit(solution)/shard_map/ppermute | solution.py:23
  37.9 7.7 %copy-start.5 = (f32[1024]{0:T(1024)S(1)}, f32[1024]{0:T(1024)}, u32[]{:S(2)}) copy-start(f32[1024]{0:T(1024)} %param.9) | copy-start | bytes 12292
  38.8 26.2 %all-to-all-start.1 = ((bf16[8,72,512]{2,1,0:T(8,128)(2,1)}), bf16[8,72,512]{2,1,0:T(8,128)(2,1)S(1)}, u32[]{:S(2)}, u32[]{:S(2)}) async-start(bf16[8,72,512]{2,1,0:T(8,128)(2,1)} %pad_maximum_fusion.5), calls=%async_computation.1 | async-start | bytes 1179648 | tf_op jit(solution)/shard_map/all_to_all | solution.py:14
  66.0 21.4 %all-to-all-start.2 = ((bf16[8,64,512]{2,1,0:T(8,128)(2,1)}), bf16[8,64,512]{2,1,0:T(8,128)(2,1)S(1)}, u32[]{:S(2)}, u32[]{:S(2)}) async-start(bf16[8,64,512]{2,1,0:T(8,128)(2,1)} %broadcast_in_dim.27), calls=%async_computation.2 | async-start | bytes 1048576 | tf_op jit(solution)/shard_map/all_to_all | solution.py:14
  87.4 3.9 %collective-permute-start.1 = (bf16[520,512]{1,0:T(8,128)(2,1)S(1)}, bf16[520,512]{1,0:T(8,128)(2,1)S(1)}, u32[]{:S(2)}, u32[]{:S(2)}) collective-permute-start(bf16[520,512]{1,0:T(8,128)(2,1)S(1)} %pad_maximum_fusion.7), channel_id=1, source_target_pairs={{0,32},{32,0},{1,33},{33,1},{2,34},{34,2},{3,35},{35,3},{4,36},{36... | collective-permute-start | bytes 1597448 | tf_op jit(solution)/shard_map/ppermute | solution.py:23
  91.5 0.8 copy-start.2
  128.7 8.1 %collective-permute-start.2 = (bf16[512,512]{1,0:T(8,128)(2,1)S(1)}, bf16[512,512]{1,0:T(8,128)(2,1)S(1)}, u32[]{:S(2)}, u32[]{:S(2)}) collective-permute-start(bf16[512,512]{1,0:T(8,128)(2,1)S(1)} %select_convert_fusion), channel_id=1, source_target_pairs={{0,32},{32,0},{1,33},{33,1},{2,34},{34,2},{3,35},{35,3},{4,36},{36... | collective-permute-start | bytes 1572872 | tf_op jit(solution)/shard_map/ppermute | solution.py:23
  179.0 4.6 %collective-permute-start.3 = (bf16[520,512]{1,0:T(8,128)(2,1)S(1)}, bf16[520,512]{1,0:T(8,128)(2,1)S(1)}, u32[]{:S(2)}, u32[]{:S(2)}) collective-permute-start(bf16[520,512]{1,0:T(8,128)(2,1)S(1)} %pad_maximum_fusion.8), channel_id=1, source_target_pairs={{0,32},{32,0},{1,33},{33,1},{2,34},{34,2},{3,35},{35,3},{4,36},{36... | collective-permute-start | bytes 1597448 | tf_op jit(solution)/shard_map/ppermute | solution.py:23
  184.5 1.5 copy-start.3

commit v2 on v1

v2 whole, which is shorter than its diff:
```python
import jax
import jax.numpy as jnp
from jax import lax
from jax.sharding import Mesh
from jax.sharding import PartitionSpec as P

ROWS = 512
TENSOR = ("x", "z")
F32 = jnp.float32
BF16 = jnp.bfloat16


def exchange(blocks, axis):
    return lax.all_to_all(blocks, axis, 0, 0, tiled=False)


def gather(block, axis):
    count = lax.axis_size(axis)
    return exchange(jnp.broadcast_to(block[None], (count,) + block.shape), axis)


def swap(block):
    return lax.ppermute(block, "core", [(0, 1), (1, 0)])


def rows_of(value):
    high = lax.reduce_precision(value, 8, 7)
    return jnp.pad(jnp.stack([high, value - high]).astype(BF16), ((0, 6), (0, 0)))


def merge(rows):
    return rows[..., 0, :].astype(F32) + rows[..., 1, :].astype(F32)


def dot(a, b, dims):
    return lax.dot_general(a, b, (dims, ((), ())), preferred_element_type=F32)


def body(residual, picked, enc_weight, enc_bias, dec_weight, dec_bias):
    sharpness = 8.0
    core = lax.axis_index("core")
    count_y = lax.axis_size("y")
    count_t = lax.axis_size(TENSOR)
    rows = ROWS // 2
    share = rows // count_y
    piece = rows // count_t
    latents = enc_weight.shape[1]
    width = enc_weight.shape[0]

    local_picked = picked - lax.axis_index(TENSOR) * residual.shape[0]
    both = jnp.take(residual, local_picked, axis=0).reshape(2, piece, width)
    own_rows = jnp.where(core == 0, both[0], both[1])
    other_rows = jnp.where(core == 0, both[1], both[0])
    local_rows = jnp.concatenate([own_rows, swap(other_rows)], axis=1)
    dec_t = dec_weight.T
    enc_all = jnp.concatenate([enc_weight, swap(enc_weight)], axis=0)
    dec_all = jnp.concatenate([dec_t, swap(dec_t)], axis=0)
    bias_all = jnp.concatenate([dec_bias, swap(dec_bias)], axis=0)
    dec_float = dec_all.astype(F32)
    squares = jnp.sum(dec_float * dec_float, axis=0)

    sampled = gather(local_rows, TENSOR).reshape(rows, 2 * width)
    centered = (sampled.astype(F32) - bias_all).astype(BF16)
    partial = dot(centered, enc_all, ((1,), (0,))).astype(BF16)
    extra = jnp.broadcast_to(rows_of(squares)[None], (count_y, 8, latents))
    blocks = jnp.concatenate([partial.reshape(count_y, share, latents), extra], axis=1)
    blocks = exchange(blocks, "y")
    pre_share = jnp.sum(blocks[:, :share].astype(F32), axis=0) + enc_bias
    row_norms = jnp.sqrt(jnp.sum(merge(blocks[:, share:]), axis=0) + 1e-06)
    active_share = (jax.nn.softplus(sharpness * pre_share) / sharpness).astype(BF16)
    active = gather(active_share, "y").reshape(rows, latents)
    unit_t = (dec_float / row_norms).astype(BF16)
    partial = dot(active, unit_t, ((1,), (1,))).astype(BF16)
    blocks = exchange(partial.reshape(count_t, piece, 2 * width), TENSOR)
    rebuilt_share = jnp.sum(blocks.astype(F32), axis=0) + bias_all
    err_share = (2.0 / ROWS * (rebuilt_share - local_rows.astype(F32))).astype(BF16)
    err_grad = gather(err_share, TENSOR).reshape(rows, 2 * width)
    partial = dot(err_grad, unit_t, ((1,), (0,))).astype(BF16)
    blocks = exchange(partial.reshape(count_y, share, latents), "y")
    raw_share = jnp.sum(blocks.astype(F32), axis=0)
    grad_share = ((raw_share + 1.0 / ROWS) * jax.nn.sigmoid(sharpness * pre_share)).astype(BF16)
    dots_share = jnp.sum(active_share.astype(F32) * raw_share, axis=0)
    own = gather(jnp.concatenate([grad_share, rows_of(dots_share)]), "y")
    its = swap(own)
    dot_sums = jnp.sum(merge(own[:, share:]), axis=0) + jnp.sum(merge(its[:, share:]), axis=0)
    own_grad = own[:, :share].reshape(rows, latents)
    its_grad = its[:, :share].reshape(rows, latents)
    its_centered = swap(centered[:, width:])
    its_err = swap(err_grad[:, width:])
    its_active = swap(active)
    enc_grad = dot(centered[:, :width], own_grad, ((0,), (0,))) + dot(
        its_centered, its_grad, ((0,), (0,))
    )
    bias_grad = jnp.sum(own_grad.astype(F32), axis=0) + jnp.sum(its_grad.astype(F32), axis=0)
    unit_grad = dot(err_grad[:, :width], active, ((0,), (0,))) + dot(
        its_err, its_active, ((0,), (0,))
    )
    dec_grad = (unit_grad - unit_t[:width].astype(F32) * dot_sums) / row_norms
    return (enc_grad, bias_grad, dec_grad.T)


def solution(mesh):
    grid = Mesh(mesh.devices.reshape(8, 2, 4, 8), ("y", "core", "x", "z"))
    dp = ("y", "core")
    return jax.shard_map(
        body,
        mesh=grid,
        in_specs=(
            P(TENSOR, dp),
            P(TENSOR),
            P(dp, TENSOR),
            P(TENSOR),
            P(TENSOR, dp),
            P(dp),
        ),
        out_specs=(P(dp, TENSOR), P(TENSOR), P(TENSOR, dp)),
        check_vma=False,
    )
```

time: 188 us -> 166 us (0.88)
  waiting for transfers between devices: 54.6 us -> 18.6 us
  starting transfers between devices: 41.8 us -> 52.9 us
  matrix products: 4.98 us -> 7.16 us
    all_to_all x3, waiting for transfers between devices: 48.6 us -> 17.8 us  [exchange(): return lax.all_to_all(blocks, axis, 0, 0, tiled=False)]
    ppermute x4 -> x8, starting transfers between devices: 17.7 us -> 38.3 us  [swap(): return lax.ppermute(block, 'core', [(0, 1), (1, 0)])]
    all_to_all x3, starting transfers between devices: 24 us -> 14.5 us  [exchange(): return lax.all_to_all(blocks, axis, 0, 0, tiled=False)]
    ppermute x4 -> x8, waiting for transfers between devices: 6.09 us -> 0.82 us  [swap(): return lax.ppermute(block, 'core', [(0, 1), (1, 0)])]
    dot_general x5 -> x7, matrix products: 4.98 us -> 7.16 us  [dot(): return lax.dot_general(a, b, (dims, ((), ())), preferred_element_type=F32)]
  transfers between devices with their start and end apart: 7 -> 11, of which waited for: 7 -> 4; matrix products, arithmetic and copies ran while one was open for 0% -> 3% of each run, Pallas kernels for 0% -> 0%
where the time goes in v2:
time: 166 us; the launch traced here: 165 us
  blocking collectives  76.5 us (46%)
  starting transfers between devices  52.9 us (32%)
  waiting for transfers between devices  18.6 us (11%)
  matrix products  7.16 us (4%)
  local copies, waits for them, and re-layouts  5.35 us (3%)
  other arithmetic  3.18 us (2%)
    all_to_all x4, blocking collectives, exchange(): return lax.all_to_all(blocks, axis, 0, 0, tiled=False)  76.5 us
    ppermute x8, starting transfers between devices, swap(): return lax.ppermute(block, 'core', [(0, 1), (1, 0)])  38.3 us
    all_to_all x3, waiting for transfers between devices, exchange(): return lax.all_to_all(blocks, axis, 0, 0, tiled=False)  17.8 us
    all_to_all x3, starting transfers between devices, exchange(): return lax.all_to_all(blocks, axis, 0, 0, tiled=False)  14.5 us
    dot_general x7, matrix products, dot(): return lax.dot_general(a, b, (dims, ((), ())), preferred_element_type=F32)  7.16 us
  transfers between devices with their start and end apart: 11, of which 4 were waited for; matrix products, arithmetic and copies ran while one was open for 3% of the time, Pallas kernels for 0%

profile of v2, /device:TPU:1, one launch (start us, length us, event | category | flops | bytes accessed | tf_op | source)
XLA Modules:
  0.0 164.7 jit_solution(2629358046626885457)
XLA Ops:
  0.7 0.8 compare_and_fusion
  1.4 1.0 copy.26
  2.4 0.6 gather_fusion
  3.1 8.8 %collective-permute-start = (bf16[8,288]{1,0:T(8,128)(2,1)S(1)}, bf16[8,288]{1,0:T(8,128)(2,1)S(1)}, u32[]{:S(2)}, u32[]{:S(2)}) collective-permute-start(bf16[8,288]{1,0:T(8,128)(2,1)S(1)} %get-tuple-element.8), channel_id=1, source_target_pairs={{0,32},{32,0},{1,33},{33,1},{2,34},{34,2},{3,35},{35,3},{4,36},{36... | collective-permute-start | bytes 13832 | tf_op jit(solution)/shard_map/ppermute | solution.py:23
  11.9 0.8 collective-permute-done
  12.8 0.8 broadcast_in_dim.25
  13.6 7.5 %all-to-all-start = ((bf16[32,8,576]{2,1,0:T(8,128)(2,1)}), bf16[32,8,576]{2,1,0:T(8,128)(2,1)S(1)}, u32[]{:S(2)}, u32[]{:S(2)}) async-start(bf16[32,8,576]{2,1,0:T(8,128)(2,1)} %broadcast_in_dim.25), calls=%async_computation | async-start | bytes 655360 | tf_op jit(solution)/shard_map/all_to_all | solution.py:14
  21.1 2.5 %collective-permute-start.3 = (bf16[288,1024]{1,0:T(8,128)(2,1)S(1)}, bf16[288,1024]{1,0:T(8,128)(2,1)S(1)}, u32[]{:S(2)}, u32[]{:S(2)}) collective-permute-start(bf16[288,1024]{1,0:T(8,128)(2,1)S(1)} %bitcast.32), channel_id=1, source_target_pairs={{0,32},{32,0},{1,33},{33,1},{2,34},{34,2},{3,35},{35,3},{4,36},{36... | collective-permute-start | bytes 1769480 | tf_op jit(solution)/shard_map/ppermute | solution.py:23
  23.6 1.9 %collective-permute-start.1 = (f32[288]{0:T(512)S(1)}, f32[288]{0:T(512)S(1)}, u32[]{:S(2)}, u32[]{:S(2)}) collective-permute-start(f32[288]{0:T(512)S(1)} %copy-done.2), channel_id=1, source_target_pairs={{0,32},{32,0},{1,33},{33,1},{2,34},{34,2},{3,35},{35,3},{4,36},{36... | collective-permute-start | bytes 3464 | tf_op jit(solution)/shard_map/ppermute | solution.py:23
  25.6 2.4 %collective-permute-start.2 = (bf16[288,1024]{1,0:T(8,128)(2,1)S(1)}, bf16[288,1024]{1,0:T(8,128)(2,1)}, u32[]{:S(2)}, u32[]{:S(2)}) collective-permute-start(bf16[288,1024]{1,0:T(8,128)(2,1)S(1)} %copy-done.3), channel_id=1, source_target_pairs={{0,32},{32,0},{1,33},{33,1},{2,34},{34,2},{3,35},{35,3},{4,36},{36... | collective-permute-start | bytes 1769480 | tf_op jit(solution)/shard_map/ppermute | solution.py:23
  28.1 3.5 %all-to-all-done = bf16[32,8,576]{2,1,0:T(8,128)(2,1)S(1)} async-done(((bf16[32,8,576]{2,1,0:T(8,128)(2,1)}), bf16[32,8,576]{2,1,0:T(8,128)(2,1)S(1)}, u32[]{:S(2)}, u32[]{:S(2)}) %all-to-all-start) | async-done | bytes 294944 | tf_op jit(solution)/shard_map/all_to_all | solution.py:14
  32.0 1.6 convolution_convert_fusion.1
  33.7 22.7 %all_to_all.35 = bf16[8,40,1024]{2,1,0:T(8,128)(2,1)S(1)} all-to-all(bf16[8,40,1024]{2,1,0:T(8,128)(2,1)S(1)} %pad_maximum_fusion.1), channel_id=1, replica_groups=mesh['y'=8,'core'=2,'x'=4,'z'=8] {'y'}, dimensions={0} | all-to-all | bytes 1310720 | tf_op jit(solution)/shard_map/all_to_all | solution.py:14
  56.5 0.9 broadcast_in_dim.27
  57.4 3.5 %all-to-all-start.2 = ((bf16[8,32,1024]{2,1,0:T(8,128)(2,1)}), bf16[8,32,1024]{2,1,0:T(8,128)(2,1)S(1)}, u32[]{:S(2)}, u32[]{:S(2)}) async-start(bf16[8,32,1024]{2,1,0:T(8,128)(2,1)} %broadcast_in_dim.27), calls=%async_computation.2 | async-start | bytes 1048576 | tf_op jit(solution)/shard_map/all_to_all | solution.py:14
  61.3 11.6 %all-to-all-done.2 = bf16[8,32,1024]{2,1,0:T(8,128)(2,1)S(1)} async-done(((bf16[8,32,1024]{2,1,0:T(8,128)(2,1)}), bf16[8,32,1024]{2,1,0:T(8,128)(2,1)S(1)}, u32[]{:S(2)}, u32[]{:S(2)}) %all-to-all-start.2) | async-done | bytes 524320 | tf_op jit(solution)/shard_map/all_to_all | solution.py:14
  72.9 0.5 convolution_convert_fusion.2
  73.6 23.7 %all_to_all.36 = bf16[32,8,576]{2,1,0:T(8,128)(2,1)S(1)} all-to-all(bf16[32,8,576]{2,1,0:T(8,128)(2,1)S(1)} %bitcast.38), channel_id=1, replica_groups=mesh['y'=8,'core'=2,'x'=4,'z'=8] {'x','z'}, dimensions={0} | all-to-all | bytes 589824 | tf_op jit(solution)/shard_map/all_to_all | solution.py:14
  97.5 14.7 %all_to_all.37 = bf16[32,8,576]{2,1,0:T(8,128)(2,1)S(1)} all-to-all(bf16[32,8,576]{2,1,0:T(8,128)(2,1)S(1)} %broadcast_in_dim.28), channel_id=1, replica_groups=mesh['y'=8,'core'=2,'x'=4,'z'=8] {'x','z'}, dimensions={0} | all-to-all | bytes 589824 | tf_op jit(solution)/shard_map/all_to_all | solution.py:14
  112.3 0.6 convolution_convert_fusion
  112.9 15.4 %all_to_all.38 = bf16[8,32,1024]{2,1,0:T(8,128)(2,1)S(1)} all-to-all(bf16[8,32,1024]{2,1,0:T(8,128)(2,1)S(1)} %bitcast.37), channel_id=1, replica_groups=mesh['y'=8,'core'=2,'x'=4,'z'=8] {'y'}, dimensions={0} | all-to-all | bytes 1048576 | tf_op jit(solution)/shard_map/all_to_all | solution.py:14
  128.6 0.9 broadcast_in_dim.29
  129.5 3.5 %all-to-all-start.6 = ((bf16[8,40,1024]{2,1,0:T(8,128)(2,1)}), bf16[8,40,1024]{2,1,0:T(8,128)(2,1)S(1)}, u32[]{:S(2)}, u32[]{:S(2)}) async-start(bf16[8,40,1024]{2,1,0:T(8,128)(2,1)} %broadcast_in_dim.29), calls=%async_computation.6 | async-start | bytes 1310720 | tf_op jit(solution)/shard_map/all_to_all | solution.py:14
  133.1 8.9 %collective-permute-start.4 = (bf16[256,288]{1,0:T(8,128)(2,1)S(1)}, bf16[256,288]{1,0:T(8,128)(2,1)S(1)}, u32[]{:S(2)}, u32[]{:S(2)}) collective-permute-start(bf16[256,288]{1,0:T(8,128)(2,1)S(1)} %slice.86), channel_id=1, source_target_pairs={{0,32},{32,0},{1,33},{33,1},{2,34},{34,2},{3,35},{35,3},{4,36},{36... | collective-permute-start | bytes 442376 | tf_op jit(solution)/shard_map/ppermute | solution.py:23
  142.1 1.9 %collective-permute-start.7 = (bf16[256,1024]{1,0:T(8,128)(2,1)S(1)}, bf16[256,1024]{1,0:T(8,128)(2,1)}, u32[]{:S(2)}, u32[]{:S(2)}) collective-permute-start(bf16[256,1024]{1,0:T(8,128)(2,1)S(1)} %bitcast.28), channel_id=1, source_target_pairs={{0,32},{32,0},{1,33},{33,1},{2,34},{34,2},{3,35},{35,3},{4,36},{36... | collective-permute-start | bytes 1572872 | tf_op jit(solution)/shard_map/ppermute | solution.py:23
  144.0 2.7 %all-to-all-done.6 = bf16[8,40,1024]{2,1,0:T(8,128)(2,1)S(1)} async-done(((bf16[8,40,1024]{2,1,0:T(8,128)(2,1)}), bf16[8,40,1024]{2,1,0:T(8,128)(2,1)S(1)}, u32[]{:S(2)}, u32[]{:S(2)}) %all-to-all-start.6) | async-done | bytes 655392 | tf_op jit(solution)/shard_map/all_to_all | solution.py:14
  146.7 0.4 copy.28
  147.0 9.9 %collective-permute-start.5 = (bf16[8,40,1024]{2,0,1:T(8,128)(2,1)S(1)}, bf16[8,40,1024]{2,0,1:T(8,128)(2,1)S(1)}, u32[]{:S(2)}, u32[]{:S(2)}) collective-permute-start(bf16[8,40,1024]{2,0,1:T(8,128)(2,1)S(1)} %copy.28), channel_id=1, source_target_pairs={{0,32},{32,0},{1,33},{33,1},{2,34},{34,2},{3,35},{35,3},{4,36},{36... | collective-permute-start | bytes 1966088 | tf_op jit(solution)/shard_map/ppermute | solution.py:23
  157.4 1.9 %collective-permute-start.6 = (bf16[256,288]{1,0:T(8,128)(2,1)S(1)}, bf16[256,288]{1,0:T(8,128)(2,1)S(1)}, u32[]{:S(2)}, u32[]{:S(2)}) collective-permute-start(bf16[256,288]{1,0:T(8,128)(2,1)S(1)} %slice.89), channel_id=1, source_target_pairs={{0,32},{32,0},{1,33},{33,1},{2,34},{34,2},{3,35},{35,3},{4,36},{36... | collective-permute-start | bytes 442376 | tf_op jit(solution)/shard_map/ppermute | solution.py:23
  160.2 1.4 convolution_add_fusion.1
  161.7 0.6 add.104
  162.3 2.4 %fusion.4 = f32[1024,288]{0,1:T(8,128)} fusion(f32[288,1024]{1,0:T(8,128)S(1)} %fusion.9, bf16[256,288]{1,0:T(8,128)(2,1)S(1)} %collective-permute-done.6, bf16[256,1024]{1,0:T(8,128)(2,1)} %collective-permute-done.7, bf16[576,1024]{1,0:T(8,128)(2,1)S(1)} %fusion.1, f32[1024]{0:T(1024)S(1)} %add_sqrt_fusion, f32[1024]{0:T(1024)S(1)} %add.108), kind=kOutput, calls=%fused_computation.8 | convolution fusion | flops 152469504 | bytes 3629056 | tf_op jit(solution)/shard_map/dot_general | solution.py:36
  (52 shorter events, 3.4 us)
Async XLA Ops:
  0.6 20.4 %copy-start = (bf16[1024,288]{0,1:T(8,128)(2,1)S(1)}, bf16[1024,288]{0,1:T(8,128)(2,1)}, u32[]{:S(2)}) copy-start(bf16[1024,288]{0,1:T(8,128)(2,1)} %param.10) | copy-start | bytes 1769476
  0.6 23.0 %copy-start.2 = (f32[288]{0:T(512)S(1)}, f32[288]{0:T(512)}, u32[]{:S(2)}) copy-start(f32[288]{0:T(512)} %param.11) | copy-start | bytes 3460
  0.7 24.9 %copy-start.3 = (bf16[288,1024]{1,0:T(8,128)(2,1)S(1)}, bf16[288,1024]{1,0:T(8,128)(2,1)}, u32[]{:S(2)}) copy-start(bf16[288,1024]{1,0:T(8,128)(2,1)} %param.8) | copy-start | bytes 1769476
  3.1 9.6 %collective-permute-start = (bf16[8,288]{1,0:T(8,128)(2,1)S(1)}, bf16[8,288]{1,0:T(8,128)(2,1)S(1)}, u32[]{:S(2)}, u32[]{:S(2)}) collective-permute-start(bf16[8,288]{1,0:T(8,128)(2,1)S(1)} %get-tuple-element.8), channel_id=1, source_target_pairs={{0,32},{32,0},{1,33},{33,1},{2,34},{34,2},{3,35},{35,3},{4,36},{36... | collective-permute-start | bytes 13832 | tf_op jit(solution)/shard_map/ppermute | solution.py:23
  13.6 18.0 %all-to-all-start = ((bf16[32,8,576]{2,1,0:T(8,128)(2,1)}), bf16[32,8,576]{2,1,0:T(8,128)(2,1)S(1)}, u32[]{:S(2)}, u32[]{:S(2)}) async-start(bf16[32,8,576]{2,1,0:T(8,128)(2,1)} %broadcast_in_dim.25), calls=%async_computation | async-start | bytes 655360 | tf_op jit(solution)/shard_map/all_to_all | solution.py:14
  21.1 10.5 %collective-permute-start.3 = (bf16[288,1024]{1,0:T(8,128)(2,1)S(1)}, bf16[288,1024]{1,0:T(8,128)(2,1)S(1)}, u32[]{:S(2)}, u32[]{:S(2)}) collective-permute-start(bf16[288,1024]{1,0:T(8,128)(2,1)S(1)} %bitcast.32), channel_id=1, source_target_pairs={{0,32},{32,0},{1,33},{33,1},{2,34},{34,2},{3,35},{35,3},{4,36},{36... | collective-permute-start | bytes 1769480 | tf_op jit(solution)/shard_map/ppermute | solution.py:23
  23.6 4.4 %collective-permute-start.1 = (f32[288]{0:T(512)S(1)}, f32[288]{0:T(512)S(1)}, u32[]{:S(2)}, u32[]{:S(2)}) collective-permute-start(f32[288]{0:T(512)S(1)} %copy-done.2), channel_id=1, source_target_pairs={{0,32},{32,0},{1,33},{33,1},{2,34},{34,2},{3,35},{35,3},{4,36},{36... | collective-permute-start | bytes 3464 | tf_op jit(solution)/shard_map/ppermute | solution.py:23
  25.6 6.4 %collective-permute-start.2 = (bf16[288,1024]{1,0:T(8,128)(2,1)S(1)}, bf16[288,1024]{1,0:T(8,128)(2,1)}, u32[]{:S(2)}, u32[]{:S(2)}) collective-permute-start(bf16[288,1024]{1,0:T(8,128)(2,1)S(1)} %copy-done.3), channel_id=1, source_target_pairs={{0,32},{32,0},{1,33},{33,1},{2,34},{34,2},{3,35},{35,3},{4,36},{36... | collective-permute-start | bytes 1769480 | tf_op jit(solution)/shard_map/ppermute | solution.py:23
  33.7 22.8 %copy-start.1 = (f32[1024]{0:T(1024)S(1)}, f32[1024]{0:T(1024)}, u32[]{:S(2)}) copy-start(f32[1024]{0:T(1024)} %param.9) | copy-start | bytes 12292
  57.4 15.5 %all-to-all-start.2 = ((bf16[8,32,1024]{2,1,0:T(8,128)(2,1)}), bf16[8,32,1024]{2,1,0:T(8,128)(2,1)S(1)}, u32[]{:S(2)}, u32[]{:S(2)}) async-start(bf16[8,32,1024]{2,1,0:T(8,128)(2,1)} %broadcast_in_dim.27), calls=%async_computation.2 | async-start | bytes 1048576 | tf_op jit(solution)/shard_map/all_to_all | solution.py:14
  129.5 17.2 %all-to-all-start.6 = ((bf16[8,40,1024]{2,1,0:T(8,128)(2,1)}), bf16[8,40,1024]{2,1,0:T(8,128)(2,1)S(1)}, u32[]{:S(2)}, u32[]{:S(2)}) async-start(bf16[8,40,1024]{2,1,0:T(8,128)(2,1)} %broadcast_in_dim.29), calls=%async_computation.6 | async-start | bytes 1310720 | tf_op jit(solution)/shard_map/all_to_all | solution.py:14
  133.1 27.1 %collective-permute-start.4 = (bf16[256,288]{1,0:T(8,128)(2,1)S(1)}, bf16[256,288]{1,0:T(8,128)(2,1)S(1)}, u32[]{:S(2)}, u32[]{:S(2)}) collective-permute-start(bf16[256,288]{1,0:T(8,128)(2,1)S(1)} %slice.86), channel_id=1, source_target_pairs={{0,32},{32,0},{1,33},{33,1},{2,34},{34,2},{3,35},{35,3},{4,36},{36... | collective-permute-start | bytes 442376 | tf_op jit(solution)/shard_map/ppermute | solution.py:23
  142.1 20.2 %collective-permute-start.7 = (bf16[256,1024]{1,0:T(8,128)(2,1)S(1)}, bf16[256,1024]{1,0:T(8,128)(2,1)}, u32[]{:S(2)}, u32[]{:S(2)}) collective-permute-start(bf16[256,1024]{1,0:T(8,128)(2,1)S(1)} %bitcast.28), channel_id=1, source_target_pairs={{0,32},{32,0},{1,33},{33,1},{2,34},{34,2},{3,35},{35,3},{4,36},{36... | collective-permute-start | bytes 1572872 | tf_op jit(solution)/shard_map/ppermute | solution.py:23
  147.0 12.8 %collective-permute-start.5 = (bf16[8,40,1024]{2,0,1:T(8,128)(2,1)S(1)}, bf16[8,40,1024]{2,0,1:T(8,128)(2,1)S(1)}, u32[]{:S(2)}, u32[]{:S(2)}) collective-permute-start(bf16[8,40,1024]{2,0,1:T(8,128)(2,1)S(1)} %copy.28), channel_id=1, source_target_pairs={{0,32},{32,0},{1,33},{33,1},{2,34},{34,2},{3,35},{35,3},{4,36},{36... | collective-permute-start | bytes 1966088 | tf_op jit(solution)/shard_map/ppermute | solution.py:23
  157.4 4.9 %collective-permute-start.6 = (bf16[256,288]{1,0:T(8,128)(2,1)S(1)}, bf16[256,288]{1,0:T(8,128)(2,1)S(1)}, u32[]{:S(2)}, u32[]{:S(2)}) collective-permute-start(bf16[256,288]{1,0:T(8,128)(2,1)S(1)} %slice.89), channel_id=1, source_target_pairs={{0,32},{32,0},{1,33},{33,1},{2,34},{34,2},{3,35},{35,3},{4,36},{36... | collective-permute-start | bytes 442376 | tf_op jit(solution)/shard_map/ppermute | solution.py:23

commit v3 on v2

v3 whole, which is shorter than its diff:
```python
import jax
import jax.numpy as jnp
from jax import lax
from jax.experimental import pallas as pl
from jax.experimental.pallas import tpu as pltpu
from jax.sharding import Mesh
from jax.sharding import PartitionSpec as P

ROWS = 512
LANES = 128
TENSOR = ("x", "z")
F32 = jnp.float32
BF16 = jnp.bfloat16
SHARPNESS = 8.0
VMEM = pl.BlockSpec(memory_space=pltpu.VMEM)
SMEM = pl.BlockSpec(memory_space=pltpu.SMEM)
ANY = pl.BlockSpec(memory_space=pl.ANY)


def exchange(blocks, axis):
    return lax.all_to_all(blocks, axis, 0, 0, tiled=False)


def swap(block):
    return lax.ppermute(block, "core", [(0, 1), (1, 0)])


def dot(a, b, dims):
    return lax.dot_general(a, b, (dims, ((), ())), preferred_element_type=F32)


def call(kernel, outs, specs, cost, scratch=(), out_specs=None):
    flops, moved = cost
    return pl.pallas_call(
        kernel,
        out_shape=outs,
        in_specs=specs,
        out_specs=jax.tree.map(lambda _: VMEM, outs) if out_specs is None else out_specs,
        scratch_shapes=list(scratch),
        compiler_params=pltpu.CompilerParams(vmem_limit_bytes=24 * 1024 * 1024),
        cost_estimate=pl.CostEstimate(flops=flops, bytes_accessed=moved, transcendentals=0),
    )


def shape(dims, kind):
    return jax.ShapeDtypeStruct(dims, kind)


def store_parts(value, store):
    high = value.astype(BF16)
    store(0, high)
    store(1, (value - high.astype(F32)).astype(BF16))


def pick_kernel(picked_ref, residual_ref, own_ref, other_ref):
    width, tokens = residual_ref.shape
    piece = own_ref.shape[0]
    core = lax.axis_index("core")
    place = lax.axis_index("x") * lax.axis_size("z") + lax.axis_index("z")
    row = lax.broadcasted_iota(jnp.int32, (piece, tokens), 0)
    token = lax.broadcasted_iota(jnp.int32, (piece, tokens), 1) + place * tokens
    table = residual_ref[...]
    zeros = jnp.zeros_like(table)

    def pick(start, columns):
        wanted = jnp.zeros((piece, tokens), jnp.int32)
        for i in range(piece):
            wanted = jnp.where(row == i, picked_ref[start + i], wanted)
        hot = jnp.where(wanted == token, 1.0, 0.0).astype(BF16)
        return dot(hot, columns, ((1,), (1,))).astype(BF16)

    own_ref[...] = pick(core * piece, jnp.concatenate([table, zeros], axis=0))
    other_ref[...] = pick((1 - core) * piece, jnp.concatenate([zeros, table], axis=0))


def join_kernel(own_ref, got_ref, rows_ref, copies_ref):
    rows = own_ref[...] + got_ref[...]
    rows_ref[...] = rows
    for i in range(copies_ref.shape[0]):
        copies_ref[i] = rows


def pack_kernel(enc_own, enc_other, dec_own, dec_other, enc_ref, dec_ref, squares_ref):
    width, latents = enc_own.shape
    enc_ref[:width] = enc_own[...]
    enc_ref[width:] = enc_other[...]
    dec_ref[:width] = dec_own[...]
    dec_ref[width:] = dec_other[...]
    count = latents // LANES
    row = lax.broadcasted_iota(jnp.int32, (count, LANES), 0)
    total = jnp.zeros((count, LANES), F32)
    for k in range(count):
        lanes = pl.ds(k * LANES, LANES)
        a = dec_own[:, lanes].astype(F32)
        b = dec_other[:, lanes].astype(F32)
        part = jnp.sum(a * a + b * b, axis=0, keepdims=True)
        total = jnp.where(row == k, part, total)
    high = total.astype(BF16).astype(F32)
    squares_ref[...] = jnp.concatenate([high, total - high], axis=0).astype(BF16)


def spread(value, out_ref, first):
    share = value.shape[0] // out_ref.shape[0]
    for y in range(out_ref.shape[0]):
        for k in range(value.shape[1] // LANES):
            out_ref[y, pl.ds((first + k) * share, share), :] = value[
                y * share : (y + 1) * share, k * LANES : (k + 1) * LANES
            ]


def pre_kernel(rows_ref, bias_ref, enc_ref, squares_ref, out_ref, centered_ref):
    count = rows_ref.shape[0] * rows_ref.shape[1]
    rows = rows_ref[...].astype(F32).reshape(count, rows_ref.shape[2])
    centered_ref[...] = (rows - bias_ref[...]).astype(BF16)
    step = 2 * LANES
    for n in range(enc_ref.shape[1] // step):
        part = dot(centered_ref[...], enc_ref[:, n * step : (n + 1) * step], ((1,), (0,)))
        spread(part.astype(BF16), out_ref, 2 * n)
    extra = squares_ref.shape[0]
    for y in range(out_ref.shape[0]):
        out_ref[y, pl.ds(out_ref.shape[1] - extra, extra), :] = squares_ref[...]


def sum_blocks(blocks_ref, size):
    total = blocks_ref[0, :size, :].astype(F32)
    for y in range(1, blocks_ref.shape[0]):
        total = total + blocks_ref[y, :size, :].astype(F32)
    return total


def sum_parts(blocks_ref, size):
    total = blocks_ref[0, size:, :].astype(F32)
    for y in range(1, blocks_ref.shape[0]):
        total = total + blocks_ref[y, size:, :].astype(F32)
    half = total.shape[0] // 2
    return total[:half] + total[half:]


def act_kernel(blocks_ref, bias_ref, copies_ref, active_ref, gate_ref, norms_ref):
    size = copies_ref.shape[1]
    count = bias_ref.shape[0]
    share = size // count
    total = sum_blocks(blocks_ref, size)
    for k in range(count):
        lines = slice(k * share, (k + 1) * share)
        value = SHARPNESS * (total[lines] + bias_ref[k : k + 1, :])
        small = jnp.exp(-jnp.abs(value))
        soft = jnp.maximum(value, 0.0) + jnp.log1p(small)
        active = (soft / SHARPNESS).astype(BF16)
        active_ref[lines, :] = active
        gate_ref[lines, :] = jnp.where(value >= 0.0, 1.0, small) / (1.0 + small)
        for y in range(copies_ref.shape[0]):
            copies_ref[y, lines, :] = active
    norms_ref[...] = jnp.sqrt(sum_parts(blocks_ref, size) + 1e-06)


def unit_kernel(dec_ref, norms_ref, unit_ref):
    for k in range(norms_ref.shape[0]):
        lanes = pl.ds(k * LANES, LANES)
        unit_ref[:, lanes] = (dec_ref[:, lanes].astype(F32) / norms_ref[k : k + 1, :]).astype(BF16)


def rebuild_kernel(copies_ref, unit_ref, out_ref, active_ref):
    latents = unit_ref.shape[1]
    count = latents // LANES
    share = copies_ref.shape[1] // count
    for y in range(copies_ref.shape[0]):
        for k in range(count):
            active_ref[y * share : (y + 1) * share, k * LANES : (k + 1) * LANES] = copies_ref[
                y, k * share : (k + 1) * share, :
            ]
    part = dot(active_ref[...], unit_ref[...], ((1,), (1,)))
    out_ref[...] = part.astype(BF16).reshape(out_ref.shape)


def error_kernel(blocks_ref, bias_ref, rows_ref, copies_ref):
    total = blocks_ref[0].astype(F32)
    for i in range(1, blocks_ref.shape[0]):
        total = total + blocks_ref[i].astype(F32)
    rebuilt = total + bias_ref[...]
    error = (2.0 / ROWS * (rebuilt - rows_ref[...].astype(F32))).astype(BF16)
    for i in range(copies_ref.shape[0]):
        copies_ref[i] = error


def raw_kernel(error_ref, unit_ref, out_ref):
    count = error_ref.shape[0] * error_ref.shape[1]
    error = error_ref[...].reshape(count, error_ref.shape[2])
    step = 2 * LANES
    for n in range(unit_ref.shape[1] // step):
        part = dot(error, unit_ref[:, n * step : (n + 1) * step], ((1,), (0,)))
        spread(part.astype(BF16), out_ref, 2 * n)


def grad_kernel(blocks_ref, active_ref, gate_ref, copies_ref):
    size = blocks_ref.shape[1]
    extra = copies_ref.shape[1] - size
    count = extra // 2
    share = size // count
    raw = sum_blocks(blocks_ref, size)
    grad = ((raw + 1.0 / ROWS) * gate_ref[...]).astype(BF16)
    product = active_ref[...].astype(F32) * raw
    row = lax.broadcasted_iota(jnp.int32, (count, LANES), 0)
    dots = jnp.zeros((count, LANES), F32)
    for k in range(count):
        part = jnp.sum(product[k * share : (k + 1) * share], axis=0, keepdims=True)
        dots = jnp.where(row == k, part, dots)
    high = dots.astype(BF16).astype(F32)
    parts = jnp.concatenate([high, dots - high], axis=0).astype(BF16)
    for y in range(copies_ref.shape[0]):
        copies_ref[y, :size, :] = grad
        copies_ref[y, size:, :] = parts


def last_kernel(
    own_ref, its_ref, centered_own, centered_its, product_ref, unit_ref, norms_ref,
    enc_out, bias_ref, dec_out,
    own_grad, its_grad, enc_ref, dec_ref, sems,
):
    count = norms_ref.shape[0]
    size = own_ref.shape[1] - 2 * count
    share = size // count
    dots = sum_parts(own_ref, size) + sum_parts(its_ref, size)
    step = 2 * LANES
    copies = []
    for n in range(count // 2):
        lanes = pl.ds(n * step, step)
        for k in (2 * n, 2 * n + 1):
            cut = pl.ds(k * LANES, LANES)
            lines = pl.ds(k * share, share)
            ratio = 1.0 / norms_ref[k : k + 1, :]
            dec_ref[:, cut] = (
                product_ref[:, cut] - unit_ref[:, cut].astype(F32) * dots[k : k + 1]
            ) * ratio
            total = jnp.zeros((share, LANES), F32)
            for y in range(own_ref.shape[0]):
                a, b = own_ref[y, lines, :], its_ref[y, lines, :]
                own_grad[pl.ds(y * share, share), cut] = a
                its_grad[pl.ds(y * share, share), cut] = b
                total = total + a.astype(F32) + b.astype(F32)
            bias_ref[k : k + 1, :] = jnp.sum(total, axis=0, keepdims=True)
        copies.append(pltpu.make_async_copy(dec_ref.at[:, lanes], dec_out.at[:, lanes], sems.at[2 * n]))
        copies[-1].start()
        enc_ref[:, lanes] = dot(centered_own[...], own_grad[:, lanes], ((1,), (0,))) + dot(
            centered_its[...], its_grad[:, lanes], ((1,), (0,))
        )
        copies.append(
            pltpu.make_async_copy(enc_ref.at[:, lanes], enc_out.at[:, lanes], sems.at[2 * n + 1])
        )
        copies[-1].start()
    for copy in copies:
        copy.wait()


def body(residual, picked, enc_weight, enc_bias, dec_weight, dec_bias):
    count_y = lax.axis_size("y")
    count_t = lax.axis_size(TENSOR)
    rows = ROWS // 2
    share = rows // count_y
    piece = rows // count_t
    width, latents = enc_weight.shape
    blocks_n = latents // LANES
    size = share * blocks_n
    extra = 2 * blocks_n
    wide = 2 * width
    matmul = 2 * rows * wide * latents
    moved = 3 << 20

    small = shape((piece, wide), BF16)
    own_rows, other_rows = call(pick_kernel, (small, small), [SMEM, VMEM], (1 << 20, 1 << 17))(
        picked, residual.T
    )
    tensor_blocks = shape((count_t, piece, wide), BF16)
    local_rows, copies = call(join_kernel, (small, tensor_blocks), [VMEM] * 2, (1 << 12, 1 << 19))(
        own_rows, swap(other_rows)
    )
    sampled = exchange(copies, TENSOR)
    dec_t = dec_weight.T
    weights = shape((wide, latents), BF16)
    enc_all, dec_all, squares = call(
        pack_kernel, (weights, weights, shape((extra, LANES), BF16)), [VMEM] * 4, (1 << 21, moved)
    )(enc_weight, swap(enc_weight), dec_t, swap(dec_t))
    bias_all = jnp.concatenate([dec_bias, swap(dec_bias)], axis=0)[None]

    pre_blocks, centered = call(
        pre_kernel,
        (shape((count_y, size + extra, LANES), BF16), shape((rows, wide), BF16)),
        [VMEM] * 4,
        (matmul, moved),
    )(sampled, bias_all, enc_all, squares)
    copies, active_share, gate, norms = call(
        act_kernel,
        (
            shape((count_y, size, LANES), BF16),
            shape((size, LANES), BF16),
            shape((size, LANES), F32),
            shape((blocks_n, LANES), F32),
        ),
        [VMEM] * 2,
        (1 << 20, 1 << 20),
    )(exchange(pre_blocks, "y"), enc_bias.reshape(blocks_n, LANES))
    copies = exchange(copies, "y")
    unit = call(unit_kernel, weights, [VMEM] * 2, (1 << 20, moved))(dec_all, norms)
    partial, active = call(
        rebuild_kernel,
        (tensor_blocks, shape((rows, latents), BF16)),
        [VMEM] * 2,
        (matmul, moved),
    )(copies, unit)
    copies = call(error_kernel, tensor_blocks, [VMEM] * 3, (1 << 20, 1 << 20))(
        exchange(partial, TENSOR), bias_all, local_rows
    )
    its_active = swap(active)
    its_centered = swap(centered[:, width:])
    error = exchange(copies, TENSOR)
    raw_blocks = call(
        raw_kernel, shape((count_y, size, LANES), BF16), [VMEM] * 2, (matmul, moved)
    )(error, unit)
    err_grad = error.reshape(rows, wide)
    its_err = swap(err_grad[:, width:])
    product = dot(err_grad[:, :width], active, ((0,), (0,))) + dot(
        its_err, its_active, ((0,), (0,))
    )
    own = exchange(
        call(
            grad_kernel,
            shape((count_y, size + extra, LANES), BF16),
            [VMEM] * 3,
            (1 << 20, 1 << 20),
        )(exchange(raw_blocks, "y"), active_share, gate),
        "y",
    )
    its = swap(own)
    out = shape((width, latents), F32)
    enc_grad, bias_grad, dec_grad = call(
        last_kernel,
        (out, shape((blocks_n, LANES), F32), out),
        [VMEM] * 7,
        (matmul, 2 * moved),
        [
            pltpu.VMEM((rows, latents), BF16),
            pltpu.VMEM((rows, latents), BF16),
            pltpu.VMEM((width, latents), F32),
            pltpu.VMEM((width, latents), F32),
            pltpu.SemaphoreType.DMA((blocks_n,)),
        ],
        (ANY, VMEM, ANY),
    )(own, its, centered[:, :width].T, its_centered.T, product, unit[:width], norms)
    return (enc_grad, bias_grad.reshape(latents), dec_grad.T)


def solution(mesh):
    grid = Mesh(mesh.devices.reshape(8, 2, 4, 8), ("y", "core", "x", "z"))
    dp = ("y", "core")
    return jax.shard_map(
        body,
        mesh=grid,
        in_specs=(
            P(TENSOR, dp),
            P(TENSOR),
            P(dp, TENSOR),
            P(TENSOR),
            P(TENSOR, dp),
            P(dp),
        ),
        out_specs=(P(dp, TENSOR), P(TENSOR), P(TENSOR, dp)),
        check_vma=False,
    )
```

time: 166 us -> 164 us (0.988)
  Pallas kernels: 0 us -> 8.55 us
  matrix products: 7.16 us -> 1.71 us
  waiting for transfers between devices: 18.6 us -> 14.6 us
  local copies, waits for them, and re-layouts: 5.35 us -> 9.07 us
  starting transfers between devices: 52.9 us -> 50.2 us
  other arithmetic: 3.18 us -> 0.76 us
    pallas_call x0 -> x11, Pallas kernels: none -> 8.55 us  [the longest x1 2.51 us: body(): call(last_kernel, (out, shape((blocks_n, LANES), F32), out), [VMEM] * 7,...]
    dot_general x7 -> x2, matrix products: 7.16 us -> 1.71 us  [dot(): return lax.dot_general(a, b, (dims, ((), ())), preferred_element_type=F32)]
    unnamed x9 -> x22, local copies, waits for them, and re-layouts: 1.02 us -> 6.37 us
    all_to_all x3, waiting for transfers between devices: 17.8 us -> 12.7 us  [exchange(): return lax.all_to_all(blocks, axis, 0, 0, tiled=False)]
    ppermute x8, starting transfers between devices: 38.3 us -> 35.3 us  [swap(): return lax.ppermute(block, 'core', [(0, 1), (1, 0)])]
    broadcast_in_dim x5 -> x1, local copies, waits for them, and re-layouts: 2.56 us -> 0.01 us  [body(): bias_all = jnp.concatenate([dec_bias, swap(dec_bias)], axis=0)[None]]
  transfers between devices with their start and end apart: 11 -> 11, of which waited for: 4 -> 4; matrix products, arithmetic and copies ran while one was open for 3% -> 3% of each run, Pallas kernels for 0% -> 1%
where the time goes in v3:
time: 164 us; the launch traced here: 163 us
  blocking collectives  77.3 us (47%)
  starting transfers between devices  50.2 us (31%)
  waiting for transfers between devices  14.6 us (9%)
  local copies, waits for them, and re-layouts  9.07 us (6%)
  Pallas kernels  8.55 us (5%)
  matrix products  1.71 us (1%)
    all_to_all x4, blocking collectives, exchange(): return lax.all_to_all(blocks, axis, 0, 0, tiled=False)  77.3 us
    ppermute x8, starting transfers between devices, swap(): return lax.ppermute(block, 'core', [(0, 1), (1, 0)])  35.3 us
    all_to_all x3, starting transfers between devices, exchange(): return lax.all_to_all(blocks, axis, 0, 0, tiled=False)  14.9 us
    all_to_all x3, waiting for transfers between devices, exchange(): return lax.all_to_all(blocks, axis, 0, 0, tiled=False)  12.7 us
    unnamed x22, local copies, waits for them, and re-layouts  6.37 us
  transfers between devices with their start and end apart: 11, of which 4 were waited for; matrix products, arithmetic and copies ran while one was open for 3% of the time, Pallas kernels for 1%

profile of v3, /device:TPU:1, one launch (start us, length us, event | category | flops | bytes accessed | tf_op | source)
XLA Modules:
  0.0 163.0 jit_solution(5508489702910710240)
XLA Ops:
  0.6 8.9 %collective-permute-start.3 = (bf16[288,1024]{1,0:T(8,128)(2,1)}, bf16[288,1024]{1,0:T(8,128)(2,1)S(1)}, u32[]{:S(2)}, u32[]{:S(2)}) collective-permute-start(bf16[288,1024]{1,0:T(8,128)(2,1)} %bitcast.14), channel_id=1, source_target_pairs={{0,32},{32,0},{1,33},{33,1},{2,34},{34,2},{3,35},{35,3},{4,36},{36... | collective-permute-start | bytes 1769480 | tf_op jit(solution)/shard_map/ppermute | solution.py:25
  9.6 1.9 %collective-permute-start.2 = (bf16[288,1024]{1,0:T(8,128)(2,1)}, bf16[288,1024]{1,0:T(8,128)(2,1)S(1)}, u32[]{:S(2)}, u32[]{:S(2)}) collective-permute-start(bf16[288,1024]{1,0:T(8,128)(2,1)} %enc_own.1), channel_id=1, source_target_pairs={{0,32},{32,0},{1,33},{33,1},{2,34},{34,2},{3,35},{35,3},{4,36},{36... | collective-permute-start | bytes 1769480 | tf_op jit(solution)/shard_map/ppermute | solution.py:25
  11.5 0.9 copy-done.8
  13.7 2.4 %collective-permute-start = (bf16[8,576]{1,0:T(8,128)(2,1)S(1)}, bf16[8,576]{1,0:T(8,128)(2,1)S(1)}, u32[]{:S(2)}, u32[]{:S(2)}) collective-permute-start(bf16[8,576]{1,0:T(8,128)(2,1)S(1)} %get-tuple-element.22), channel_id=1, source_target_pairs={{0,32},{32,0},{1,33},{33,1},{2,34},{34,2},{3,35},{35,3},{4,36},{36... | collective-permute-start | bytes 27656 | tf_op jit(solution)/shard_map/ppermute | solution.py:25
  16.2 0.8 collective-permute-done.got_ref
  17.7 7.5 %all-to-all-start = ((bf16[32,8,576]{2,1,0:T(8,128)(2,1)}), bf16[32,8,576]{2,1,0:T(8,128)(2,1)S(1)}, u32[]{:S(2)}, u32[]{:S(2)}) async-start(bf16[32,8,576]{2,1,0:T(8,128)(2,1)} %get-tuple-element.23), calls=%async_computation | async-start | bytes 655360 | tf_op jit(solution)/shard_map/all_to_all | solution.py:21
  25.2 2.5 %collective-permute-start.1 = (f32[288]{0:T(512)}, f32[288]{0:T(512)S(1)}, u32[]{:S(2)}, u32[]{:S(2)}) collective-permute-start(f32[288]{0:T(512)} %param.11), channel_id=1, source_target_pairs={{0,32},{32,0},{1,33},{33,1},{2,34},{34,2},{3,35},{35,3},{4,36},{36... | collective-permute-start | bytes 3464 | tf_op jit(solution)/shard_map/ppermute | solution.py:25
  27.8 1.0 collective-permute-done.1
  28.8 0.8 pad_maximum_fusion
  29.6 0.8 copy-done.2
  30.4 0.8 copy-done.4
  31.2 1.1 copy-done.1
  32.3 1.1 copy-done.3
  33.3 1.1 copy-done.5
  34.9 0.9 all-to-all-done.rows_ref
  36.3 20.0 %all_to_all.35.blocks_ref = bf16[8,272,128]{2,1,0:T(8,128)(2,1)S(1)} all-to-all(bf16[8,272,128]{2,1,0:T(8,128)(2,1)S(1)} %get-tuple-element.26), channel_id=1, replica_groups=mesh['y'=8,'core'=2,'x'=4,'z'=8] {'y'}, dimensions={0} | all-to-all | bytes 1114112 | tf_op jit(solution)/shard_map/all_to_all | solution.py:21
  56.3 1.0 shard_map.89
  57.3 3.8 %all-to-all-start.2 = ((bf16[8,256,128]{2,1,0:T(8,128)(2,1)}), bf16[8,256,128]{2,1,0:T(8,128)(2,1)S(1)}, u32[]{:S(2)}, u32[]{:S(2)}) async-start(bf16[8,256,128]{2,1,0:T(8,128)(2,1)} %get-tuple-element.27), calls=%async_computation.2 | async-start | bytes 1048576 | tf_op jit(solution)/shard_map/all_to_all | solution.py:21
  61.5 11.9 %all-to-all-done.2.copies_ref = bf16[8,256,128]{2,1,0:T(8,128)(2,1)S(1)} async-done(((bf16[8,256,128]{2,1,0:T(8,128)(2,1)}), bf16[8,256,128]{2,1,0:T(8,128)(2,1)S(1)}, u32[]{:S(2)}, u32[]{:S(2)}) %all-to-all-start.2) | async-done | bytes 524320 | tf_op jit(solution)/shard_map/all_to_all | solution.py:21
  74.0 26.8 %all_to_all.36.blocks_ref = bf16[32,8,576]{2,1,0:T(8,128)(2,1)S(1)} all-to-all(bf16[32,8,576]{2,1,0:T(8,128)(2,1)S(1)} %get-tuple-element.30), channel_id=1, replica_groups=mesh['y'=8,'core'=2,'x'=4,'z'=8] {'x','z'}, dimensions={0} | all-to-all | bytes 589824 | tf_op jit(solution)/shard_map/all_to_all | solution.py:21
  100.9 15.9 %all_to_all.37.error_ref = bf16[32,8,576]{2,1,0:T(8,128)(2,1)S(1)} all-to-all(bf16[32,8,576]{2,1,0:T(8,128)(2,1)S(1)} %shard_map.92), channel_id=1, replica_groups=mesh['y'=8,'core'=2,'x'=4,'z'=8] {'x','z'}, dimensions={0} | all-to-all | bytes 589824 | tf_op jit(solution)/shard_map/all_to_all | solution.py:21
  117.4 14.6 %all_to_all.38.blocks_ref = bf16[8,256,128]{2,1,0:T(8,128)(2,1)S(1)} all-to-all(bf16[8,256,128]{2,1,0:T(8,128)(2,1)S(1)} %shard_map.93), channel_id=1, replica_groups=mesh['y'=8,'core'=2,'x'=4,'z'=8] {'y'}, dimensions={0} | all-to-all | bytes 1048576 | tf_op jit(solution)/shard_map/all_to_all | solution.py:21
  132.0 0.9 shard_map.94
  132.9 3.5 %all-to-all-start.6 = ((bf16[8,272,128]{2,1,0:T(8,128)(2,1)}), bf16[8,272,128]{2,1,0:T(8,128)(2,1)S(1)}, u32[]{:S(2)}, u32[]{:S(2)}) async-start(bf16[8,272,128]{2,1,0:T(8,128)(2,1)} %shard_map.94), calls=%async_computation.6 | async-start | bytes 1114112 | tf_op jit(solution)/shard_map/all_to_all | solution.py:21
  136.4 8.7 %collective-permute-start.7 = (bf16[256,1024]{1,0:T(8,128)(2,1)S(1)}, bf16[256,1024]{1,0:T(8,128)(2,1)}, u32[]{:S(2)}, u32[]{:S(2)}) collective-permute-start(bf16[256,1024]{1,0:T(8,128)(2,1)S(1)} %get-tuple-element.35), channel_id=1, source_target_pairs={{0,32},{32,0},{1,33},{33,1},{2,34},{34,2},{3,35},{35,3},{4,36},{36... | collective-permute-start | bytes 1572872 | tf_op jit(solution)/shard_map/ppermute | solution.py:25
  145.2 0.9 copy.9
  146.0 1.7 %fusion.2 = (bf16[256,288]{0,1:T(8,128)(2,1)}, bf16[288,256]{1,0:T(8,128)(2,1)S(1)}) fusion(bf16[256,576]{0,1:T(8,128)(2,1)} %copy.9), kind=kLoop, calls=%fused_computation.5 | loop fusion | bytes 589824 | tf_op jit(solution)/shard_map/slice | solution.py:314
  147.7 1.9 %collective-permute-start.5 = (bf16[256,288]{0,1:T(8,128)(2,1)}, bf16[256,288]{0,1:T(8,128)(2,1)S(1)}, u32[]{:S(2)}, u32[]{:S(2)}) collective-permute-start(bf16[256,288]{0,1:T(8,128)(2,1)} %get-tuple-element.39), channel_id=1, source_target_pairs={{0,32},{32,0},{1,33},{33,1},{2,34},{34,2},{3,35},{35,3},{4,36},{36... | collective-permute-start | bytes 442376 | tf_op jit(solution)/shard_map/ppermute | solution.py:25
  149.8 2.4 %collective-permute-start.6 = (bf16[256,288]{1,0:T(8,128)(2,1)S(1)}, bf16[256,288]{1,0:T(8,128)(2,1)S(1)}, u32[]{:S(2)}, u32[]{:S(2)}) collective-permute-start(bf16[256,288]{1,0:T(8,128)(2,1)S(1)} %slice.23), channel_id=1, source_target_pairs={{0,32},{32,0},{1,33},{33,1},{2,34},{34,2},{3,35},{35,3},{4,36},{36... | collective-permute-start | bytes 442376 | tf_op jit(solution)/shard_map/ppermute | solution.py:25
  152.2 6.5 %collective-permute-start.4 = (bf16[8,272,128]{2,1,0:T(8,128)(2,1)S(1)}, bf16[8,272,128]{2,1,0:T(8,128)(2,1)S(1)}, u32[]{:S(2)}, u32[]{:S(2)}) collective-permute-start(bf16[8,272,128]{2,1,0:T(8,128)(2,1)S(1)} %all-to-all-done.6.own_ref), channel_id=1, source_target_pairs={{0,32},{32,0},{1,33},{33,1},{2,34},{34,2},{3,35},{35,3},{4,36},{36... | collective-permute-start | bytes 1671176 | tf_op jit(solution)/shard_map/ppermute | solution.py:25
  159.1 1.4 convolution_add_fusion.product_ref
  160.5 2.5 %shard_map.95 = (f32[288,1024]{1,0:T(8,128)}, f32[8,128]{1,0:T(8,128)}, f32[288,1024]{1,0:T(8,128)}) custom-call(bf16[8,272,128]{2,1,0:T(8,128)(2,1)S(1)} %all-to-all-done.6.own_ref, bf16[8,272,128]{2,1,0:T(8,128)(2,1)S(1)} %collective-permute-done.4.its_ref, bf16[288,256]{1,0:T(8,128)(2,1)S(1)} %get-tuple-element.40.centered_own, ...), custom_call_target="tpu_custom_call" | custom-call | flops 301989888 | bytes 6291456 | tf_op jit(solution)/shard_map/pallas_call | solution.py:335
  (35 shorter events, 5.4 us)
Async XLA Ops:
  0.6 30.6 %copy-start = (bf16[288,1024]{1,0:T(8,128)(2,1)S(1)}, bf16[288,1024]{1,0:T(8,128)(2,1)}, u32[]{:S(2)}) copy-start(bf16[288,1024]{1,0:T(8,128)(2,1)} %enc_own.1) | copy-start | bytes 1769476
  0.6 28.9 %collective-permute-start.3 = (bf16[288,1024]{1,0:T(8,128)(2,1)}, bf16[288,1024]{1,0:T(8,128)(2,1)S(1)}, u32[]{:S(2)}, u32[]{:S(2)}) collective-permute-start(bf16[288,1024]{1,0:T(8,128)(2,1)} %bitcast.14), channel_id=1, source_target_pairs={{0,32},{32,0},{1,33},{33,1},{2,34},{34,2},{3,35},{35,3},{4,36},{36... | collective-permute-start | bytes 1769480 | tf_op jit(solution)/shard_map/ppermute | solution.py:25
  9.6 20.8 %collective-permute-start.2 = (bf16[288,1024]{1,0:T(8,128)(2,1)}, bf16[288,1024]{1,0:T(8,128)(2,1)S(1)}, u32[]{:S(2)}, u32[]{:S(2)}) collective-permute-start(bf16[288,1024]{1,0:T(8,128)(2,1)} %enc_own.1), channel_id=1, source_target_pairs={{0,32},{32,0},{1,33},{33,1},{2,34},{34,2},{3,35},{35,3},{4,36},{36... | collective-permute-start | bytes 1769480 | tf_op jit(solution)/shard_map/ppermute | solution.py:25
  11.5 0.9 copy-start.8
  12.4 0.7 copy-start.10
  13.7 3.2 %collective-permute-start = (bf16[8,576]{1,0:T(8,128)(2,1)S(1)}, bf16[8,576]{1,0:T(8,128)(2,1)S(1)}, u32[]{:S(2)}, u32[]{:S(2)}) collective-permute-start(bf16[8,576]{1,0:T(8,128)(2,1)S(1)} %get-tuple-element.22), channel_id=1, source_target_pairs={{0,32},{32,0},{1,33},{33,1},{2,34},{34,2},{3,35},{35,3},{4,36},{36... | collective-permute-start | bytes 27656 | tf_op jit(solution)/shard_map/ppermute | solution.py:25
  17.7 18.0 %all-to-all-start = ((bf16[32,8,576]{2,1,0:T(8,128)(2,1)}), bf16[32,8,576]{2,1,0:T(8,128)(2,1)S(1)}, u32[]{:S(2)}, u32[]{:S(2)}) async-start(bf16[32,8,576]{2,1,0:T(8,128)(2,1)} %get-tuple-element.23), calls=%async_computation | async-start | bytes 655360 | tf_op jit(solution)/shard_map/all_to_all | solution.py:21
  25.2 3.6 %collective-permute-start.1 = (f32[288]{0:T(512)}, f32[288]{0:T(512)S(1)}, u32[]{:S(2)}, u32[]{:S(2)}) collective-permute-start(f32[288]{0:T(512)} %param.11), channel_id=1, source_target_pairs={{0,32},{32,0},{1,33},{33,1},{2,34},{34,2},{3,35},{35,3},{4,36},{36... | collective-permute-start | bytes 3464 | tf_op jit(solution)/shard_map/ppermute | solution.py:25
  29.6 0.8 copy-start.2
  30.4 0.8 copy-start.4
  31.2 1.1 copy-start.1
  32.3 1.1 copy-start.3
  33.3 1.1 copy-start.5
  35.7 20.6 %copy-start.9 = (f32[1024]{0:T(1024)S(1)}, f32[1024]{0:T(1024)}, u32[]{:S(2)}) copy-start(f32[1024]{0:T(1024)} %param.9) | copy-start | bytes 12292
  36.3 20.0 %copy-start.6 = (bf16[256,576]{1,0:T(8,128)(2,1)}, bf16[256,576]{1,0:T(8,128)(2,1)S(1)}, u32[]{:S(2)}) copy-start(bf16[256,576]{1,0:T(8,128)(2,1)S(1)} %get-tuple-element.34) | copy-start | bytes 884740
  57.3 16.1 %all-to-all-start.2 = ((bf16[8,256,128]{2,1,0:T(8,128)(2,1)}), bf16[8,256,128]{2,1,0:T(8,128)(2,1)S(1)}, u32[]{:S(2)}, u32[]{:S(2)}) async-start(bf16[8,256,128]{2,1,0:T(8,128)(2,1)} %get-tuple-element.27), calls=%async_computation.2 | async-start | bytes 1048576 | tf_op jit(solution)/shard_map/all_to_all | solution.py:21
  132.0 13.2 %copy-start.7 = (bf16[256,576]{1,0:T(8,128)(2,1)S(1)}, bf16[256,576]{1,0:T(8,128)(2,1)}, u32[]{:S(2)}) copy-start(bf16[256,576]{1,0:T(8,128)(2,1)} %copy-done.6) | copy-start | bytes 884740
  132.9 19.3 %all-to-all-start.6 = ((bf16[8,272,128]{2,1,0:T(8,128)(2,1)}), bf16[8,272,128]{2,1,0:T(8,128)(2,1)S(1)}, u32[]{:S(2)}, u32[]{:S(2)}) async-start(bf16[8,272,128]{2,1,0:T(8,128)(2,1)} %shard_map.94), calls=%async_computation.6 | async-start | bytes 1114112 | tf_op jit(solution)/shard_map/all_to_all | solution.py:21
  136.4 22.6 %collective-permute-start.7 = (bf16[256,1024]{1,0:T(8,128)(2,1)S(1)}, bf16[256,1024]{1,0:T(8,128)(2,1)}, u32[]{:S(2)}, u32[]{:S(2)}) collective-permute-start(bf16[256,1024]{1,0:T(8,128)(2,1)S(1)} %get-tuple-element.35), channel_id=1, source_target_pairs={{0,32},{32,0},{1,33},{33,1},{2,34},{34,2},{3,35},{35,3},{4,36},{36... | collective-permute-start | bytes 1572872 | tf_op jit(solution)/shard_map/ppermute | solution.py:25
  147.7 12.8 %collective-permute-start.5 = (bf16[256,288]{0,1:T(8,128)(2,1)}, bf16[256,288]{0,1:T(8,128)(2,1)S(1)}, u32[]{:S(2)}, u32[]{:S(2)}) collective-permute-start(bf16[256,288]{0,1:T(8,128)(2,1)} %get-tuple-element.39), channel_id=1, source_target_pairs={{0,32},{32,0},{1,33},{33,1},{2,34},{34,2},{3,35},{35,3},{4,36},{36... | collective-permute-start | bytes 442376 | tf_op jit(solution)/shard_map/ppermute | solution.py:25
  149.8 9.3 %collective-permute-start.6 = (bf16[256,288]{1,0:T(8,128)(2,1)S(1)}, bf16[256,288]{1,0:T(8,128)(2,1)S(1)}, u32[]{:S(2)}, u32[]{:S(2)}) collective-permute-start(bf16[256,288]{1,0:T(8,128)(2,1)S(1)} %slice.23), channel_id=1, source_target_pairs={{0,32},{32,0},{1,33},{33,1},{2,34},{34,2},{3,35},{35,3},{4,36},{36... | collective-permute-start | bytes 442376 | tf_op jit(solution)/shard_map/ppermute | solution.py:25
  152.2 8.2 %collective-permute-start.4 = (bf16[8,272,128]{2,1,0:T(8,128)(2,1)S(1)}, bf16[8,272,128]{2,1,0:T(8,128)(2,1)S(1)}, u32[]{:S(2)}, u32[]{:S(2)}) collective-permute-start(bf16[8,272,128]{2,1,0:T(8,128)(2,1)S(1)} %all-to-all-done.6.own_ref), channel_id=1, source_target_pairs={{0,32},{32,0},{1,33},{33,1},{2,34},{34,2},{3,35},{35,3},{4,36},{36... | collective-permute-start | bytes 1671176 | tf_op jit(solution)/shard_map/ppermute | solution.py:25

commit v4 on v3

--- a/solution.py
+++ b/solution.py
@@ -13,8 +13,8 @@
 BF16 = jnp.bfloat16
 SHARPNESS = 8.0
 VMEM = pl.BlockSpec(memory_space=pltpu.VMEM)
-SMEM = pl.BlockSpec(memory_space=pltpu.SMEM)
 ANY = pl.BlockSpec(memory_space=pl.ANY)
+HBM = pl.BlockSpec(memory_space=pltpu.HBM)
 
 
 def exchange(blocks, axis):
@@ -46,57 +46,91 @@
     return jax.ShapeDtypeStruct(dims, kind)
 
 
-def store_parts(value, store):
-    high = value.astype(BF16)
-    store(0, high)
-    store(1, (value - high.astype(F32)).astype(BF16))
-
-
-def pick_kernel(picked_ref, residual_ref, own_ref, other_ref):
-    width, tokens = residual_ref.shape
+def pick_kernel(picked_hbm, residual_hbm, bias_hbm, own_ref, other_ref, bias, picked, table, sems):
+    width, tokens = table.shape
     piece = own_ref.shape[0]
+    pairs = ((residual_hbm, table), (picked_hbm, picked), (bias_hbm, bias))
+    copies = [pltpu.make_async_copy(a, b, sems.at[i]) for i, (a, b) in enumerate(pairs)]
+    for copy in copies:
+        copy.start()
+    for copy in copies:
+        copy.wait()
     core = lax.axis_index("core")
     place = lax.axis_index("x") * lax.axis_size("z") + lax.axis_index("z")
     row = lax.broadcasted_iota(jnp.int32, (piece, tokens), 0)
     token = lax.broadcasted_iota(jnp.int32, (piece, tokens), 1) + place * tokens
-    table = residual_ref[...]
-    zeros = jnp.zeros_like(table)
+    columns = table[...]
+    zeros = jnp.zeros_like(columns)
 
     def pick(start, columns):
         wanted = jnp.zeros((piece, tokens), jnp.int32)
         for i in range(piece):
-            wanted = jnp.where(row == i, picked_ref[start + i], wanted)
+            wanted = jnp.where(row == i, picked[start + i], wanted)
         hot = jnp.where(wanted == token, 1.0, 0.0).astype(BF16)
         return dot(hot, columns, ((1,), (1,))).astype(BF16)
 
-    own_ref[...] = pick(core * piece, jnp.concatenate([table, zeros], axis=0))
-    other_ref[...] = pick((1 - core) * piece, jnp.concatenate([zeros, table], axis=0))
-
-
-def join_kernel(own_ref, got_ref, rows_ref, copies_ref):
-    rows = own_ref[...] + got_ref[...]
+    own_ref[...] = pick(core * piece, jnp.concatenate([columns, zeros], axis=0))
+    other_ref[:piece] = pick((1 - core) * piece, jnp.concatenate([zeros, columns], axis=0))
+    high = bias[...].astype(BF16).astype(F32)
+    middle = (bias[...] - high).astype(BF16).astype(F32)
+    low = bias[...] - high - middle
+    row = lax.broadcasted_iota(jnp.int32, (piece, width), 0)
+    parts = jnp.where(row == 0, high, jnp.where(row == 1, middle, jnp.where(row == 2, low, 0.0)))
+    line = lax.broadcasted_iota(jnp.int32, (width, 2 * width), 0)
+    lane = lax.broadcasted_iota(jnp.int32, (width, 2 * width), 1)
+    move = jnp.where(lane == line + width, 1.0, 0.0).astype(BF16)
+    other_ref[piece:] = dot(parts.astype(BF16), move, ((1,), (0,))).astype(BF16)
+
+
+def join_kernel(own_ref, got_ref, bias_ref, rows_ref, copies_ref, biases_ref):
+    piece = own_ref.shape[0]
+    width = bias_ref.shape[1]
+    rows = own_ref[...] + got_ref[:piece]
     rows_ref[...] = rows
     for i in range(copies_ref.shape[0]):
         copies_ref[i] = rows
-
-
-def pack_kernel(enc_own, enc_other, dec_own, dec_other, enc_ref, dec_ref, squares_ref):
-    width, latents = enc_own.shape
-    enc_ref[:width] = enc_own[...]
-    enc_ref[width:] = enc_other[...]
-    dec_ref[:width] = dec_own[...]
-    dec_ref[width:] = dec_other[...]
+    parts = got_ref[piece:].astype(F32)
+    biases_ref[...] = parts[0:1] + parts[1:2] + parts[2:3]
+    biases_ref[:, :width] = bias_ref[...]
+
+
+def stage_kernel(enc_hbm, dec_hbm, after_hbm, both_ref, sems):
+    width = enc_hbm.shape[0]
+    copies = [
+        pltpu.make_async_copy(enc_hbm, both_ref.at[pl.ds(0, width)], sems.at[0]),
+        pltpu.make_async_copy(dec_hbm, both_ref.at[pl.ds(width, width)], sems.at[1]),
+    ]
+    for copy in copies:
+        copy.start()
+    for copy in copies:
+        copy.wait()
+
+
+def pack_kernel(own_ref, other_ref, enc_ref, dec_ref, squares_ref):
+    width = own_ref.shape[0] // 2
+    latents = own_ref.shape[1]
+    enc_ref[:width] = own_ref[:width]
+    enc_ref[width:] = other_ref[:width]
+    dec_ref[:width] = own_ref[width:]
+    dec_ref[width:] = other_ref[width:]
     count = latents // LANES
     row = lax.broadcasted_iota(jnp.int32, (count, LANES), 0)
     total = jnp.zeros((count, LANES), F32)
     for k in range(count):
         lanes = pl.ds(k * LANES, LANES)
-        a = dec_own[:, lanes].astype(F32)
-        b = dec_other[:, lanes].astype(F32)
+        a = own_ref[width:, lanes].astype(F32)
+        b = other_ref[width:, lanes].astype(F32)
         part = jnp.sum(a * a + b * b, axis=0, keepdims=True)
         total = jnp.where(row == k, part, total)
     high = total.astype(BF16).astype(F32)
     squares_ref[...] = jnp.concatenate([high, total - high], axis=0).astype(BF16)
+
+
+def turn_kernel(value_ref, own_ref, other_ref):
+    turned = value_ref[...].astype(F32).T
+    width = own_ref.shape[0]
+    own_ref[...] = turned[:width].astype(BF16)
+    other_ref[...] = turned[width:].astype(BF16)
 
 
 def spread(value, out_ref, first):
@@ -267,20 +301,29 @@
     moved = 3 << 20
 
     small = shape((piece, wide), BF16)
-    own_rows, other_rows = call(pick_kernel, (small, small), [SMEM, VMEM], (1 << 20, 1 << 17))(
-        picked, residual.T
-    )
+    own_rows, other_rows, own_bias = call(
+        pick_kernel,
+        (small, shape((2 * piece, wide), BF16), shape((1, width), F32)),
+        [HBM] * 3,
+        (1 << 20, 1 << 17),
+        [
+            pltpu.SMEM(picked.shape, jnp.int32),
+            pltpu.VMEM(residual.shape[::-1], BF16),
+            pltpu.SemaphoreType.DMA((3,)),
+        ],
+    )(picked, residual.T, dec_bias[None])
     tensor_blocks = shape((count_t, piece, wide), BF16)
-    local_rows, copies = call(join_kernel, (small, tensor_blocks), [VMEM] * 2, (1 << 12, 1 << 19))(
-        own_rows, swap(other_rows)
-    )
+    local_rows, copies, bias_all = call(
+        join_kernel, (small, tensor_blocks, shape((1, wide), F32)), [VMEM] * 3, (1 << 12, 1 << 19)
+    )(own_rows, swap(other_rows), own_bias)
     sampled = exchange(copies, TENSOR)
-    dec_t = dec_weight.T
     weights = shape((wide, latents), BF16)
+    both = call(
+        stage_kernel, weights, [HBM] * 2 + [ANY], (1, moved), [pltpu.SemaphoreType.DMA((2,))]
+    )(enc_weight, dec_weight.T, local_rows)
     enc_all, dec_all, squares = call(
-        pack_kernel, (weights, weights, shape((extra, LANES), BF16)), [VMEM] * 4, (1 << 21, moved)
-    )(enc_weight, swap(enc_weight), dec_t, swap(dec_t))
-    bias_all = jnp.concatenate([dec_bias, swap(dec_bias)], axis=0)[None]
+        pack_kernel, (weights, weights, shape((extra, LANES), BF16)), [VMEM] * 2, (1 << 21, moved)
+    )(both, swap(both))
 
     pre_blocks, centered = call(
         pre_kernel,
@@ -307,11 +350,15 @@
         [VMEM] * 2,
         (matmul, moved),
     )(copies, unit)
+    its_active = swap(active)
+    turned = shape((width, rows), BF16)
+    centered_own, centered_other = call(turn_kernel, (turned, turned), [VMEM], (1 << 20, 1 << 20))(
+        centered
+    )
+    centered_its = swap(centered_other)
     copies = call(error_kernel, tensor_blocks, [VMEM] * 3, (1 << 20, 1 << 20))(
         exchange(partial, TENSOR), bias_all, local_rows
     )
-    its_active = swap(active)
-    its_centered = swap(centered[:, width:])
     error = exchange(copies, TENSOR)
     raw_blocks = call(
         raw_kernel, shape((count_y, size, LANES), BF16), [VMEM] * 2, (matmul, moved)
@@ -345,7 +392,7 @@
             pltpu.SemaphoreType.DMA((blocks_n,)),
         ],
         (ANY, VMEM, ANY),
-    )(own, its, centered[:, :width].T, its_centered.T, product, unit[:width], norms)
+    )(own, its, centered_own, centered_its, product, unit[:width], norms)
     return (enc_grad, bias_grad.reshape(latents), dec_grad.T)
 
 

time: 164 us -> 164 us (level)
  waiting for transfers between devices: 14.6 us -> 19.1 us
  blocking collectives: 77.3 us -> 73.4 us
  starting transfers between devices: 50.2 us -> 47.8 us
    all_to_all x3, waiting for transfers between devices: 12.7 us -> 18.2 us  [exchange(): return lax.all_to_all(blocks, axis, 0, 0, tiled=False)]
    all_to_all x4, blocking collectives: 77.3 us -> 73.4 us  [exchange(): return lax.all_to_all(blocks, axis, 0, 0, tiled=False)]
    unnamed x22 -> x30, local copies, waits for them, and re-layouts: 6.37 us -> 9.52 us
    ppermute x8 -> x6, starting transfers between devices: 35.3 us -> 32.5 us  [swap(): return lax.ppermute(block, 'core', [(0, 1), (1, 0)])]
    slice x1 -> x0, local copies, waits for them, and re-layouts: 1.65 us -> none  [body(): its_centered = swap(centered[:, width:])]
  transfers between devices with their start and end apart: 11 -> 9, of which waited for: 4 -> 3; matrix products, arithmetic and copies ran while one was open for 3% -> 1% of each run, Pallas kernels for 1% -> 1%
where the time goes in v4:
time: 164 us; the launch traced here: 163 us
  blocking collectives  73.4 us (45%)
  starting transfers between devices  47.8 us (29%)
  waiting for transfers between devices  19.1 us (12%)
  local copies, waits for them, and re-layouts  10.4 us (6%)
  Pallas kernels  9.81 us (6%)
  matrix products  1.75 us (1%)
    all_to_all x4, blocking collectives, exchange(): return lax.all_to_all(blocks, axis, 0, 0, tiled=False)  73.4 us
    ppermute x6, starting transfers between devices, swap(): return lax.ppermute(block, 'core', [(0, 1), (1, 0)])  32.5 us
    all_to_all x3, waiting for transfers between devices, exchange(): return lax.all_to_all(blocks, axis, 0, 0, tiled=False)  18.2 us
    all_to_all x3, starting transfers between devices, exchange(): return lax.all_to_all(blocks, axis, 0, 0, tiled=False)  15.3 us
    unnamed x30, local copies, waits for them, and re-layouts  9.52 us
  transfers between devices with their start and end apart: 9, of which 3 were waited for; matrix products, arithmetic and copies ran while one was open for 1% of the time, Pallas kernels for 1%

profile of v4, /device:TPU:1, one launch (start us, length us, event | category | flops | bytes accessed | tf_op | source)
XLA Modules:
  0.0 163.1 jit_solution(16602305134847254924)
XLA Ops:
  0.6 0.7 broadcast_in_dim.3.bias_hbm
  1.3 0.9 copy-done.10
  2.2 0.7 copy-done.14
  2.9 0.8 shard_map.85
  3.7 8.8 %collective-permute-start = (bf16[16,576]{1,0:T(8,128)(2,1)S(1)}, bf16[16,576]{1,0:T(8,128)(2,1)S(1)}, u32[]{:S(2)}, u32[]{:S(2)}) collective-permute-start(bf16[16,576]{1,0:T(8,128)(2,1)S(1)} %get-tuple-element.26), channel_id=1, source_target_pairs={{0,32},{32,0},{1,33},{33,1},{2,34},{34,2},{3,35},{35,3},{4,36},{36... | collective-permute-start | bytes 55304 | tf_op jit(solution)/shard_map/ppermute | solution.py:25
  12.5 0.8 collective-permute-done.got_ref
  13.3 0.8 shard_map.86
  14.1 1.1 copy-done.4
  15.1 1.1 copy-done.5
  16.5 2.3 %collective-permute-start.1 = (bf16[576,1024]{1,0:T(8,128)(2,1)S(1)}, bf16[576,1024]{1,0:T(8,128)(2,1)S(1)}, u32[]{:S(2)}, u32[]{:S(2)}) collective-permute-start(bf16[576,1024]{1,0:T(8,128)(2,1)S(1)} %shard_map.87.own_ref), channel_id=1, source_target_pairs={{0,32},{32,0},{1,33},{33,1},{2,34},{34,2},{3,35},{35,3},{4,36},{36... | collective-permute-start | bytes 3538952 | tf_op jit(solution)/shard_map/ppermute | solution.py:25
  18.7 7.5 %all-to-all-start = ((bf16[32,8,576]{2,1,0:T(8,128)(2,1)}), bf16[32,8,576]{2,1,0:T(8,128)(2,1)S(1)}, u32[]{:S(2)}, u32[]{:S(2)}) async-start(bf16[32,8,576]{2,1,0:T(8,128)(2,1)} %get-tuple-element.28), calls=%async_computation | async-start | bytes 655360 | tf_op jit(solution)/shard_map/all_to_all | solution.py:21
  26.3 1.0 copy-done.2
  27.3 1.3 copy-done.3
  29.0 1.0 copy-done
  30.1 7.0 %all-to-all-done.rows_ref = bf16[32,8,576]{2,1,0:T(8,128)(2,1)S(1)} async-done(((bf16[32,8,576]{2,1,0:T(8,128)(2,1)}), bf16[32,8,576]{2,1,0:T(8,128)(2,1)S(1)}, u32[]{:S(2)}, u32[]{:S(2)}) %all-to-all-start) | async-done | bytes 294944 | tf_op jit(solution)/shard_map/all_to_all | solution.py:21
  37.0 1.3 copy-done.1
  38.9 20.3 %all_to_all.35.blocks_ref = bf16[8,272,128]{2,1,0:T(8,128)(2,1)S(1)} all-to-all(bf16[8,272,128]{2,1,0:T(8,128)(2,1)S(1)} %get-tuple-element.33), channel_id=1, replica_groups=mesh['y'=8,'core'=2,'x'=4,'z'=8] {'y'}, dimensions={0} | all-to-all | bytes 1114112 | tf_op jit(solution)/shard_map/all_to_all | solution.py:21
  59.2 1.0 shard_map.90
  61.4 4.3 %all-to-all-start.2 = ((bf16[8,256,128]{2,1,0:T(8,128)(2,1)}), bf16[8,256,128]{2,1,0:T(8,128)(2,1)S(1)}, u32[]{:S(2)}, u32[]{:S(2)}) async-start(bf16[8,256,128]{2,1,0:T(8,128)(2,1)} %get-tuple-element.34), calls=%async_computation.2 | async-start | bytes 1048576 | tf_op jit(solution)/shard_map/all_to_all | solution.py:21
  66.1 11.3 %all-to-all-done.2.copies_ref = bf16[8,256,128]{2,1,0:T(8,128)(2,1)S(1)} async-done(((bf16[8,256,128]{2,1,0:T(8,128)(2,1)}), bf16[8,256,128]{2,1,0:T(8,128)(2,1)S(1)}, u32[]{:S(2)}, u32[]{:S(2)}) %all-to-all-start.2) | async-done | bytes 524320 | tf_op jit(solution)/shard_map/all_to_all | solution.py:21
  78.0 23.0 %all_to_all.36.blocks_ref = bf16[32,8,576]{2,1,0:T(8,128)(2,1)S(1)} all-to-all(bf16[32,8,576]{2,1,0:T(8,128)(2,1)S(1)} %get-tuple-element.37), channel_id=1, replica_groups=mesh['y'=8,'core'=2,'x'=4,'z'=8] {'x','z'}, dimensions={0} | all-to-all | bytes 589824 | tf_op jit(solution)/shard_map/all_to_all | solution.py:21
  101.1 14.7 %all_to_all.37.error_ref = bf16[32,8,576]{2,1,0:T(8,128)(2,1)S(1)} all-to-all(bf16[32,8,576]{2,1,0:T(8,128)(2,1)S(1)} %shard_map.93), channel_id=1, replica_groups=mesh['y'=8,'core'=2,'x'=4,'z'=8] {'x','z'}, dimensions={0} | all-to-all | bytes 589824 | tf_op jit(solution)/shard_map/all_to_all | solution.py:21
  116.4 15.4 %all_to_all.38.blocks_ref = bf16[8,256,128]{2,1,0:T(8,128)(2,1)S(1)} all-to-all(bf16[8,256,128]{2,1,0:T(8,128)(2,1)S(1)} %shard_map.94), channel_id=1, replica_groups=mesh['y'=8,'core'=2,'x'=4,'z'=8] {'y'}, dimensions={0} | all-to-all | bytes 1048576 | tf_op jit(solution)/shard_map/all_to_all | solution.py:21
  131.8 0.9 shard_map.95
  132.7 3.5 %all-to-all-start.6 = ((bf16[8,272,128]{2,1,0:T(8,128)(2,1)}), bf16[8,272,128]{2,1,0:T(8,128)(2,1)S(1)}, u32[]{:S(2)}, u32[]{:S(2)}) async-start(bf16[8,272,128]{2,1,0:T(8,128)(2,1)} %shard_map.95), calls=%async_computation.6 | async-start | bytes 1114112 | tf_op jit(solution)/shard_map/all_to_all | solution.py:21
  136.2 8.9 %collective-permute-start.5 = (bf16[256,1024]{1,0:T(8,128)(2,1)S(1)}, bf16[256,1024]{1,0:T(8,128)(2,1)}, u32[]{:S(2)}, u32[]{:S(2)}) collective-permute-start(bf16[256,1024]{1,0:T(8,128)(2,1)S(1)} %get-tuple-element.43), channel_id=1, source_target_pairs={{0,32},{32,0},{1,33},{33,1},{2,34},{34,2},{3,35},{35,3},{4,36},{36... | collective-permute-start | bytes 1572872 | tf_op jit(solution)/shard_map/ppermute | solution.py:25
  145.2 0.8 shard_map.96
  146.0 1.9 %collective-permute-start.3 = (bf16[288,256]{1,0:T(8,128)(2,1)}, bf16[288,256]{1,0:T(8,128)(2,1)S(1)}, u32[]{:S(2)}, u32[]{:S(2)}) collective-permute-start(bf16[288,256]{1,0:T(8,128)(2,1)} %get-tuple-element.42), channel_id=1, source_target_pairs={{0,32},{32,0},{1,33},{33,1},{2,34},{34,2},{3,35},{35,3},{4,36},{36... | collective-permute-start | bytes 442376 | tf_op jit(solution)/shard_map/ppermute | solution.py:25
  148.1 2.4 %collective-permute-start.4 = (bf16[256,288]{1,0:T(8,128)(2,1)S(1)}, bf16[256,288]{1,0:T(8,128)(2,1)S(1)}, u32[]{:S(2)}, u32[]{:S(2)}) collective-permute-start(bf16[256,288]{1,0:T(8,128)(2,1)S(1)} %slice.13), channel_id=1, source_target_pairs={{0,32},{32,0},{1,33},{33,1},{2,34},{34,2},{3,35},{35,3},{4,36},{36... | collective-permute-start | bytes 442376 | tf_op jit(solution)/shard_map/ppermute | solution.py:25
  150.5 8.2 %collective-permute-start.2 = (bf16[8,272,128]{2,1,0:T(8,128)(2,1)S(1)}, bf16[8,272,128]{2,1,0:T(8,128)(2,1)S(1)}, u32[]{:S(2)}, u32[]{:S(2)}) collective-permute-start(bf16[8,272,128]{2,1,0:T(8,128)(2,1)S(1)} %all-to-all-done.6.own_ref), channel_id=1, source_target_pairs={{0,32},{32,0},{1,33},{33,1},{2,34},{34,2},{3,35},{35,3},{4,36},{36... | collective-permute-start | bytes 1671176 | tf_op jit(solution)/shard_map/ppermute | solution.py:25
  159.1 1.4 convolution_add_fusion.product_ref
  160.6 2.5 %shard_map.97 = (f32[288,1024]{1,0:T(8,128)}, f32[8,128]{1,0:T(8,128)}, f32[288,1024]{1,0:T(8,128)}) custom-call(bf16[8,272,128]{2,1,0:T(8,128)(2,1)S(1)} %all-to-all-done.6.own_ref, bf16[8,272,128]{2,1,0:T(8,128)(2,1)S(1)} %collective-permute-done.2.its_ref, bf16[288,256]{1,0:T(8,128)(2,1)S(1)} %copy-done.7, ...), custom_call_target="tpu_custom_call" | custom-call | flops 301989888 | bytes 6291456 | tf_op jit(solution)/shard_map/pallas_call | solution.py:382
  (38 shorter events, 4.8 us)
Async XLA Ops:
  1.3 0.9 copy-start.10
  2.2 0.7 copy-start.14
  3.7 9.6 %collective-permute-start = (bf16[16,576]{1,0:T(8,128)(2,1)S(1)}, bf16[16,576]{1,0:T(8,128)(2,1)S(1)}, u32[]{:S(2)}, u32[]{:S(2)}) collective-permute-start(bf16[16,576]{1,0:T(8,128)(2,1)S(1)} %get-tuple-element.26), channel_id=1, source_target_pairs={{0,32},{32,0},{1,33},{33,1},{2,34},{34,2},{3,35},{35,3},{4,36},{36... | collective-permute-start | bytes 55304 | tf_op jit(solution)/shard_map/ppermute | solution.py:25
  14.1 1.1 copy-start.4
  15.1 1.1 copy-start.5
  16.5 9.8 %collective-permute-start.1 = (bf16[576,1024]{1,0:T(8,128)(2,1)S(1)}, bf16[576,1024]{1,0:T(8,128)(2,1)S(1)}, u32[]{:S(2)}, u32[]{:S(2)}) collective-permute-start(bf16[576,1024]{1,0:T(8,128)(2,1)S(1)} %shard_map.87.own_ref), channel_id=1, source_target_pairs={{0,32},{32,0},{1,33},{33,1},{2,34},{34,2},{3,35},{35,3},{4,36},{36... | collective-permute-start | bytes 3538952 | tf_op jit(solution)/shard_map/ppermute | solution.py:25
  18.7 18.3 %all-to-all-start = ((bf16[32,8,576]{2,1,0:T(8,128)(2,1)}), bf16[32,8,576]{2,1,0:T(8,128)(2,1)S(1)}, u32[]{:S(2)}, u32[]{:S(2)}) async-start(bf16[32,8,576]{2,1,0:T(8,128)(2,1)} %get-tuple-element.28), calls=%async_computation | async-start | bytes 655360 | tf_op jit(solution)/shard_map/all_to_all | solution.py:21
  26.3 1.0 copy-start.2
  27.3 1.3 copy-start.3
  29.0 1.0 copy-start
  37.0 1.3 copy-start.1
  38.3 20.9 %copy-start.13 = (f32[1024]{0:T(1024)S(1)}, f32[1024]{0:T(1024)}, u32[]{:S(2)}) copy-start(f32[1024]{0:T(1024)} %param.9) | copy-start | bytes 12292
  60.2 0.7 copy-start.8
  60.8 0.6 copy-start.11
  61.4 15.9 %all-to-all-start.2 = ((bf16[8,256,128]{2,1,0:T(8,128)(2,1)}), bf16[8,256,128]{2,1,0:T(8,128)(2,1)S(1)}, u32[]{:S(2)}, u32[]{:S(2)}) async-start(bf16[8,256,128]{2,1,0:T(8,128)(2,1)} %get-tuple-element.34), calls=%async_computation.2 | async-start | bytes 1048576 | tf_op jit(solution)/shard_map/all_to_all | solution.py:21
  115.8 15.9 %copy-start.9 = (f32[256,128]{1,0:T(8,128)S(1)}, f32[256,128]{1,0:T(8,128)}, u32[]{:S(2)}) copy-start(f32[256,128]{1,0:T(8,128)} %copy-done.8) | copy-start | bytes 393220
  115.8 15.9 %copy-start.12 = (bf16[256,128]{1,0:T(8,128)(2,1)S(1)}, bf16[256,128]{1,0:T(8,128)(2,1)}, u32[]{:S(2)}) copy-start(bf16[256,128]{1,0:T(8,128)(2,1)} %copy-done.11) | copy-start | bytes 196612
  132.7 17.8 %all-to-all-start.6 = ((bf16[8,272,128]{2,1,0:T(8,128)(2,1)}), bf16[8,272,128]{2,1,0:T(8,128)(2,1)S(1)}, u32[]{:S(2)}, u32[]{:S(2)}) async-start(bf16[8,272,128]{2,1,0:T(8,128)(2,1)} %shard_map.95), calls=%async_computation.6 | async-start | bytes 1114112 | tf_op jit(solution)/shard_map/all_to_all | solution.py:21
  136.2 22.8 %collective-permute-start.5 = (bf16[256,1024]{1,0:T(8,128)(2,1)S(1)}, bf16[256,1024]{1,0:T(8,128)(2,1)}, u32[]{:S(2)}, u32[]{:S(2)}) collective-permute-start(bf16[256,1024]{1,0:T(8,128)(2,1)S(1)} %get-tuple-element.43), channel_id=1, source_target_pairs={{0,32},{32,0},{1,33},{33,1},{2,34},{34,2},{3,35},{35,3},{4,36},{36... | collective-permute-start | bytes 1572872 | tf_op jit(solution)/shard_map/ppermute | solution.py:25
  146.0 2.1 %copy-start.6 = (bf16[288,256]{1,0:T(8,128)(2,1)}, bf16[288,256]{1,0:T(8,128)(2,1)S(1)}, u32[]{:S(2)}) copy-start(bf16[288,256]{1,0:T(8,128)(2,1)S(1)} %get-tuple-element.41.centered_own) | copy-start | bytes 442372
  146.0 14.5 %collective-permute-start.3 = (bf16[288,256]{1,0:T(8,128)(2,1)}, bf16[288,256]{1,0:T(8,128)(2,1)S(1)}, u32[]{:S(2)}, u32[]{:S(2)}) collective-permute-start(bf16[288,256]{1,0:T(8,128)(2,1)} %get-tuple-element.42), channel_id=1, source_target_pairs={{0,32},{32,0},{1,33},{33,1},{2,34},{34,2},{3,35},{35,3},{4,36},{36... | collective-permute-start | bytes 442376 | tf_op jit(solution)/shard_map/ppermute | solution.py:25
  148.1 11.0 %collective-permute-start.4 = (bf16[256,288]{1,0:T(8,128)(2,1)S(1)}, bf16[256,288]{1,0:T(8,128)(2,1)S(1)}, u32[]{:S(2)}, u32[]{:S(2)}) collective-permute-start(bf16[256,288]{1,0:T(8,128)(2,1)S(1)} %slice.13), channel_id=1, source_target_pairs={{0,32},{32,0},{1,33},{33,1},{2,34},{34,2},{3,35},{35,3},{4,36},{36... | collective-permute-start | bytes 442376 | tf_op jit(solution)/shard_map/ppermute | solution.py:25
  150.5 10.0 %collective-permute-start.2 = (bf16[8,272,128]{2,1,0:T(8,128)(2,1)S(1)}, bf16[8,272,128]{2,1,0:T(8,128)(2,1)S(1)}, u32[]{:S(2)}, u32[]{:S(2)}) collective-permute-start(bf16[8,272,128]{2,1,0:T(8,128)(2,1)S(1)} %all-to-all-done.6.own_ref), channel_id=1, source_target_pairs={{0,32},{32,0},{1,33},{33,1},{2,34},{34,2},{3,35},{35,3},{4,36},{36... | collective-permute-start | bytes 1671176 | tf_op jit(solution)/shard_map/ppermute | solution.py:25
  159.1 1.5 copy-start.7

commit v5 on v4

v5 whole, which is shorter than its diff:
```python
import jax
import jax.numpy as jnp
from jax import lax
from jax.experimental import pallas as pl
from jax.experimental.pallas import tpu as pltpu
from jax.sharding import Mesh
from jax.sharding import PartitionSpec as P

ROWS = 512
LANES = 128
TENSOR = ("x", "z")
F32 = jnp.float32
BF16 = jnp.bfloat16
SHARPNESS = 8.0
VMEM = pl.BlockSpec(memory_space=pltpu.VMEM)
ANY = pl.BlockSpec(memory_space=pl.ANY)
HBM = pl.BlockSpec(memory_space=pltpu.HBM)


def exchange(blocks, axis):
    return lax.all_to_all(blocks, axis, 0, 0, tiled=False)


def swap(block):
    return lax.ppermute(block, "core", [(0, 1), (1, 0)])


def dot(a, b, dims):
    return lax.dot_general(a, b, (dims, ((), ())), preferred_element_type=F32)


def call(kernel, outs, specs, cost, scratch=(), out_specs=None, limit=12):
    flops, moved = cost
    return pl.pallas_call(
        kernel,
        out_shape=outs,
        in_specs=specs,
        out_specs=jax.tree.map(lambda _: VMEM, outs) if out_specs is None else out_specs,
        scratch_shapes=list(scratch),
        compiler_params=pltpu.CompilerParams(vmem_limit_bytes=limit * 1024 * 1024),
        cost_estimate=pl.CostEstimate(flops=flops, bytes_accessed=moved, transcendentals=0),
    )


def shape(dims, kind):
    return jax.ShapeDtypeStruct(dims, kind)


def pick_kernel(picked_hbm, residual_hbm, own_ref, other_ref, picked, table, sems):
    width, tokens = table.shape
    piece = own_ref.shape[0]
    pairs = ((residual_hbm, table), (picked_hbm, picked))
    copies = [pltpu.make_async_copy(a, b, sems.at[i]) for i, (a, b) in enumerate(pairs)]
    for copy in copies:
        copy.start()
    for copy in copies:
        copy.wait()
    core = lax.axis_index("core")
    place = lax.axis_index("x") * lax.axis_size("z") + lax.axis_index("z")
    row = lax.broadcasted_iota(jnp.int32, (piece, tokens), 0)
    token = lax.broadcasted_iota(jnp.int32, (piece, tokens), 1) + place * tokens
    columns = table[...]
    zeros = jnp.zeros_like(columns)

    def pick(start, columns):
        wanted = jnp.zeros((piece, tokens), jnp.int32)
        for i in range(piece):
            wanted = jnp.where(row == i, picked[start + i], wanted)
        hot = jnp.where(wanted == token, 1.0, 0.0).astype(BF16)
        return dot(hot, columns, ((1,), (1,))).astype(BF16)

    own_ref[...] = pick(core * piece, jnp.concatenate([columns, zeros], axis=0))
    other_ref[...] = pick((1 - core) * piece, jnp.concatenate([zeros, columns], axis=0))


def join_kernel(own_ref, got_ref, rows_ref, copies_ref):
    rows = own_ref[...] + got_ref[...]
    rows_ref[...] = rows
    for i in range(copies_ref.shape[0]):
        copies_ref[i] = rows


def turn_kernel(value_ref, own_ref, other_ref):
    turned = value_ref[...].astype(F32).T
    width = own_ref.shape[0]
    own_ref[...] = turned[:width].astype(BF16)
    other_ref[...] = turned[width:].astype(BF16)


def spread(value, out_ref, first):
    share = value.shape[0] // out_ref.shape[0]
    for y in range(out_ref.shape[0]):
        for k in range(value.shape[1] // LANES):
            out_ref[y, pl.ds((first + k) * share, share), :] = value[
                y * share : (y + 1) * share, k * LANES : (k + 1) * LANES
            ]


def pre_kernel(centered_ref, enc_own, enc_other, out_ref, enc_ref):
    width, latents = enc_own.shape
    step = 2 * LANES
    for n in range(latents // step):
        lanes = pl.ds(n * step, step)
        enc_ref[:width, lanes] = enc_own[:, lanes]
        enc_ref[width:, lanes] = enc_other[:, lanes]
        part = dot(centered_ref[...], enc_ref[:, lanes], ((1,), (0,)))
        spread(part.astype(BF16), out_ref, 2 * n)


def sum_blocks(blocks_ref, size):
    total = blocks_ref[0, :size, :].astype(F32)
    for y in range(1, blocks_ref.shape[0]):
        total = total + blocks_ref[y, :size, :].astype(F32)
    return total


def sum_parts(blocks_ref, size):
    total = blocks_ref[0, size:, :].astype(F32)
    for y in range(1, blocks_ref.shape[0]):
        total = total + blocks_ref[y, size:, :].astype(F32)
    half = total.shape[0] // 2
    return total[:half] + total[half:]


def soft_parts(total, bias):
    value = SHARPNESS * (total + bias)
    small = jnp.exp(-jnp.abs(value))
    soft = jnp.maximum(value, 0.0) + jnp.log1p(small)
    return value, small, (soft / SHARPNESS).astype(BF16)


def act_kernel(blocks_ref, bias_ref, squares_ref, copies_ref):
    size = blocks_ref.shape[1]
    share = size // bias_ref.shape[0]
    total = sum_blocks(blocks_ref, size)
    squares = squares_ref[...]
    high = squares.astype(BF16).astype(F32)
    parts = jnp.concatenate([high, squares - high], axis=0).astype(BF16)
    for k in range(bias_ref.shape[0]):
        lines = slice(k * share, (k + 1) * share)
        _, _, active = soft_parts(total[lines], bias_ref[k : k + 1, :])
        for y in range(copies_ref.shape[0]):
            copies_ref[y, lines, :] = active
    for y in range(copies_ref.shape[0]):
        copies_ref[y, size:, :] = parts


def join_lanes(copies_ref, active_ref, share, k):
    for y in range(copies_ref.shape[0]):
        active_ref[y * share : (y + 1) * share, k * LANES : (k + 1) * LANES] = copies_ref[
            y, k * share : (k + 1) * share, :
        ]


def rebuild_kernel(copies_ref, dec_own, dec_other, out_ref, unit_ref, active_ref):
    width, latents = dec_own.shape
    count = latents // LANES
    size = copies_ref.shape[1] - 2 * count
    norms = jnp.sqrt(sum_parts(copies_ref, size) + 1e-06)
    for k in range(count):
        lanes = pl.ds(k * LANES, LANES)
        norm = norms[k : k + 1]
        unit_ref[:width, lanes] = (dec_own[:, lanes].astype(F32) / norm).astype(BF16)
        unit_ref[width:, lanes] = (dec_other[:, lanes].astype(F32) / norm).astype(BF16)
        join_lanes(copies_ref, active_ref, size // count, k)
    part = dot(active_ref[...], unit_ref[...], ((1,), (1,)))
    out_ref[...] = part.astype(BF16).reshape(out_ref.shape)


def keep_kernel(copies_ref, active_ref, norms_ref):
    count = norms_ref.shape[0]
    size = copies_ref.shape[1] - 2 * count
    norms_ref[...] = jnp.sqrt(sum_parts(copies_ref, size) + 1e-06)
    for k in range(count):
        join_lanes(copies_ref, active_ref, size // count, k)


def error_kernel(blocks_ref, bias_ref, rows_ref, copies_ref):
    total = blocks_ref[0].astype(F32)
    for i in range(1, blocks_ref.shape[0]):
        total = total + blocks_ref[i].astype(F32)
    rebuilt = total + bias_ref[...]
    error = (2.0 / ROWS * (rebuilt - rows_ref[...].astype(F32))).astype(BF16)
    for i in range(copies_ref.shape[0]):
        copies_ref[i] = error


def raw_kernel(error_ref, unit_ref, out_ref):
    count = error_ref.shape[0] * error_ref.shape[1]
    error = error_ref[...].reshape(count, error_ref.shape[2])
    step = 2 * LANES
    for n in range(unit_ref.shape[1] // step):
        part = dot(error, unit_ref[:, n * step : (n + 1) * step], ((1,), (0,)))
        spread(part.astype(BF16), out_ref, 2 * n)


def grad_kernel(blocks_ref, pre_ref, bias_ref, copies_ref):
    size = blocks_ref.shape[1]
    count = bias_ref.shape[0]
    share = size // count
    raw = sum_blocks(blocks_ref, size)
    pre = sum_blocks(pre_ref, size)
    row = lax.broadcasted_iota(jnp.int32, (count, LANES), 0)
    dots = jnp.zeros((count, LANES), F32)
    for k in range(count):
        lines = slice(k * share, (k + 1) * share)
        value, small, active = soft_parts(pre[lines], bias_ref[k : k + 1, :])
        gate = jnp.where(value >= 0.0, 1.0, small) / (1.0 + small)
        grad = ((raw[lines] + 1.0 / ROWS) * gate).astype(BF16)
        for y in range(copies_ref.shape[0]):
            copies_ref[y, lines, :] = grad
        part = jnp.sum(active.astype(F32) * raw[lines], axis=0, keepdims=True)
        dots = jnp.where(row == k, part, dots)
    high = dots.astype(BF16).astype(F32)
    parts = jnp.concatenate([high, dots - high], axis=0).astype(BF16)
    for y in range(copies_ref.shape[0]):
        copies_ref[y, size:, :] = parts


def last_kernel(
    own_ref, its_ref, centered_own, centered_its, product_ref, unit_ref, norms_ref,
    enc_out, bias_ref, dec_out,
    own_grad, its_grad, enc_ref, dec_ref, sems,
):
    count = norms_ref.shape[0]
    size = own_ref.shape[1] - 2 * count
    share = size // count
    dots = sum_parts(own_ref, size) + sum_parts(its_ref, size)
    step = 2 * LANES
    copies = []
    for n in range(count // 2):
        lanes = pl.ds(n * step, step)
        for k in (2 * n, 2 * n + 1):
            cut = pl.ds(k * LANES, LANES)
            lines = pl.ds(k * share, share)
            ratio = 1.0 / norms_ref[k : k + 1, :]
            dec_ref[:, cut] = (
                product_ref[:, cut] - unit_ref[:, cut].astype(F32) * dots[k : k + 1]
            ) * ratio
            total = jnp.zeros((share, LANES), F32)
            for y in range(own_ref.shape[0]):
                a, b = own_ref[y, lines, :], its_ref[y, lines, :]
                own_grad[pl.ds(y * share, share), cut] = a
                its_grad[pl.ds(y * share, share), cut] = b
                total = total + a.astype(F32) + b.astype(F32)
            bias_ref[k : k + 1, :] = jnp.sum(total, axis=0, keepdims=True)
        copies.append(pltpu.make_async_copy(dec_ref.at[:, lanes], dec_out.at[:, lanes], sems.at[2 * n]))
        copies[-1].start()
        enc_ref[:, lanes] = dot(centered_own[...], own_grad[:, lanes], ((1,), (0,))) + dot(
            centered_its[...], its_grad[:, lanes], ((1,), (0,))
        )
        copies.append(
            pltpu.make_async_copy(enc_ref.at[:, lanes], enc_out.at[:, lanes], sems.at[2 * n + 1])
        )
        copies[-1].start()
    for copy in copies:
        copy.wait()


def body(residual, picked, enc_weight, enc_bias, dec_weight, dec_bias):
    count_y = lax.axis_size("y")
    count_t = lax.axis_size(TENSOR)
    rows = ROWS // 2
    share = rows // count_y
    piece = rows // count_t
    width, latents = enc_weight.shape
    blocks_n = latents // LANES
    size = share * blocks_n
    extra = 2 * blocks_n
    wide = 2 * width
    matmul = 2 * rows * wide * latents
    moved = 3 << 20

    small = shape((piece, wide), BF16)
    own_rows, other_rows = call(
        pick_kernel,
        (small, small),
        [HBM] * 2,
        (1 << 20, 1 << 17),
        [
            pltpu.SMEM(picked.shape, jnp.int32),
            pltpu.VMEM(residual.shape[::-1], BF16),
            pltpu.SemaphoreType.DMA((2,)),
        ],
    )(picked, residual.T)
    tensor_blocks = shape((count_t, piece, wide), BF16)
    local_rows, copies = call(join_kernel, (small, tensor_blocks), [VMEM] * 2, (1 << 12, 1 << 19))(
        own_rows, swap(other_rows)
    )
    sampled = exchange(copies, TENSOR)
    bias_all = jnp.concatenate([dec_bias, swap(dec_bias)])[None]
    enc_other = swap(enc_weight)
    centered = (sampled.reshape(rows, wide).astype(F32) - bias_all).astype(BF16)
    pre_blocks = call(
        pre_kernel,
        shape((count_y, size, LANES), BF16),
        [VMEM] * 3,
        (matmul, moved),
        [pltpu.VMEM((wide, latents), BF16)],
    )(centered, enc_weight, enc_other)
    dec_own = dec_weight.T
    dec_other = swap(dec_own)
    squares = jnp.sum(jnp.square(dec_own.astype(F32)) + jnp.square(dec_other.astype(F32)), axis=0)
    blocks = exchange(pre_blocks, "y")
    enc_bias = enc_bias.reshape(blocks_n, LANES)
    copies = call(
        act_kernel, shape((count_y, size + extra, LANES), BF16), [VMEM] * 3, (1 << 20, 1 << 20)
    )(blocks, enc_bias, squares.reshape(blocks_n, LANES))
    copies = exchange(copies, "y")
    partial, unit = call(
        rebuild_kernel,
        (tensor_blocks, shape((wide, latents), BF16)),
        [VMEM] * 3,
        (matmul, moved),
        [pltpu.VMEM((rows, latents), BF16)],
    )(copies, dec_own, dec_other)
    active, norms = call(
        keep_kernel,
        (shape((rows, latents), BF16), shape((blocks_n, LANES), F32)),
        [VMEM],
        (1 << 20, 1 << 20),
    )(copies)
    its_active = swap(active)
    turned = shape((width, rows), BF16)
    centered_own, centered_other = call(turn_kernel, (turned, turned), [VMEM], (1 << 20, 1 << 20))(
        centered
    )
    centered_its = swap(centered_other)
    errors = call(error_kernel, tensor_blocks, [VMEM] * 3, (1 << 20, 1 << 20))(
        exchange(partial, TENSOR), bias_all, local_rows
    )
    error = exchange(errors, TENSOR)
    raw_blocks = call(
        raw_kernel, shape((count_y, size, LANES), BF16), [VMEM] * 2, (matmul, moved)
    )(error, unit)
    err_grad = error.reshape(rows, wide)
    its_err = swap(err_grad[:, width:])
    product = dot(err_grad[:, :width], active, ((0,), (0,))) + dot(
        its_err, its_active, ((0,), (0,))
    )
    own = exchange(
        call(
            grad_kernel,
            shape((count_y, size + extra, LANES), BF16),
            [VMEM] * 3,
            (1 << 20, 1 << 20),
        )(exchange(raw_blocks, "y"), blocks, enc_bias),
        "y",
    )
    its = swap(own)
    out = shape((width, latents), F32)
    enc_grad, bias_grad, dec_grad = call(
        last_kernel,
        (out, shape((blocks_n, LANES), F32), out),
        [VMEM] * 7,
        (matmul, 2 * moved),
        [
            pltpu.VMEM((rows, latents), BF16),
            pltpu.VMEM((rows, latents), BF16),
            pltpu.VMEM((width, latents), F32),
            pltpu.VMEM((width, latents), F32),
            pltpu.SemaphoreType.DMA((blocks_n,)),
        ],
        (ANY, VMEM, ANY),
    )(own, its, centered_own, centered_its, product, unit[:width], norms)
    return (enc_grad, bias_grad.reshape(latents), dec_grad.T)


def solution(mesh):
    grid = Mesh(mesh.devices.reshape(8, 2, 4, 8), ("y", "core", "x", "z"))
    dp = ("y", "core")
    return jax.shard_map(
        body,
        mesh=grid,
        in_specs=(
            P(TENSOR, dp),
            P(TENSOR),
            P(dp, TENSOR),
            P(TENSOR),
            P(TENSOR, dp),
            P(dp),
        ),
        out_specs=(P(dp, TENSOR), P(TENSOR), P(TENSOR, dp)),
        check_vma=False,
    )
```

time: 164 us -> 162 us (0.988)
  starting transfers between devices: 47.8 us -> 74.8 us
  blocking collectives: 73.4 us -> 46.7 us
  local copies, waits for them, and re-layouts: 10.4 us -> 3.5 us
  waiting for transfers between devices: 19.1 us -> 22.8 us
    all_to_all x4 -> x3, blocking collectives: 73.4 us -> 46.7 us  [exchange(): return lax.all_to_all(blocks, axis, 0, 0, tiled=False)]
    all_to_all x3 -> x4, starting transfers between devices: 15.3 us -> 36.1 us  [exchange(): return lax.all_to_all(blocks, axis, 0, 0, tiled=False)]
    ppermute x6 -> x8, starting transfers between devices: 32.5 us -> 38.7 us  [swap(): return lax.ppermute(block, 'core', [(0, 1), (1, 0)])]
    unnamed x30 -> x18, local copies, waits for them, and re-layouts: 9.52 us -> 3.34 us
    ppermute x6 -> x8, waiting for transfers between devices: 0.84 us -> 3.76 us  [swap(): return lax.ppermute(block, 'core', [(0, 1), (1, 0)])]
    all_to_all x3 -> x4, waiting for transfers between devices: 18.2 us -> 19 us  [exchange(): return lax.all_to_all(blocks, axis, 0, 0, tiled=False)]
    pallas_call x8 -> x6, Pallas kernels: 4.9 us -> 4.63 us  [the longest x1 1.41 us: body(): call(rebuild_kernel, (tensor_blocks, shape((wide, latents), BF16)), [VMEM...]
  transfers between devices with their start and end apart: 9 -> 12, of which waited for: 3 -> 6; matrix products, arithmetic and copies ran while one was open for 1% -> 2% of each run, Pallas kernels for 1% -> 1%
where the time goes in v5:
time: 162 us; the launch traced here: 161 us
  starting transfers between devices  74.8 us (46%)
  blocking collectives  46.7 us (29%)
  waiting for transfers between devices  22.8 us (14%)
  Pallas kernels  9.7 us (6%)
  local copies, waits for them, and re-layouts  3.5 us (2%)
  matrix products  1.75 us (1%)
    all_to_all x3, blocking collectives, exchange(): return lax.all_to_all(blocks, axis, 0, 0, tiled=False)  46.7 us
    ppermute x8, starting transfers between devices, swap(): return lax.ppermute(block, 'core', [(0, 1), (1, 0)])  38.7 us
    all_to_all x4, starting transfers between devices, exchange(): return lax.all_to_all(blocks, axis, 0, 0, tiled=False)  36.1 us
    all_to_all x4, waiting for transfers between devices, exchange(): return lax.all_to_all(blocks, axis, 0, 0, tiled=False)  19 us
    ppermute x8, waiting for transfers between devices, swap(): return lax.ppermute(block, 'core', [(0, 1), (1, 0)])  3.76 us
    unnamed x18, local copies, waits for them, and re-layouts  3.34 us
  transfers between devices with their start and end apart: 12, of which 6 were waited for; matrix products, arithmetic and copies ran while one was open for 2% of the time, Pallas kernels for 1%

profile of v5, /device:TPU:1, one launch (start us, length us, event | category | flops | bytes accessed | tf_op | source)
XLA Modules:
  0.0 161.2 jit_solution(113111235872743221)
XLA Ops:
  0.7 0.9 copy-done.6
  2.2 0.8 shard_map.85
  3.0 8.8 %collective-permute-start = (bf16[8,576]{1,0:T(8,128)(2,1)S(1)}, bf16[8,576]{1,0:T(8,128)(2,1)S(1)}, u32[]{:S(2)}, u32[]{:S(2)}) collective-permute-start(bf16[8,576]{1,0:T(8,128)(2,1)S(1)} %get-tuple-element.17), channel_id=1, source_target_pairs={{0,32},{32,0},{1,33},{33,1},{2,34},{34,2},{3,35},{35,3},{4,36},{36... | collective-permute-start | bytes 27656 | tf_op jit(solution)/shard_map/ppermute | solution.py:25
  11.8 0.8 collective-permute-done.got_ref
  12.7 0.8 shard_map.86
  13.4 7.5 %all-to-all-start = ((bf16[32,8,576]{2,1,0:T(8,128)(2,1)}), bf16[32,8,576]{2,1,0:T(8,128)(2,1)S(1)}, u32[]{:S(2)}, u32[]{:S(2)}) async-start(bf16[32,8,576]{2,1,0:T(8,128)(2,1)} %get-tuple-element.18), calls=%async_computation | async-start | bytes 655360 | tf_op jit(solution)/shard_map/all_to_all | solution.py:21
  20.9 2.5 %collective-permute-start.2 = (bf16[288,1024]{1,0:T(8,128)(2,1)}, bf16[288,1024]{1,0:T(8,128)(2,1)S(1)}, u32[]{:S(2)}, u32[]{:S(2)}) collective-permute-start(bf16[288,1024]{1,0:T(8,128)(2,1)} %enc_own.1), channel_id=1, source_target_pairs={{0,32},{32,0},{1,33},{33,1},{2,34},{34,2},{3,35},{35,3},{4,36},{36... | collective-permute-start | bytes 1769480 | tf_op jit(solution)/shard_map/ppermute | solution.py:25
  23.5 1.9 %collective-permute-start.1 = (f32[288]{0:T(512)}, f32[288]{0:T(512)S(1)}, u32[]{:S(2)}, u32[]{:S(2)}) collective-permute-start(f32[288]{0:T(512)} %param.11), channel_id=1, source_target_pairs={{0,32},{32,0},{1,33},{33,1},{2,34},{34,2},{3,35},{35,3},{4,36},{36... | collective-permute-start | bytes 3464 | tf_op jit(solution)/shard_map/ppermute | solution.py:25
  25.4 1.3 collective-permute-done.1
  26.7 0.8 pad_maximum_fusion
  27.5 3.9 %all-to-all-done = bf16[32,8,576]{2,1,0:T(8,128)(2,1)S(1)} async-done(((bf16[32,8,576]{2,1,0:T(8,128)(2,1)}), bf16[32,8,576]{2,1,0:T(8,128)(2,1)S(1)}, u32[]{:S(2)}, u32[]{:S(2)}) %all-to-all-start) | async-done | bytes 294944 | tf_op jit(solution)/shard_map/all_to_all | solution.py:21
  31.5 1.4 shard_map.87
  32.9 7.0 %all-to-all-start.1 = ((bf16[8,256,128]{2,1,0:T(8,128)(2,1)}), bf16[8,256,128]{2,1,0:T(8,128)(2,1)S(1)}, u32[]{:S(2)}, u32[]{:S(2)}) async-start(bf16[8,256,128]{2,1,0:T(8,128)(2,1)} %shard_map.87), calls=%async_computation.1 | async-start | bytes 1048576 | tf_op jit(solution)/shard_map/all_to_all | solution.py:21
  39.8 6.0 %collective-permute-start.3 = (bf16[288,1024]{1,0:T(8,128)(2,1)S(1)}, bf16[288,1024]{1,0:T(8,128)(2,1)S(1)}, u32[]{:S(2)}, u32[]{:S(2)}) collective-permute-start(bf16[288,1024]{1,0:T(8,128)(2,1)S(1)} %bitcast.16), channel_id=1, source_target_pairs={{0,32},{32,0},{1,33},{33,1},{2,34},{34,2},{3,35},{35,3},{4,36},{36... | collective-permute-start | bytes 1769480 | tf_op jit(solution)/shard_map/ppermute | solution.py:25
  45.8 1.6 collective-permute-done.3.dec_other
  47.7 5.1 %all-to-all-done.1.blocks_ref.pre_ref = bf16[8,256,128]{2,1,0:T(8,128)(2,1)S(1)} async-done(((bf16[8,256,128]{2,1,0:T(8,128)(2,1)}), bf16[8,256,128]{2,1,0:T(8,128)(2,1)S(1)}, u32[]{:S(2)}, u32[]{:S(2)}) %all-to-all-start.1) | async-done | bytes 524320 | tf_op jit(solution)/shard_map/all_to_all | solution.py:21
  53.0 14.8 %all_to_all.35.copies_ref = bf16[8,272,128]{2,1,0:T(8,128)(2,1)S(1)} all-to-all(bf16[8,272,128]{2,1,0:T(8,128)(2,1)S(1)} %shard_map.88), channel_id=1, replica_groups=mesh['y'=8,'core'=2,'x'=4,'z'=8] {'y'}, dimensions={0} | all-to-all | bytes 1114112 | tf_op jit(solution)/shard_map/all_to_all | solution.py:21
  67.9 1.1 copy-done.2
  68.9 1.4 shard_map.89
  70.3 18.1 %all-to-all-start.3 = ((bf16[32,8,576]{2,1,0:T(8,128)(2,1)}), bf16[32,8,576]{2,1,0:T(8,128)(2,1)S(1)}, u32[]{:S(2)}, u32[]{:S(2)}) async-start(bf16[32,8,576]{2,1,0:T(8,128)(2,1)} %get-tuple-element.19), calls=%async_computation.3 | async-start | bytes 655360 | tf_op jit(solution)/shard_map/all_to_all | solution.py:21
  88.5 9.9 %all-to-all-done.3.blocks_ref = bf16[32,8,576]{2,1,0:T(8,128)(2,1)S(1)} async-done(((bf16[32,8,576]{2,1,0:T(8,128)(2,1)}), bf16[32,8,576]{2,1,0:T(8,128)(2,1)S(1)}, u32[]{:S(2)}, u32[]{:S(2)}) %all-to-all-start.3) | async-done | bytes 294944 | tf_op jit(solution)/shard_map/all_to_all | solution.py:21
  98.5 16.8 %all_to_all.36.error_ref = bf16[32,8,576]{2,1,0:T(8,128)(2,1)S(1)} all-to-all(bf16[32,8,576]{2,1,0:T(8,128)(2,1)S(1)} %shard_map.90), channel_id=1, replica_groups=mesh['y'=8,'core'=2,'x'=4,'z'=8] {'x','z'}, dimensions={0} | all-to-all | bytes 589824 | tf_op jit(solution)/shard_map/all_to_all | solution.py:21
  115.9 15.0 %all_to_all.37.blocks_ref = bf16[8,256,128]{2,1,0:T(8,128)(2,1)S(1)} all-to-all(bf16[8,256,128]{2,1,0:T(8,128)(2,1)S(1)} %shard_map.91), channel_id=1, replica_groups=mesh['y'=8,'core'=2,'x'=4,'z'=8] {'y'}, dimensions={0} | all-to-all | bytes 1048576 | tf_op jit(solution)/shard_map/all_to_all | solution.py:21
  130.9 1.1 shard_map.92
  132.0 3.5 %all-to-all-start.6 = ((bf16[8,272,128]{2,1,0:T(8,128)(2,1)}), bf16[8,272,128]{2,1,0:T(8,128)(2,1)S(1)}, u32[]{:S(2)}, u32[]{:S(2)}) async-start(bf16[8,272,128]{2,1,0:T(8,128)(2,1)} %shard_map.92), calls=%async_computation.6 | async-start | bytes 1114112 | tf_op jit(solution)/shard_map/all_to_all | solution.py:21
  135.7 7.8 %collective-permute-start.7 = (bf16[256,1024]{1,0:T(8,128)(2,1)S(1)}, bf16[256,1024]{1,0:T(8,128)(2,1)}, u32[]{:S(2)}, u32[]{:S(2)}) collective-permute-start(bf16[256,1024]{1,0:T(8,128)(2,1)S(1)} %get-tuple-element.24), channel_id=1, source_target_pairs={{0,32},{32,0},{1,33},{33,1},{2,34},{34,2},{3,35},{35,3},{4,36},{36... | collective-permute-start | bytes 1572872 | tf_op jit(solution)/shard_map/ppermute | solution.py:25
  143.5 0.8 shard_map.93
  144.9 1.9 %collective-permute-start.5 = (bf16[288,256]{1,0:T(8,128)(2,1)}, bf16[288,256]{1,0:T(8,128)(2,1)S(1)}, u32[]{:S(2)}, u32[]{:S(2)}) collective-permute-start(bf16[288,256]{1,0:T(8,128)(2,1)} %get-tuple-element.23), channel_id=1, source_target_pairs={{0,32},{32,0},{1,33},{33,1},{2,34},{34,2},{3,35},{35,3},{4,36},{36... | collective-permute-start | bytes 442376 | tf_op jit(solution)/shard_map/ppermute | solution.py:25
  147.0 2.4 %collective-permute-start.6 = (bf16[256,288]{1,0:T(8,128)(2,1)S(1)}, bf16[256,288]{1,0:T(8,128)(2,1)S(1)}, u32[]{:S(2)}, u32[]{:S(2)}) collective-permute-start(bf16[256,288]{1,0:T(8,128)(2,1)S(1)} %slice.13), channel_id=1, source_target_pairs={{0,32},{32,0},{1,33},{33,1},{2,34},{34,2},{3,35},{35,3},{4,36},{36... | collective-permute-start | bytes 442376 | tf_op jit(solution)/shard_map/ppermute | solution.py:25
  149.5 7.4 %collective-permute-start.4 = (bf16[8,272,128]{2,1,0:T(8,128)(2,1)S(1)}, bf16[8,272,128]{2,1,0:T(8,128)(2,1)S(1)}, u32[]{:S(2)}, u32[]{:S(2)}) collective-permute-start(bf16[8,272,128]{2,1,0:T(8,128)(2,1)S(1)} %all-to-all-done.6.own_ref), channel_id=1, source_target_pairs={{0,32},{32,0},{1,33},{33,1},{2,34},{34,2},{3,35},{35,3},{4,36},{36... | collective-permute-start | bytes 1671176 | tf_op jit(solution)/shard_map/ppermute | solution.py:25
  157.2 1.4 convolution_add_fusion.product_ref
  158.7 2.5 %shard_map.95 = (f32[288,1024]{1,0:T(8,128)}, f32[8,128]{1,0:T(8,128)}, f32[288,1024]{1,0:T(8,128)}) custom-call(bf16[8,272,128]{2,1,0:T(8,128)(2,1)S(1)} %all-to-all-done.6.own_ref, bf16[8,272,128]{2,1,0:T(8,128)(2,1)S(1)} %collective-permute-done.4.its_ref, bf16[288,256]{1,0:T(8,128)(2,1)S(1)} %copy-done.5, ...), custom_call_target="tpu_custom_call" | custom-call | flops 301989888 | bytes 6291456 | tf_op jit(solution)/shard_map/pallas_call | solution.py:352
  (32 shorter events, 3.1 us)
Async XLA Ops:
  0.6 30.9 %copy-start.3 = (bf16[288,1024]{1,0:T(8,128)(2,1)S(1)}, bf16[288,1024]{1,0:T(8,128)(2,1)}, u32[]{:S(2)}) copy-start(bf16[288,1024]{1,0:T(8,128)(2,1)} %enc_own.1) | copy-start | bytes 1769476
  0.6 0.9 copy-start.6
  1.6 0.7 copy-start.8
  3.0 9.6 %collective-permute-start = (bf16[8,576]{1,0:T(8,128)(2,1)S(1)}, bf16[8,576]{1,0:T(8,128)(2,1)S(1)}, u32[]{:S(2)}, u32[]{:S(2)}) collective-permute-start(bf16[8,576]{1,0:T(8,128)(2,1)S(1)} %get-tuple-element.17), channel_id=1, source_target_pairs={{0,32},{32,0},{1,33},{33,1},{2,34},{34,2},{3,35},{35,3},{4,36},{36... | collective-permute-start | bytes 27656 | tf_op jit(solution)/shard_map/ppermute | solution.py:25
  13.4 18.0 %all-to-all-start = ((bf16[32,8,576]{2,1,0:T(8,128)(2,1)}), bf16[32,8,576]{2,1,0:T(8,128)(2,1)S(1)}, u32[]{:S(2)}, u32[]{:S(2)}) async-start(bf16[32,8,576]{2,1,0:T(8,128)(2,1)} %get-tuple-element.18), calls=%async_computation | async-start | bytes 655360 | tf_op jit(solution)/shard_map/all_to_all | solution.py:21
  20.9 10.6 %collective-permute-start.2 = (bf16[288,1024]{1,0:T(8,128)(2,1)}, bf16[288,1024]{1,0:T(8,128)(2,1)S(1)}, u32[]{:S(2)}, u32[]{:S(2)}) collective-permute-start(bf16[288,1024]{1,0:T(8,128)(2,1)} %enc_own.1), channel_id=1, source_target_pairs={{0,32},{32,0},{1,33},{33,1},{2,34},{34,2},{3,35},{35,3},{4,36},{36... | collective-permute-start | bytes 1769480 | tf_op jit(solution)/shard_map/ppermute | solution.py:25
  23.5 3.3 %collective-permute-start.1 = (f32[288]{0:T(512)}, f32[288]{0:T(512)S(1)}, u32[]{:S(2)}, u32[]{:S(2)}) collective-permute-start(f32[288]{0:T(512)} %param.11), channel_id=1, source_target_pairs={{0,32},{32,0},{1,33},{33,1},{2,34},{34,2},{3,35},{35,3},{4,36},{36... | collective-permute-start | bytes 3464 | tf_op jit(solution)/shard_map/ppermute | solution.py:25
  31.5 8.4 %copy-start = (bf16[1024,288]{0,1:T(8,128)(2,1)S(1)}, bf16[1024,288]{0,1:T(8,128)(2,1)}, u32[]{:S(2)}) copy-start(bf16[1024,288]{0,1:T(8,128)(2,1)} %param.10) | copy-start | bytes 1769476
  32.9 20.0 %copy-start.7 = (f32[1024]{0:T(1024)S(1)}, f32[1024]{0:T(1024)}, u32[]{:S(2)}) copy-start(f32[1024]{0:T(1024)} %param.9) | copy-start | bytes 12292
  32.9 20.0 %all-to-all-start.1 = ((bf16[8,256,128]{2,1,0:T(8,128)(2,1)}), bf16[8,256,128]{2,1,0:T(8,128)(2,1)S(1)}, u32[]{:S(2)}, u32[]{:S(2)}) async-start(bf16[8,256,128]{2,1,0:T(8,128)(2,1)} %shard_map.87), calls=%async_computation.1 | async-start | bytes 1048576 | tf_op jit(solution)/shard_map/all_to_all | solution.py:21
  39.8 7.6 %collective-permute-start.3 = (bf16[288,1024]{1,0:T(8,128)(2,1)S(1)}, bf16[288,1024]{1,0:T(8,128)(2,1)S(1)}, u32[]{:S(2)}, u32[]{:S(2)}) collective-permute-start(bf16[288,1024]{1,0:T(8,128)(2,1)S(1)} %bitcast.16), channel_id=1, source_target_pairs={{0,32},{32,0},{1,33},{33,1},{2,34},{34,2},{3,35},{35,3},{4,36},{36... | collective-permute-start | bytes 1769480 | tf_op jit(solution)/shard_map/ppermute | solution.py:25
  47.4 5.6 %copy-start.1 = (bf16[288,1024]{1,0:T(8,128)(2,1)}, bf16[288,1024]{1,0:T(8,128)(2,1)S(1)}, u32[]{:S(2)}) copy-start(bf16[288,1024]{1,0:T(8,128)(2,1)S(1)} %collective-permute-done.3.dec_other) | copy-start | bytes 1769476
  67.9 1.1 copy-start.2
  70.3 28.1 %all-to-all-start.3 = ((bf16[32,8,576]{2,1,0:T(8,128)(2,1)}), bf16[32,8,576]{2,1,0:T(8,128)(2,1)S(1)}, u32[]{:S(2)}, u32[]{:S(2)}) async-start(bf16[32,8,576]{2,1,0:T(8,128)(2,1)} %get-tuple-element.19), calls=%async_computation.3 | async-start | bytes 655360 | tf_op jit(solution)/shard_map/all_to_all | solution.py:21
  132.0 17.5 %all-to-all-start.6 = ((bf16[8,272,128]{2,1,0:T(8,128)(2,1)}), bf16[8,272,128]{2,1,0:T(8,128)(2,1)S(1)}, u32[]{:S(2)}, u32[]{:S(2)}) async-start(bf16[8,272,128]{2,1,0:T(8,128)(2,1)} %shard_map.92), calls=%async_computation.6 | async-start | bytes 1114112 | tf_op jit(solution)/shard_map/all_to_all | solution.py:21
  135.7 21.5 %collective-permute-start.7 = (bf16[256,1024]{1,0:T(8,128)(2,1)S(1)}, bf16[256,1024]{1,0:T(8,128)(2,1)}, u32[]{:S(2)}, u32[]{:S(2)}) collective-permute-start(bf16[256,1024]{1,0:T(8,128)(2,1)S(1)} %get-tuple-element.24), channel_id=1, source_target_pairs={{0,32},{32,0},{1,33},{33,1},{2,34},{34,2},{3,35},{35,3},{4,36},{36... | collective-permute-start | bytes 1572872 | tf_op jit(solution)/shard_map/ppermute | solution.py:25
  144.3 0.7 copy-start.4
  144.9 13.7 %collective-permute-start.5 = (bf16[288,256]{1,0:T(8,128)(2,1)}, bf16[288,256]{1,0:T(8,128)(2,1)S(1)}, u32[]{:S(2)}, u32[]{:S(2)}) collective-permute-start(bf16[288,256]{1,0:T(8,128)(2,1)} %get-tuple-element.23), channel_id=1, source_target_pairs={{0,32},{32,0},{1,33},{33,1},{2,34},{34,2},{3,35},{35,3},{4,36},{36... | collective-permute-start | bytes 442376 | tf_op jit(solution)/shard_map/ppermute | solution.py:25
  147.0 10.2 %collective-permute-start.6 = (bf16[256,288]{1,0:T(8,128)(2,1)S(1)}, bf16[256,288]{1,0:T(8,128)(2,1)S(1)}, u32[]{:S(2)}, u32[]{:S(2)}) collective-permute-start(bf16[256,288]{1,0:T(8,128)(2,1)S(1)} %slice.13), channel_id=1, source_target_pairs={{0,32},{32,0},{1,33},{33,1},{2,34},{34,2},{3,35},{35,3},{4,36},{36... | collective-permute-start | bytes 442376 | tf_op jit(solution)/shard_map/ppermute | solution.py:25
  149.5 9.2 %collective-permute-start.4 = (bf16[8,272,128]{2,1,0:T(8,128)(2,1)S(1)}, bf16[8,272,128]{2,1,0:T(8,128)(2,1)S(1)}, u32[]{:S(2)}, u32[]{:S(2)}) collective-permute-start(bf16[8,272,128]{2,1,0:T(8,128)(2,1)S(1)} %all-to-all-done.6.own_ref), channel_id=1, source_target_pairs={{0,32},{32,0},{1,33},{33,1},{2,34},{34,2},{3,35},{35,3},{4,36},{36... | collective-permute-start | bytes 1671176 | tf_op jit(solution)/shard_map/ppermute | solution.py:25
  157.2 1.5 copy-start.5

commit v6 on v5

--- a/solution.py
+++ b/solution.py
@@ -96,9 +96,14 @@
             ]
 
 
-def pre_kernel(centered_ref, enc_own, enc_other, out_ref, enc_ref):
+def pre_kernel(centered_ref, enc_own, enc_other, squares_ref, out_ref, enc_ref):
     width, latents = enc_own.shape
     step = 2 * LANES
+    squares = squares_ref[...]
+    high = squares.astype(BF16).astype(F32)
+    parts = jnp.concatenate([high, squares - high], axis=0).astype(BF16)
+    for y in range(out_ref.shape[0]):
+        out_ref[y, pl.ds(out_ref.shape[1] - parts.shape[0], parts.shape[0]), :] = parts
     for n in range(latents // step):
         lanes = pl.ds(n * step, step)
         enc_ref[:width, lanes] = enc_own[:, lanes]
@@ -129,20 +134,29 @@
     return value, small, (soft / SHARPNESS).astype(BF16)
 
 
-def act_kernel(blocks_ref, bias_ref, squares_ref, copies_ref):
-    size = blocks_ref.shape[1]
+def act_kernel(blocks_ref, bias_ref, copies_ref):
+    size = copies_ref.shape[1]
     share = size // bias_ref.shape[0]
     total = sum_blocks(blocks_ref, size)
-    squares = squares_ref[...]
-    high = squares.astype(BF16).astype(F32)
-    parts = jnp.concatenate([high, squares - high], axis=0).astype(BF16)
     for k in range(bias_ref.shape[0]):
         lines = slice(k * share, (k + 1) * share)
         _, _, active = soft_parts(total[lines], bias_ref[k : k + 1, :])
         for y in range(copies_ref.shape[0]):
             copies_ref[y, lines, :] = active
-    for y in range(copies_ref.shape[0]):
-        copies_ref[y, size:, :] = parts
+
+
+def norms_of(blocks_ref, count):
+    return jnp.sqrt(sum_parts(blocks_ref, blocks_ref.shape[1] - 2 * count) + 1e-06)
+
+
+def unit_kernel(blocks_ref, dec_own, dec_other, unit_ref):
+    width, latents = dec_own.shape
+    norms = norms_of(blocks_ref, latents // LANES)
+    for k in range(latents // LANES):
+        lanes = pl.ds(k * LANES, LANES)
+        norm = norms[k : k + 1]
+        unit_ref[:width, lanes] = (dec_own[:, lanes].astype(F32) / norm).astype(BF16)
+        unit_ref[width:, lanes] = (dec_other[:, lanes].astype(F32) / norm).astype(BF16)
 
 
 def join_lanes(copies_ref, active_ref, share, k):
@@ -152,27 +166,18 @@
         ]
 
 
-def rebuild_kernel(copies_ref, dec_own, dec_other, out_ref, unit_ref, active_ref):
-    width, latents = dec_own.shape
-    count = latents // LANES
-    size = copies_ref.shape[1] - 2 * count
-    norms = jnp.sqrt(sum_parts(copies_ref, size) + 1e-06)
+def rebuild_kernel(copies_ref, unit_ref, out_ref, active_ref):
+    count = unit_ref.shape[1] // LANES
     for k in range(count):
-        lanes = pl.ds(k * LANES, LANES)
-        norm = norms[k : k + 1]
-        unit_ref[:width, lanes] = (dec_own[:, lanes].astype(F32) / norm).astype(BF16)
-        unit_ref[width:, lanes] = (dec_other[:, lanes].astype(F32) / norm).astype(BF16)
-        join_lanes(copies_ref, active_ref, size // count, k)
+        join_lanes(copies_ref, active_ref, copies_ref.shape[1] // count, k)
     part = dot(active_ref[...], unit_ref[...], ((1,), (1,)))
     out_ref[...] = part.astype(BF16).reshape(out_ref.shape)
 
 
-def keep_kernel(copies_ref, active_ref, norms_ref):
-    count = norms_ref.shape[0]
-    size = copies_ref.shape[1] - 2 * count
-    norms_ref[...] = jnp.sqrt(sum_parts(copies_ref, size) + 1e-06)
+def keep_kernel(copies_ref, active_ref):
+    count = active_ref.shape[1] // LANES
     for k in range(count):
-        join_lanes(copies_ref, active_ref, size // count, k)
+        join_lanes(copies_ref, active_ref, copies_ref.shape[1] // count, k)
 
 
 def error_kernel(blocks_ref, bias_ref, rows_ref, copies_ref):
@@ -218,11 +223,12 @@
 
 
 def last_kernel(
-    own_ref, its_ref, centered_own, centered_its, product_ref, unit_ref, norms_ref,
+    own_ref, its_ref, centered_own, centered_its, product_ref, unit_ref, blocks_ref,
     enc_out, bias_ref, dec_out,
     own_grad, its_grad, enc_ref, dec_ref, sems,
 ):
-    count = norms_ref.shape[0]
+    count = enc_ref.shape[1] // LANES
+    norms = norms_of(blocks_ref, count)
     size = own_ref.shape[1] - 2 * count
     share = size // count
     dots = sum_parts(own_ref, size) + sum_parts(its_ref, size)
@@ -233,7 +239,7 @@
         for k in (2 * n, 2 * n + 1):
             cut = pl.ds(k * LANES, LANES)
             lines = pl.ds(k * share, share)
-            ratio = 1.0 / norms_ref[k : k + 1, :]
+            ratio = 1.0 / norms[k : k + 1]
             dec_ref[:, cut] = (
                 product_ref[:, cut] - unit_ref[:, cut].astype(F32) * dots[k : k + 1]
             ) * ratio
@@ -290,36 +296,34 @@
     sampled = exchange(copies, TENSOR)
     bias_all = jnp.concatenate([dec_bias, swap(dec_bias)])[None]
     enc_other = swap(enc_weight)
+    dec_own = dec_weight.T
+    dec_other = swap(dec_own)
+    squares = jnp.sum(jnp.square(dec_own.astype(F32)) + jnp.square(dec_other.astype(F32)), axis=0)
     centered = (sampled.reshape(rows, wide).astype(F32) - bias_all).astype(BF16)
     pre_blocks = call(
         pre_kernel,
-        shape((count_y, size, LANES), BF16),
-        [VMEM] * 3,
+        shape((count_y, size + extra, LANES), BF16),
+        [VMEM] * 4,
         (matmul, moved),
         [pltpu.VMEM((wide, latents), BF16)],
-    )(centered, enc_weight, enc_other)
-    dec_own = dec_weight.T
-    dec_other = swap(dec_own)
-    squares = jnp.sum(jnp.square(dec_own.astype(F32)) + jnp.square(dec_other.astype(F32)), axis=0)
+    )(centered, enc_weight, enc_other, squares.reshape(blocks_n, LANES))
     blocks = exchange(pre_blocks, "y")
     enc_bias = enc_bias.reshape(blocks_n, LANES)
     copies = call(
-        act_kernel, shape((count_y, size + extra, LANES), BF16), [VMEM] * 3, (1 << 20, 1 << 20)
-    )(blocks, enc_bias, squares.reshape(blocks_n, LANES))
+        act_kernel, shape((count_y, size, LANES), BF16), [VMEM] * 2, (1 << 20, 1 << 20)
+    )(blocks, enc_bias)
+    unit = call(unit_kernel, shape((wide, latents), BF16), [VMEM] * 3, (1 << 20, moved))(
+        blocks, dec_own, dec_other
+    )
     copies = exchange(copies, "y")
-    partial, unit = call(
+    partial = call(
         rebuild_kernel,
-        (tensor_blocks, shape((wide, latents), BF16)),
-        [VMEM] * 3,
+        tensor_blocks,
+        [VMEM] * 2,
         (matmul, moved),
         [pltpu.VMEM((rows, latents), BF16)],
-    )(copies, dec_own, dec_other)
-    active, norms = call(
-        keep_kernel,
-        (shape((rows, latents), BF16), shape((blocks_n, LANES), F32)),
-        [VMEM],
-        (1 << 20, 1 << 20),
-    )(copies)
+    )(copies, unit)
+    active = call(keep_kernel, shape((rows, latents), BF16), [VMEM], (1 << 20, 1 << 20))(copies)
     its_active = swap(active)
     turned = shape((width, rows), BF16)
     centered_own, centered_other = call(turn_kernel, (turned, turned), [VMEM], (1 << 20, 1 << 20))(
@@ -362,7 +366,7 @@
             pltpu.SemaphoreType.DMA((blocks_n,)),
         ],
         (ANY, VMEM, ANY),
-    )(own, its, centered_own, centered_its, product, unit[:width], norms)
+    )(own, its, centered_own, centered_its, product, unit[:width], blocks)
     return (enc_grad, bias_grad.reshape(latents), dec_grad.T)
 
 

time: 162 us -> 161 us (level)
  starting transfers between devices: 74.8 us -> 66.2 us
  blocking collectives: 46.7 us -> 50.3 us
    all_to_all x4, starting transfers between devices: 36.1 us -> 29.3 us  [exchange(): return lax.all_to_all(blocks, axis, 0, 0, tiled=False)]
    all_to_all x3, blocking collectives: 46.7 us -> 50.3 us  [exchange(): return lax.all_to_all(blocks, axis, 0, 0, tiled=False)]
    all_to_all x4, waiting for transfers between devices: 19 us -> 22.6 us  [exchange(): return lax.all_to_all(blocks, axis, 0, 0, tiled=False)]
    ppermute x8, waiting for transfers between devices: 3.76 us -> 1.83 us  [swap(): return lax.ppermute(block, 'core', [(0, 1), (1, 0)])]
    ppermute x8, starting transfers between devices: 38.7 us -> 36.9 us  [swap(): return lax.ppermute(block, 'core', [(0, 1), (1, 0)])]
    pallas_call x4 -> x5, Pallas kernels: 3.08 us -> 4.24 us  [the longest x1 1.35 us: body(): call(rebuild_kernel, tensor_blocks, [VMEM] * 2, (matmul, moved), [pltpu.V...]
    unnamed x18 -> x14, local copies, waits for them, and re-layouts: 3.34 us -> 2.68 us
  transfers between devices with their start and end apart: 12 -> 12, of which waited for: 6 -> 5; matrix products, arithmetic and copies ran while one was open for 2% -> 2% of each run, Pallas kernels for 1% -> 1%
where the time goes in v6:
time: 161 us; the launch traced here: 160 us
  starting transfers between devices  66.2 us (41%)
  blocking collectives  50.3 us (31%)
  waiting for transfers between devices  24.4 us (15%)
  Pallas kernels  11.2 us (7%)
  local copies, waits for them, and re-layouts  2.84 us (2%)
  matrix products  2.76 us (2%)
    all_to_all x3, blocking collectives, exchange(): return lax.all_to_all(blocks, axis, 0, 0, tiled=False)  50.3 us
    ppermute x8, starting transfers between devices, swap(): return lax.ppermute(block, 'core', [(0, 1), (1, 0)])  36.9 us
    all_to_all x4, starting transfers between devices, exchange(): return lax.all_to_all(blocks, axis, 0, 0, tiled=False)  29.3 us
    all_to_all x4, waiting for transfers between devices, exchange(): return lax.all_to_all(blocks, axis, 0, 0, tiled=False)  22.6 us
    pallas_call x1, Pallas kernels, body(): call(last_kernel, (out, shape((blocks_n, LANES), F32), out), [VMEM] * 7,...  3.55 us
  transfers between devices with their start and end apart: 12, of which 5 were waited for; matrix products, arithmetic and copies ran while one was open for 2% of the time, Pallas kernels for 1%

profile of v6, /device:TPU:1, one launch (start us, length us, event | category | flops | bytes accessed | tf_op | source)
XLA Modules:
  0.0 159.8 jit_solution(8897768739127577567)
XLA Ops:
  0.7 0.9 copy-done.4
  2.2 0.8 shard_map.85
  3.0 8.8 %collective-permute-start = (bf16[8,576]{1,0:T(8,128)(2,1)S(1)}, bf16[8,576]{1,0:T(8,128)(2,1)S(1)}, u32[]{:S(2)}, u32[]{:S(2)}) collective-permute-start(bf16[8,576]{1,0:T(8,128)(2,1)S(1)} %get-tuple-element.13), channel_id=1, source_target_pairs={{0,32},{32,0},{1,33},{33,1},{2,34},{34,2},{3,35},{35,3},{4,36},{36... | collective-permute-start | bytes 27656 | tf_op jit(solution)/shard_map/ppermute | solution.py:25
  11.8 0.8 collective-permute-done.got_ref
  12.7 0.8 shard_map.86
  13.4 7.6 %all-to-all-start = ((bf16[32,8,576]{2,1,0:T(8,128)(2,1)}), bf16[32,8,576]{2,1,0:T(8,128)(2,1)S(1)}, u32[]{:S(2)}, u32[]{:S(2)}) async-start(bf16[32,8,576]{2,1,0:T(8,128)(2,1)} %get-tuple-element.14), calls=%async_computation | async-start | bytes 655360 | tf_op jit(solution)/shard_map/all_to_all | solution.py:21
  21.1 2.5 %collective-permute-start.3 = (bf16[288,1024]{1,0:T(8,128)(2,1)}, bf16[288,1024]{1,0:T(8,128)(2,1)S(1)}, u32[]{:S(2)}, u32[]{:S(2)}) collective-permute-start(bf16[288,1024]{1,0:T(8,128)(2,1)} %bitcast.16), channel_id=1, source_target_pairs={{0,32},{32,0},{1,33},{33,1},{2,34},{34,2},{3,35},{35,3},{4,36},{36... | collective-permute-start | bytes 1769480 | tf_op jit(solution)/shard_map/ppermute | solution.py:25
  23.6 1.9 %collective-permute-start.2 = (bf16[288,1024]{1,0:T(8,128)(2,1)}, bf16[288,1024]{1,0:T(8,128)(2,1)S(1)}, u32[]{:S(2)}, u32[]{:S(2)}) collective-permute-start(bf16[288,1024]{1,0:T(8,128)(2,1)} %enc_own.1), channel_id=1, source_target_pairs={{0,32},{32,0},{1,33},{33,1},{2,34},{34,2},{3,35},{35,3},{4,36},{36... | collective-permute-start | bytes 1769480 | tf_op jit(solution)/shard_map/ppermute | solution.py:25
  25.5 2.4 %collective-permute-start.1 = (f32[288]{0:T(512)}, f32[288]{0:T(512)S(1)}, u32[]{:S(2)}, u32[]{:S(2)}) collective-permute-start(f32[288]{0:T(512)} %param.11), channel_id=1, source_target_pairs={{0,32},{32,0},{1,33},{33,1},{2,34},{34,2},{3,35},{35,3},{4,36},{36... | collective-permute-start | bytes 3464 | tf_op jit(solution)/shard_map/ppermute | solution.py:25
  27.9 1.0 collective-permute-done.1
  29.0 0.8 pad_maximum_fusion
  29.7 1.8 %all-to-all-done = bf16[32,8,576]{2,1,0:T(8,128)(2,1)S(1)} async-done(((bf16[32,8,576]{2,1,0:T(8,128)(2,1)}), bf16[32,8,576]{2,1,0:T(8,128)(2,1)S(1)}, u32[]{:S(2)}, u32[]{:S(2)}) %all-to-all-start) | async-done | bytes 294944 | tf_op jit(solution)/shard_map/all_to_all | solution.py:21
  32.5 20.0 %all_to_all.35.blocks_ref.pre_ref = bf16[8,272,128]{2,1,0:T(8,128)(2,1)S(1)} all-to-all(bf16[8,272,128]{2,1,0:T(8,128)(2,1)S(1)} %shard_map.87), channel_id=1, replica_groups=mesh['y'=8,'core'=2,'x'=4,'z'=8] {'y'}, dimensions={0} | all-to-all | bytes 1114112 | tf_op jit(solution)/shard_map/all_to_all | solution.py:21
  52.5 1.0 shard_map.88
  53.5 3.8 %all-to-all-start.2 = ((bf16[8,256,128]{2,1,0:T(8,128)(2,1)}), bf16[8,256,128]{2,1,0:T(8,128)(2,1)S(1)}, u32[]{:S(2)}, u32[]{:S(2)}) async-start(bf16[8,256,128]{2,1,0:T(8,128)(2,1)} %shard_map.88), calls=%async_computation.2 | async-start | bytes 1048576 | tf_op jit(solution)/shard_map/all_to_all | solution.py:21
  57.3 1.1 copy-done.2
  58.8 10.8 %all-to-all-done.2.copies_ref = bf16[8,256,128]{2,1,0:T(8,128)(2,1)S(1)} async-done(((bf16[8,256,128]{2,1,0:T(8,128)(2,1)}), bf16[8,256,128]{2,1,0:T(8,128)(2,1)S(1)}, u32[]{:S(2)}, u32[]{:S(2)}) %all-to-all-start.2) | async-done | bytes 524320 | tf_op jit(solution)/shard_map/all_to_all | solution.py:21
  69.5 1.3 shard_map.90
  70.9 13.7 %all-to-all-start.3 = ((bf16[32,8,576]{2,1,0:T(8,128)(2,1)}), bf16[32,8,576]{2,1,0:T(8,128)(2,1)S(1)}, u32[]{:S(2)}, u32[]{:S(2)}) async-start(bf16[32,8,576]{2,1,0:T(8,128)(2,1)} %shard_map.90), calls=%async_computation.3 | async-start | bytes 655360 | tf_op jit(solution)/shard_map/all_to_all | solution.py:21
  84.6 10.0 %all-to-all-done.3.blocks_ref = bf16[32,8,576]{2,1,0:T(8,128)(2,1)S(1)} async-done(((bf16[32,8,576]{2,1,0:T(8,128)(2,1)}), bf16[32,8,576]{2,1,0:T(8,128)(2,1)S(1)}, u32[]{:S(2)}, u32[]{:S(2)}) %all-to-all-start.3) | async-done | bytes 294944 | tf_op jit(solution)/shard_map/all_to_all | solution.py:21
  94.7 14.7 %all_to_all.36.error_ref = bf16[32,8,576]{2,1,0:T(8,128)(2,1)S(1)} all-to-all(bf16[32,8,576]{2,1,0:T(8,128)(2,1)S(1)} %shard_map.91), channel_id=1, replica_groups=mesh['y'=8,'core'=2,'x'=4,'z'=8] {'x','z'}, dimensions={0} | all-to-all | bytes 589824 | tf_op jit(solution)/shard_map/all_to_all | solution.py:21
  110.0 15.6 %all_to_all.37.blocks_ref = bf16[8,256,128]{2,1,0:T(8,128)(2,1)S(1)} all-to-all(bf16[8,256,128]{2,1,0:T(8,128)(2,1)S(1)} %shard_map.92), channel_id=1, replica_groups=mesh['y'=8,'core'=2,'x'=4,'z'=8] {'y'}, dimensions={0} | all-to-all | bytes 1048576 | tf_op jit(solution)/shard_map/all_to_all | solution.py:21
  125.6 1.1 shard_map.93
  126.7 4.2 %all-to-all-start.6 = ((bf16[8,272,128]{2,1,0:T(8,128)(2,1)}), bf16[8,272,128]{2,1,0:T(8,128)(2,1)}, u32[]{:S(2)}, u32[]{:S(2)}) async-start(bf16[8,272,128]{2,1,0:T(8,128)(2,1)} %shard_map.93), calls=%async_computation.6 | async-start | bytes 1114112 | tf_op jit(solution)/shard_map/all_to_all | solution.py:21
  130.9 0.9 shard_map.95
  131.8 8.9 %collective-permute-start.7 = (bf16[256,1024]{1,0:T(8,128)(2,1)}, bf16[256,1024]{1,0:T(8,128)(2,1)}, u32[]{:S(2)}, u32[]{:S(2)}) collective-permute-start(bf16[256,1024]{1,0:T(8,128)(2,1)} %shard_map.95), channel_id=1, source_target_pairs={{0,32},{32,0},{1,33},{33,1},{2,34},{34,2},{3,35},{35,3},{4,36},{36... | collective-permute-start | bytes 1572872 | tf_op jit(solution)/shard_map/ppermute | solution.py:25
  140.9 1.9 %collective-permute-start.5 = (bf16[288,256]{1,0:T(8,128)(2,1)S(1)}, bf16[288,256]{1,0:T(8,128)(2,1)S(1)}, u32[]{:S(2)}, u32[]{:S(2)}) collective-permute-start(bf16[288,256]{1,0:T(8,128)(2,1)S(1)} %get-tuple-element.17), channel_id=1, source_target_pairs={{0,32},{32,0},{1,33},{33,1},{2,34},{34,2},{3,35},{35,3},{4,36},{36... | collective-permute-start | bytes 442376 | tf_op jit(solution)/shard_map/ppermute | solution.py:25
  143.0 2.4 %collective-permute-start.6 = (bf16[256,288]{1,0:T(8,128)(2,1)S(1)}, bf16[256,288]{1,0:T(8,128)(2,1)S(1)}, u32[]{:S(2)}, u32[]{:S(2)}) collective-permute-start(bf16[256,288]{1,0:T(8,128)(2,1)S(1)} %slice.13), channel_id=1, source_target_pairs={{0,32},{32,0},{1,33},{33,1},{2,34},{34,2},{3,35},{35,3},{4,36},{36... | collective-permute-start | bytes 442376 | tf_op jit(solution)/shard_map/ppermute | solution.py:25
  145.5 8.0 %collective-permute-start.4 = (bf16[8,272,128]{2,1,0:T(8,128)(2,1)}, bf16[8,272,128]{2,1,0:T(8,128)(2,1)S(1)}, u32[]{:S(2)}, u32[]{:S(2)}) collective-permute-start(bf16[8,272,128]{2,1,0:T(8,128)(2,1)} %all-to-all-done.6.own_ref), channel_id=1, source_target_pairs={{0,32},{32,0},{1,33},{33,1},{2,34},{34,2},{3,35},{35,3},{4,36},{36... | collective-permute-start | bytes 1671176 | tf_op jit(solution)/shard_map/ppermute | solution.py:25
  153.5 1.4 fusion.1
  154.9 1.4 convolution_add_fusion.product_ref
  156.3 3.5 %shard_map.96 = (f32[288,1024]{1,0:T(8,128)}, f32[8,128]{1,0:T(8,128)}, f32[288,1024]{1,0:T(8,128)}) custom-call(bf16[8,272,128]{2,1,0:T(8,128)(2,1)} %all-to-all-done.6.own_ref, bf16[8,272,128]{2,1,0:T(8,128)(2,1)S(1)} %collective-permute-done.4.its_ref, bf16[288,256]{1,0:T(8,128)(2,1)S(1)} %get-tuple-element.16.centered_own, ...), custom_call_target="tpu_custom_call" | custom-call | flops 301989888 | bytes 6291456 | tf_op jit(solution)/shard_map/pallas_call | solution.py:356
  (29 shorter events, 3.0 us)
Async XLA Ops:
  0.6 31.0 %copy-start = (bf16[1024,288]{0,1:T(8,128)(2,1)S(1)}, bf16[1024,288]{0,1:T(8,128)(2,1)}, u32[]{:S(2)}) copy-start(bf16[1024,288]{0,1:T(8,128)(2,1)} %param.10) | copy-start | bytes 1769476
  0.6 0.9 copy-start.4
  1.6 0.7 copy-start.6
  3.0 9.6 %collective-permute-start = (bf16[8,576]{1,0:T(8,128)(2,1)S(1)}, bf16[8,576]{1,0:T(8,128)(2,1)S(1)}, u32[]{:S(2)}, u32[]{:S(2)}) collective-permute-start(bf16[8,576]{1,0:T(8,128)(2,1)S(1)} %get-tuple-element.13), channel_id=1, source_target_pairs={{0,32},{32,0},{1,33},{33,1},{2,34},{34,2},{3,35},{35,3},{4,36},{36... | collective-permute-start | bytes 27656 | tf_op jit(solution)/shard_map/ppermute | solution.py:25
  13.4 18.5 %copy-start.3 = (bf16[288,1024]{1,0:T(8,128)(2,1)S(1)}, bf16[288,1024]{1,0:T(8,128)(2,1)}, u32[]{:S(2)}) copy-start(bf16[288,1024]{1,0:T(8,128)(2,1)} %enc_own.1) | copy-start | bytes 1769476
  13.4 18.1 %all-to-all-start = ((bf16[32,8,576]{2,1,0:T(8,128)(2,1)}), bf16[32,8,576]{2,1,0:T(8,128)(2,1)S(1)}, u32[]{:S(2)}, u32[]{:S(2)}) async-start(bf16[32,8,576]{2,1,0:T(8,128)(2,1)} %get-tuple-element.14), calls=%async_computation | async-start | bytes 655360 | tf_op jit(solution)/shard_map/all_to_all | solution.py:21
  21.1 10.6 %collective-permute-start.3 = (bf16[288,1024]{1,0:T(8,128)(2,1)}, bf16[288,1024]{1,0:T(8,128)(2,1)S(1)}, u32[]{:S(2)}, u32[]{:S(2)}) collective-permute-start(bf16[288,1024]{1,0:T(8,128)(2,1)} %bitcast.16), channel_id=1, source_target_pairs={{0,32},{32,0},{1,33},{33,1},{2,34},{34,2},{3,35},{35,3},{4,36},{36... | collective-permute-start | bytes 1769480 | tf_op jit(solution)/shard_map/ppermute | solution.py:25
  23.6 8.3 %collective-permute-start.2 = (bf16[288,1024]{1,0:T(8,128)(2,1)}, bf16[288,1024]{1,0:T(8,128)(2,1)S(1)}, u32[]{:S(2)}, u32[]{:S(2)}) collective-permute-start(bf16[288,1024]{1,0:T(8,128)(2,1)} %enc_own.1), channel_id=1, source_target_pairs={{0,32},{32,0},{1,33},{33,1},{2,34},{34,2},{3,35},{35,3},{4,36},{36... | collective-permute-start | bytes 1769480 | tf_op jit(solution)/shard_map/ppermute | solution.py:25
  25.5 3.4 %collective-permute-start.1 = (f32[288]{0:T(512)}, f32[288]{0:T(512)S(1)}, u32[]{:S(2)}, u32[]{:S(2)}) collective-permute-start(f32[288]{0:T(512)} %param.11), channel_id=1, source_target_pairs={{0,32},{32,0},{1,33},{33,1},{2,34},{34,2},{3,35},{35,3},{4,36},{36... | collective-permute-start | bytes 3464 | tf_op jit(solution)/shard_map/ppermute | solution.py:25
  31.6 0.9 copy-start.1
  31.9 20.6 %copy-start.5 = (f32[1024]{0:T(1024)S(1)}, f32[1024]{0:T(1024)}, u32[]{:S(2)}) copy-start(f32[1024]{0:T(1024)} %param.9) | copy-start | bytes 12292
  53.5 16.1 %all-to-all-start.2 = ((bf16[8,256,128]{2,1,0:T(8,128)(2,1)}), bf16[8,256,128]{2,1,0:T(8,128)(2,1)S(1)}, u32[]{:S(2)}, u32[]{:S(2)}) async-start(bf16[8,256,128]{2,1,0:T(8,128)(2,1)} %shard_map.88), calls=%async_computation.2 | async-start | bytes 1048576 | tf_op jit(solution)/shard_map/all_to_all | solution.py:21
  57.3 1.1 copy-start.2
  70.9 23.7 %all-to-all-start.3 = ((bf16[32,8,576]{2,1,0:T(8,128)(2,1)}), bf16[32,8,576]{2,1,0:T(8,128)(2,1)S(1)}, u32[]{:S(2)}, u32[]{:S(2)}) async-start(bf16[32,8,576]{2,1,0:T(8,128)(2,1)} %shard_map.90), calls=%async_computation.3 | async-start | bytes 655360 | tf_op jit(solution)/shard_map/all_to_all | solution.py:21
  126.7 18.8 %all-to-all-start.6 = ((bf16[8,272,128]{2,1,0:T(8,128)(2,1)}), bf16[8,272,128]{2,1,0:T(8,128)(2,1)}, u32[]{:S(2)}, u32[]{:S(2)}) async-start(bf16[8,272,128]{2,1,0:T(8,128)(2,1)} %shard_map.93), calls=%async_computation.6 | async-start | bytes 1114112 | tf_op jit(solution)/shard_map/all_to_all | solution.py:21
  131.8 23.0 %collective-permute-start.7 = (bf16[256,1024]{1,0:T(8,128)(2,1)}, bf16[256,1024]{1,0:T(8,128)(2,1)}, u32[]{:S(2)}, u32[]{:S(2)}) collective-permute-start(bf16[256,1024]{1,0:T(8,128)(2,1)} %shard_map.95), channel_id=1, source_target_pairs={{0,32},{32,0},{1,33},{33,1},{2,34},{34,2},{3,35},{35,3},{4,36},{36... | collective-permute-start | bytes 1572872 | tf_op jit(solution)/shard_map/ppermute | solution.py:25
  140.9 15.3 %collective-permute-start.5 = (bf16[288,256]{1,0:T(8,128)(2,1)S(1)}, bf16[288,256]{1,0:T(8,128)(2,1)S(1)}, u32[]{:S(2)}, u32[]{:S(2)}) collective-permute-start(bf16[288,256]{1,0:T(8,128)(2,1)S(1)} %get-tuple-element.17), channel_id=1, source_target_pairs={{0,32},{32,0},{1,33},{33,1},{2,34},{34,2},{3,35},{35,3},{4,36},{36... | collective-permute-start | bytes 442376 | tf_op jit(solution)/shard_map/ppermute | solution.py:25
  143.0 11.8 %collective-permute-start.6 = (bf16[256,288]{1,0:T(8,128)(2,1)S(1)}, bf16[256,288]{1,0:T(8,128)(2,1)S(1)}, u32[]{:S(2)}, u32[]{:S(2)}) collective-permute-start(bf16[256,288]{1,0:T(8,128)(2,1)S(1)} %slice.13), channel_id=1, source_target_pairs={{0,32},{32,0},{1,33},{33,1},{2,34},{34,2},{3,35},{35,3},{4,36},{36... | collective-permute-start | bytes 442376 | tf_op jit(solution)/shard_map/ppermute | solution.py:25
  145.5 10.8 %collective-permute-start.4 = (bf16[8,272,128]{2,1,0:T(8,128)(2,1)}, bf16[8,272,128]{2,1,0:T(8,128)(2,1)S(1)}, u32[]{:S(2)}, u32[]{:S(2)}) collective-permute-start(bf16[8,272,128]{2,1,0:T(8,128)(2,1)} %all-to-all-done.6.own_ref), channel_id=1, source_target_pairs={{0,32},{32,0},{1,33},{33,1},{2,34},{34,2},{3,35},{35,3},{4,36},{36... | collective-permute-start | bytes 1671176 | tf_op jit(solution)/shard_map/ppermute | solution.py:25

commit v7 on v6

--- a/solution.py
+++ b/solution.py
@@ -222,16 +222,33 @@
         copies_ref[y, size:, :] = parts
 
 
+def own_kernel(own_ref, centered_ref, blocks_ref, enc_ref, sums_ref, grad_ref):
+    count = enc_ref.shape[1] // LANES
+    size = own_ref.shape[1] - 2 * count
+    share = size // count
+    for k in range(count):
+        cut = pl.ds(k * LANES, LANES)
+        lines = pl.ds(k * share, share)
+        total = jnp.zeros((share, LANES), F32)
+        for y in range(own_ref.shape[0]):
+            value = own_ref[y, lines, :]
+            grad_ref[pl.ds(y * share, share), cut] = value
+            total = total + value.astype(F32)
+        sums_ref[k : k + 1, :] = jnp.sum(total, axis=0, keepdims=True)
+    sums_ref[count : 2 * count] = sum_parts(own_ref, size)
+    sums_ref[2 * count :] = 1.0 / norms_of(blocks_ref, count)
+    enc_ref[...] = dot(centered_ref[...], grad_ref[...], ((1,), (0,)))
+
+
 def last_kernel(
-    own_ref, its_ref, centered_own, centered_its, product_ref, unit_ref, blocks_ref,
+    its_ref, part_ref, sums_ref, centered_ref, product_ref, unit_ref,
     enc_out, bias_ref, dec_out,
-    own_grad, its_grad, enc_ref, dec_ref, sems,
+    grad_ref, enc_ref, dec_ref, sems,
 ):
     count = enc_ref.shape[1] // LANES
-    norms = norms_of(blocks_ref, count)
-    size = own_ref.shape[1] - 2 * count
+    size = its_ref.shape[1] - 2 * count
     share = size // count
-    dots = sum_parts(own_ref, size) + sum_parts(its_ref, size)
+    dots = sums_ref[count : 2 * count] + sum_parts(its_ref, size)
     step = 2 * LANES
     copies = []
     for n in range(count // 2):
@@ -239,21 +256,20 @@
         for k in (2 * n, 2 * n + 1):
             cut = pl.ds(k * LANES, LANES)
             lines = pl.ds(k * share, share)
-            ratio = 1.0 / norms[k : k + 1]
+            ratio = sums_ref[2 * count + k : 2 * count + k + 1]
             dec_ref[:, cut] = (
                 product_ref[:, cut] - unit_ref[:, cut].astype(F32) * dots[k : k + 1]
             ) * ratio
             total = jnp.zeros((share, LANES), F32)
-            for y in range(own_ref.shape[0]):
-                a, b = own_ref[y, lines, :], its_ref[y, lines, :]
-                own_grad[pl.ds(y * share, share), cut] = a
-                its_grad[pl.ds(y * share, share), cut] = b
-                total = total + a.astype(F32) + b.astype(F32)
-            bias_ref[k : k + 1, :] = jnp.sum(total, axis=0, keepdims=True)
+            for y in range(its_ref.shape[0]):
+                value = its_ref[y, lines, :]
+                grad_ref[pl.ds(y * share, share), cut] = value
+                total = total + value.astype(F32)
+            bias_ref[k : k + 1, :] = sums_ref[k : k + 1, :] + jnp.sum(total, axis=0, keepdims=True)
         copies.append(pltpu.make_async_copy(dec_ref.at[:, lanes], dec_out.at[:, lanes], sems.at[2 * n]))
         copies[-1].start()
-        enc_ref[:, lanes] = dot(centered_own[...], own_grad[:, lanes], ((1,), (0,))) + dot(
-            centered_its[...], its_grad[:, lanes], ((1,), (0,))
+        enc_ref[:, lanes] = part_ref[:, lanes] + dot(
+            centered_ref[...], grad_ref[:, lanes], ((1,), (0,))
         )
         copies.append(
             pltpu.make_async_copy(enc_ref.at[:, lanes], enc_out.at[:, lanes], sems.at[2 * n + 1])
@@ -294,7 +310,7 @@
         own_rows, swap(other_rows)
     )
     sampled = exchange(copies, TENSOR)
-    bias_all = jnp.concatenate([dec_bias, swap(dec_bias)])[None]
+    bias_all = jnp.concatenate([dec_bias[None], swap(dec_bias)[None]], axis=1)
     enc_other = swap(enc_weight)
     dec_own = dec_weight.T
     dec_other = swap(dec_own)
@@ -353,20 +369,26 @@
     )
     its = swap(own)
     out = shape((width, latents), F32)
+    enc_part, sums = call(
+        own_kernel,
+        (out, shape((3 * blocks_n, LANES), F32)),
+        [VMEM] * 3,
+        (40 * matmul, 20 * moved),
+        [pltpu.VMEM((rows, latents), BF16)],
+    )(own, centered_own, blocks)
     enc_grad, bias_grad, dec_grad = call(
         last_kernel,
         (out, shape((blocks_n, LANES), F32), out),
-        [VMEM] * 7,
+        [VMEM] * 6,
         (matmul, 2 * moved),
         [
-            pltpu.VMEM((rows, latents), BF16),
             pltpu.VMEM((rows, latents), BF16),
             pltpu.VMEM((width, latents), F32),
             pltpu.VMEM((width, latents), F32),
             pltpu.SemaphoreType.DMA((blocks_n,)),
         ],
         (ANY, VMEM, ANY),
-    )(own, its, centered_own, centered_its, product, unit[:width], blocks)
+    )(its, enc_part, sums, centered_its, product, unit[:width])
     return (enc_grad, bias_grad.reshape(latents), dec_grad.T)
 
 

time: 161 us -> 157 us (0.975)
  blocking collectives: 50.3 us -> 73.7 us
  starting transfers between devices: 66.2 us -> 51.9 us
  waiting for transfers between devices: 24.4 us -> 15.4 us
  matrix products: 2.76 us -> 0.67 us
    all_to_all x3 -> x4, blocking collectives: 50.3 us -> 73.7 us  [exchange(): return lax.all_to_all(blocks, axis, 0, 0, tiled=False)]
    all_to_all x4 -> x3, starting transfers between devices: 29.3 us -> 15.6 us  [exchange(): return lax.all_to_all(blocks, axis, 0, 0, tiled=False)]
    all_to_all x4 -> x3, waiting for transfers between devices: 22.6 us -> 13.3 us  [exchange(): return lax.all_to_all(blocks, axis, 0, 0, tiled=False)]
    dot_general x2, matrix products: 2.76 us -> 0.67 us  [dot(): return lax.dot_general(a, b, (dims, ((), ())), preferred_element_type=F32)]
    pallas_call x1 -> x2, Pallas kernels: 3.55 us -> 3.82 us  [the longest x1 2.4 us: body(): call(last_kernel, (out, shape((blocks_n, LANES), F32), out), [VMEM] * 6,...]
  transfers between devices with their start and end apart: 12 -> 11, of which waited for: 5 -> 6; matrix products, arithmetic and copies ran while one was open for 2% -> 1% of each run, Pallas kernels for 1% -> 1%
where the time goes in v7:
time: 157 us
  blocking collectives  73.7 us (47%)
  starting transfers between devices  51.9 us (33%)
  waiting for transfers between devices  15.4 us (10%)
  Pallas kernels  9.98 us (6%)
  local copies, waits for them, and re-layouts  3.53 us (2%)
    all_to_all x4, blocking collectives, exchange(): return lax.all_to_all(blocks, axis, 0, 0, tiled=False)  73.7 us
    ppermute x8, starting transfers between devices, swap(): return lax.ppermute(block, 'core', [(0, 1), (1, 0)])  36.3 us
    all_to_all x3, starting transfers between devices, exchange(): return lax.all_to_all(blocks, axis, 0, 0, tiled=False)  15.6 us
    all_to_all x3, waiting for transfers between devices, exchange(): return lax.all_to_all(blocks, axis, 0, 0, tiled=False)  13.3 us
  transfers between devices with their start and end apart: 11, of which 6 were waited for; matrix products, arithmetic and copies ran while one was open for 1% of the time, Pallas kernels for 1%

profile of v7, /device:TPU:1, one launch (start us, length us, event | category | flops | bytes accessed | tf_op | source)
XLA Modules:
  0.0 156.6 jit_solution(195606336095476466)
XLA Ops:
  0.7 0.9 copy-done.4
  1.6 0.7 copy-done.6
  2.2 0.8 shard_map.85
  3.0 8.8 %collective-permute-start = (bf16[8,576]{1,0:T(8,128)(2,1)S(1)}, bf16[8,576]{1,0:T(8,128)(2,1)S(1)}, u32[]{:S(2)}, u32[]{:S(2)}) collective-permute-start(bf16[8,576]{1,0:T(8,128)(2,1)S(1)} %get-tuple-element.15), channel_id=1, source_target_pairs={{0,32},{32,0},{1,33},{33,1},{2,34},{34,2},{3,35},{35,3},{4,36},{36... | collective-permute-start | bytes 27656 | tf_op jit(solution)/shard_map/ppermute | solution.py:25
  11.8 0.8 collective-permute-done.got_ref
  12.7 0.8 shard_map.86
  13.4 7.6 %all-to-all-start = ((bf16[32,8,576]{2,1,0:T(8,128)(2,1)}), bf16[32,8,576]{2,1,0:T(8,128)(2,1)S(1)}, u32[]{:S(2)}, u32[]{:S(2)}) async-start(bf16[32,8,576]{2,1,0:T(8,128)(2,1)} %get-tuple-element.16), calls=%async_computation | async-start | bytes 655360 | tf_op jit(solution)/shard_map/all_to_all | solution.py:21
  21.1 2.5 %collective-permute-start.3 = (bf16[288,1024]{1,0:T(8,128)(2,1)}, bf16[288,1024]{1,0:T(8,128)(2,1)S(1)}, u32[]{:S(2)}, u32[]{:S(2)}) collective-permute-start(bf16[288,1024]{1,0:T(8,128)(2,1)} %bitcast.16), channel_id=1, source_target_pairs={{0,32},{32,0},{1,33},{33,1},{2,34},{34,2},{3,35},{35,3},{4,36},{36... | collective-permute-start | bytes 1769480 | tf_op jit(solution)/shard_map/ppermute | solution.py:25
  23.6 1.9 %collective-permute-start.2 = (bf16[288,1024]{1,0:T(8,128)(2,1)}, bf16[288,1024]{1,0:T(8,128)(2,1)S(1)}, u32[]{:S(2)}, u32[]{:S(2)}) collective-permute-start(bf16[288,1024]{1,0:T(8,128)(2,1)} %enc_own.1), channel_id=1, source_target_pairs={{0,32},{32,0},{1,33},{33,1},{2,34},{34,2},{3,35},{35,3},{4,36},{36... | collective-permute-start | bytes 1769480 | tf_op jit(solution)/shard_map/ppermute | solution.py:25
  25.5 2.4 %collective-permute-start.1 = (f32[288]{0:T(512)}, f32[288]{0:T(512)S(1)}, u32[]{:S(2)}, u32[]{:S(2)}) collective-permute-start(f32[288]{0:T(512)} %param.11), channel_id=1, source_target_pairs={{0,32},{32,0},{1,33},{33,1},{2,34},{34,2},{3,35},{35,3},{4,36},{36... | collective-permute-start | bytes 3464 | tf_op jit(solution)/shard_map/ppermute | solution.py:25
  27.9 0.7 broadcast_in_dim.6
  29.1 2.5 %all-to-all-done = bf16[32,8,576]{2,1,0:T(8,128)(2,1)S(1)} async-done(((bf16[32,8,576]{2,1,0:T(8,128)(2,1)}), bf16[32,8,576]{2,1,0:T(8,128)(2,1)S(1)}, u32[]{:S(2)}, u32[]{:S(2)}) %all-to-all-start) | async-done | bytes 294944 | tf_op jit(solution)/shard_map/all_to_all | solution.py:21
  31.9 0.6 shard_map.87
  32.5 20.0 %all_to_all.35.blocks_ref.pre_ref = bf16[8,272,128]{2,1,0:T(8,128)(2,1)S(1)} all-to-all(bf16[8,272,128]{2,1,0:T(8,128)(2,1)S(1)} %shard_map.87), channel_id=1, replica_groups=mesh['y'=8,'core'=2,'x'=4,'z'=8] {'y'}, dimensions={0} | all-to-all | bytes 1114112 | tf_op jit(solution)/shard_map/all_to_all | solution.py:21
  52.5 1.0 shard_map.88
  53.5 3.8 %all-to-all-start.2 = ((bf16[8,256,128]{2,1,0:T(8,128)(2,1)}), bf16[8,256,128]{2,1,0:T(8,128)(2,1)S(1)}, u32[]{:S(2)}, u32[]{:S(2)}) async-start(bf16[8,256,128]{2,1,0:T(8,128)(2,1)} %shard_map.88), calls=%async_computation.2 | async-start | bytes 1048576 | tf_op jit(solution)/shard_map/all_to_all | solution.py:21
  57.3 1.1 copy-done.2
  58.8 10.8 %all-to-all-done.2.copies_ref = bf16[8,256,128]{2,1,0:T(8,128)(2,1)S(1)} async-done(((bf16[8,256,128]{2,1,0:T(8,128)(2,1)}), bf16[8,256,128]{2,1,0:T(8,128)(2,1)S(1)}, u32[]{:S(2)}, u32[]{:S(2)}) %all-to-all-start.2) | async-done | bytes 524320 | tf_op jit(solution)/shard_map/all_to_all | solution.py:21
  69.5 0.6 shard_map.90
  70.2 23.5 %all_to_all.36.blocks_ref = bf16[32,8,576]{2,1,0:T(8,128)(2,1)S(1)} all-to-all(bf16[32,8,576]{2,1,0:T(8,128)(2,1)S(1)} %shard_map.90), channel_id=1, replica_groups=mesh['y'=8,'core'=2,'x'=4,'z'=8] {'x','z'}, dimensions={0} | all-to-all | bytes 589824 | tf_op jit(solution)/shard_map/all_to_all | solution.py:21
  93.8 14.7 %all_to_all.37.error_ref = bf16[32,8,576]{2,1,0:T(8,128)(2,1)S(1)} all-to-all(bf16[32,8,576]{2,1,0:T(8,128)(2,1)S(1)} %shard_map.91), channel_id=1, replica_groups=mesh['y'=8,'core'=2,'x'=4,'z'=8] {'x','z'}, dimensions={0} | all-to-all | bytes 589824 | tf_op jit(solution)/shard_map/all_to_all | solution.py:21
  108.5 0.6 shard_map.92
  109.1 15.5 %all_to_all.38.blocks_ref = bf16[8,256,128]{2,1,0:T(8,128)(2,1)S(1)} all-to-all(bf16[8,256,128]{2,1,0:T(8,128)(2,1)S(1)} %shard_map.92), channel_id=1, replica_groups=mesh['y'=8,'core'=2,'x'=4,'z'=8] {'y'}, dimensions={0} | all-to-all | bytes 1048576 | tf_op jit(solution)/shard_map/all_to_all | solution.py:21
  124.6 1.1 shard_map.93
  125.6 4.2 %all-to-all-start.6 = ((bf16[8,272,128]{2,1,0:T(8,128)(2,1)}), bf16[8,272,128]{2,1,0:T(8,128)(2,1)}, u32[]{:S(2)}, u32[]{:S(2)}) async-start(bf16[8,272,128]{2,1,0:T(8,128)(2,1)} %shard_map.93), calls=%async_computation.6 | async-start | bytes 1114112 | tf_op jit(solution)/shard_map/all_to_all | solution.py:21
  130.0 8.9 %collective-permute-start.7 = (bf16[256,1024]{1,0:T(8,128)(2,1)S(1)}, bf16[256,1024]{1,0:T(8,128)(2,1)S(1)}, u32[]{:S(2)}, u32[]{:S(2)}) collective-permute-start(bf16[256,1024]{1,0:T(8,128)(2,1)S(1)} %shard_map.96), channel_id=1, source_target_pairs={{0,32},{32,0},{1,33},{33,1},{2,34},{34,2},{3,35},{35,3},{4,36},{36... | collective-permute-start | bytes 1572872 | tf_op jit(solution)/shard_map/ppermute | solution.py:25
  139.1 1.9 %collective-permute-start.5 = (bf16[288,256]{1,0:T(8,128)(2,1)S(1)}, bf16[288,256]{1,0:T(8,128)(2,1)S(1)}, u32[]{:S(2)}, u32[]{:S(2)}) collective-permute-start(bf16[288,256]{1,0:T(8,128)(2,1)S(1)} %get-tuple-element.21), channel_id=1, source_target_pairs={{0,32},{32,0},{1,33},{33,1},{2,34},{34,2},{3,35},{35,3},{4,36},{36... | collective-permute-start | bytes 442376 | tf_op jit(solution)/shard_map/ppermute | solution.py:25
  141.2 2.4 %collective-permute-start.6 = (bf16[256,288]{1,0:T(8,128)(2,1)S(1)}, bf16[256,288]{1,0:T(8,128)(2,1)S(1)}, u32[]{:S(2)}, u32[]{:S(2)}) collective-permute-start(bf16[256,288]{1,0:T(8,128)(2,1)S(1)} %slice.13), channel_id=1, source_target_pairs={{0,32},{32,0},{1,33},{33,1},{2,34},{34,2},{3,35},{35,3},{4,36},{36... | collective-permute-start | bytes 442376 | tf_op jit(solution)/shard_map/ppermute | solution.py:25
  144.0 0.7 collective-permute-done.6
  145.0 7.4 %collective-permute-start.4 = (bf16[8,272,128]{2,1,0:T(8,128)(2,1)}, bf16[8,272,128]{2,1,0:T(8,128)(2,1)S(1)}, u32[]{:S(2)}, u32[]{:S(2)}) collective-permute-start(bf16[8,272,128]{2,1,0:T(8,128)(2,1)} %all-to-all-done.6.own_ref), channel_id=1, source_target_pairs={{0,32},{32,0},{1,33},{33,1},{2,34},{34,2},{3,35},{35,3},{4,36},{36... | collective-permute-start | bytes 1671176 | tf_op jit(solution)/shard_map/ppermute | solution.py:25
  152.4 1.4 shard_map.95
  154.2 2.4 %shard_map.97 = (f32[288,1024]{1,0:T(8,128)}, f32[8,128]{1,0:T(8,128)}, f32[288,1024]{1,0:T(8,128)}) custom-call(bf16[8,272,128]{2,1,0:T(8,128)(2,1)S(1)} %collective-permute-done.4.its_ref, f32[288,1024]{1,0:T(8,128)S(1)} %get-tuple-element.19.part_ref, f32[24,128]{1,0:T(8,128)S(1)} %get-tuple-element.20.sums_ref, ...), custom_call_target="tpu_custom_call" | custom-call | flops 301989888 | bytes 6291456 | tf_op jit(solution)/shard_map/pallas_call | solution.py:379
  (30 shorter events, 2.7 us)
Async XLA Ops:
  0.6 31.0 %copy-start = (bf16[1024,288]{0,1:T(8,128)(2,1)S(1)}, bf16[1024,288]{0,1:T(8,128)(2,1)}, u32[]{:S(2)}) copy-start(bf16[1024,288]{0,1:T(8,128)(2,1)} %param.10) | copy-start | bytes 1769476
  0.6 0.9 copy-start.4
  1.6 0.7 copy-start.6
  3.0 9.6 %collective-permute-start = (bf16[8,576]{1,0:T(8,128)(2,1)S(1)}, bf16[8,576]{1,0:T(8,128)(2,1)S(1)}, u32[]{:S(2)}, u32[]{:S(2)}) collective-permute-start(bf16[8,576]{1,0:T(8,128)(2,1)S(1)} %get-tuple-element.15), channel_id=1, source_target_pairs={{0,32},{32,0},{1,33},{33,1},{2,34},{34,2},{3,35},{35,3},{4,36},{36... | collective-permute-start | bytes 27656 | tf_op jit(solution)/shard_map/ppermute | solution.py:25
  13.4 18.5 %copy-start.3 = (bf16[288,1024]{1,0:T(8,128)(2,1)S(1)}, bf16[288,1024]{1,0:T(8,128)(2,1)}, u32[]{:S(2)}) copy-start(bf16[288,1024]{1,0:T(8,128)(2,1)} %enc_own.1) | copy-start | bytes 1769476
  13.4 18.1 %all-to-all-start = ((bf16[32,8,576]{2,1,0:T(8,128)(2,1)}), bf16[32,8,576]{2,1,0:T(8,128)(2,1)S(1)}, u32[]{:S(2)}, u32[]{:S(2)}) async-start(bf16[32,8,576]{2,1,0:T(8,128)(2,1)} %get-tuple-element.16), calls=%async_computation | async-start | bytes 655360 | tf_op jit(solution)/shard_map/all_to_all | solution.py:21
  21.1 10.6 %collective-permute-start.3 = (bf16[288,1024]{1,0:T(8,128)(2,1)}, bf16[288,1024]{1,0:T(8,128)(2,1)S(1)}, u32[]{:S(2)}, u32[]{:S(2)}) collective-permute-start(bf16[288,1024]{1,0:T(8,128)(2,1)} %bitcast.16), channel_id=1, source_target_pairs={{0,32},{32,0},{1,33},{33,1},{2,34},{34,2},{3,35},{35,3},{4,36},{36... | collective-permute-start | bytes 1769480 | tf_op jit(solution)/shard_map/ppermute | solution.py:25
  23.6 8.3 %collective-permute-start.2 = (bf16[288,1024]{1,0:T(8,128)(2,1)}, bf16[288,1024]{1,0:T(8,128)(2,1)S(1)}, u32[]{:S(2)}, u32[]{:S(2)}) collective-permute-start(bf16[288,1024]{1,0:T(8,128)(2,1)} %enc_own.1), channel_id=1, source_target_pairs={{0,32},{32,0},{1,33},{33,1},{2,34},{34,2},{3,35},{35,3},{4,36},{36... | collective-permute-start | bytes 1769480 | tf_op jit(solution)/shard_map/ppermute | solution.py:25
  25.5 3.4 %collective-permute-start.1 = (f32[288]{0:T(512)}, f32[288]{0:T(512)S(1)}, u32[]{:S(2)}, u32[]{:S(2)}) collective-permute-start(f32[288]{0:T(512)} %param.11), channel_id=1, source_target_pairs={{0,32},{32,0},{1,33},{33,1},{2,34},{34,2},{3,35},{35,3},{4,36},{36... | collective-permute-start | bytes 3464 | tf_op jit(solution)/shard_map/ppermute | solution.py:25
  31.6 0.9 copy-start.1
  31.9 20.6 %copy-start.5 = (f32[1024]{0:T(1024)S(1)}, f32[1024]{0:T(1024)}, u32[]{:S(2)}) copy-start(f32[1024]{0:T(1024)} %param.9) | copy-start | bytes 12292
  53.5 16.1 %all-to-all-start.2 = ((bf16[8,256,128]{2,1,0:T(8,128)(2,1)}), bf16[8,256,128]{2,1,0:T(8,128)(2,1)S(1)}, u32[]{:S(2)}, u32[]{:S(2)}) async-start(bf16[8,256,128]{2,1,0:T(8,128)(2,1)} %shard_map.88), calls=%async_computation.2 | async-start | bytes 1048576 | tf_op jit(solution)/shard_map/all_to_all | solution.py:21
  57.3 1.1 copy-start.2
  125.6 19.4 %all-to-all-start.6 = ((bf16[8,272,128]{2,1,0:T(8,128)(2,1)}), bf16[8,272,128]{2,1,0:T(8,128)(2,1)}, u32[]{:S(2)}, u32[]{:S(2)}) async-start(bf16[8,272,128]{2,1,0:T(8,128)(2,1)} %shard_map.93), calls=%async_computation.6 | async-start | bytes 1114112 | tf_op jit(solution)/shard_map/all_to_all | solution.py:21
  130.0 14.0 %collective-permute-start.7 = (bf16[256,1024]{1,0:T(8,128)(2,1)S(1)}, bf16[256,1024]{1,0:T(8,128)(2,1)S(1)}, u32[]{:S(2)}, u32[]{:S(2)}) collective-permute-start(bf16[256,1024]{1,0:T(8,128)(2,1)S(1)} %shard_map.96), channel_id=1, source_target_pairs={{0,32},{32,0},{1,33},{33,1},{2,34},{34,2},{3,35},{35,3},{4,36},{36... | collective-permute-start | bytes 1572872 | tf_op jit(solution)/shard_map/ppermute | solution.py:25
  139.1 14.7 %collective-permute-start.5 = (bf16[288,256]{1,0:T(8,128)(2,1)S(1)}, bf16[288,256]{1,0:T(8,128)(2,1)S(1)}, u32[]{:S(2)}, u32[]{:S(2)}) collective-permute-start(bf16[288,256]{1,0:T(8,128)(2,1)S(1)} %get-tuple-element.21), channel_id=1, source_target_pairs={{0,32},{32,0},{1,33},{33,1},{2,34},{34,2},{3,35},{35,3},{4,36},{36... | collective-permute-start | bytes 442376 | tf_op jit(solution)/shard_map/ppermute | solution.py:25
  141.2 3.5 %collective-permute-start.6 = (bf16[256,288]{1,0:T(8,128)(2,1)S(1)}, bf16[256,288]{1,0:T(8,128)(2,1)S(1)}, u32[]{:S(2)}, u32[]{:S(2)}) collective-permute-start(bf16[256,288]{1,0:T(8,128)(2,1)S(1)} %slice.13), channel_id=1, source_target_pairs={{0,32},{32,0},{1,33},{33,1},{2,34},{34,2},{3,35},{35,3},{4,36},{36... | collective-permute-start | bytes 442376 | tf_op jit(solution)/shard_map/ppermute | solution.py:25
  145.0 9.2 %collective-permute-start.4 = (bf16[8,272,128]{2,1,0:T(8,128)(2,1)}, bf16[8,272,128]{2,1,0:T(8,128)(2,1)S(1)}, u32[]{:S(2)}, u32[]{:S(2)}) collective-permute-start(bf16[8,272,128]{2,1,0:T(8,128)(2,1)} %all-to-all-done.6.own_ref), channel_id=1, source_target_pairs={{0,32},{32,0},{1,33},{33,1},{2,34},{34,2},{3,35},{35,3},{4,36},{36... | collective-permute-start | bytes 1671176 | tf_op jit(solution)/shard_map/ppermute | solution.py:25

commit v8 on v7

--- a/solution.py
+++ b/solution.py
@@ -12,6 +12,7 @@
 F32 = jnp.float32
 BF16 = jnp.bfloat16
 SHARPNESS = 8.0
+PICK = 56
 VMEM = pl.BlockSpec(memory_space=pltpu.VMEM)
 ANY = pl.BlockSpec(memory_space=pl.ANY)
 HBM = pl.BlockSpec(memory_space=pltpu.HBM)
@@ -73,11 +74,20 @@
     other_ref[...] = pick((1 - core) * piece, jnp.concatenate([zeros, columns], axis=0))
 
 
-def join_kernel(own_ref, got_ref, rows_ref, copies_ref):
-    rows = own_ref[...] + got_ref[...]
-    rows_ref[...] = rows
-    for i in range(copies_ref.shape[0]):
-        copies_ref[i] = rows
+def give(one_ref, copies_hbm, sems):
+    copies = [
+        pltpu.make_async_copy(one_ref, copies_hbm.at[i], sems.at[i])
+        for i in range(copies_hbm.shape[0])
+    ]
+    for copy in copies:
+        copy.start()
+    for copy in copies:
+        copy.wait()
+
+
+def join_kernel(own_ref, got_ref, rows_ref, copies_hbm, sems):
+    rows_ref[...] = own_ref[...] + got_ref[...]
+    give(rows_ref, copies_hbm, sems)
 
 
 def turn_kernel(value_ref, own_ref, other_ref):
@@ -134,15 +144,14 @@
     return value, small, (soft / SHARPNESS).astype(BF16)
 
 
-def act_kernel(blocks_ref, bias_ref, copies_ref):
-    size = copies_ref.shape[1]
+def act_kernel(blocks_ref, bias_ref, copies_hbm, one_ref, sems):
+    size = copies_hbm.shape[1]
     share = size // bias_ref.shape[0]
     total = sum_blocks(blocks_ref, size)
     for k in range(bias_ref.shape[0]):
         lines = slice(k * share, (k + 1) * share)
-        _, _, active = soft_parts(total[lines], bias_ref[k : k + 1, :])
-        for y in range(copies_ref.shape[0]):
-            copies_ref[y, lines, :] = active
+        _, _, one_ref[lines, :] = soft_parts(total[lines], bias_ref[k : k + 1, :])
+    give(one_ref, copies_hbm, sems)
 
 
 def norms_of(blocks_ref, count):
@@ -199,7 +208,7 @@
         spread(part.astype(BF16), out_ref, 2 * n)
 
 
-def grad_kernel(blocks_ref, pre_ref, bias_ref, copies_ref):
+def grad_kernel(blocks_ref, pre_ref, bias_ref, copies_hbm, one_ref, sems):
     size = blocks_ref.shape[1]
     count = bias_ref.shape[0]
     share = size // count
@@ -211,15 +220,12 @@
         lines = slice(k * share, (k + 1) * share)
         value, small, active = soft_parts(pre[lines], bias_ref[k : k + 1, :])
         gate = jnp.where(value >= 0.0, 1.0, small) / (1.0 + small)
-        grad = ((raw[lines] + 1.0 / ROWS) * gate).astype(BF16)
-        for y in range(copies_ref.shape[0]):
-            copies_ref[y, lines, :] = grad
+        one_ref[lines, :] = ((raw[lines] + 1.0 / ROWS) * gate).astype(BF16)
         part = jnp.sum(active.astype(F32) * raw[lines], axis=0, keepdims=True)
         dots = jnp.where(row == k, part, dots)
     high = dots.astype(BF16).astype(F32)
-    parts = jnp.concatenate([high, dots - high], axis=0).astype(BF16)
-    for y in range(copies_ref.shape[0]):
-        copies_ref[y, size:, :] = parts
+    one_ref[size:] = jnp.concatenate([high, dots - high], axis=0).astype(BF16)
+    give(one_ref, copies_hbm, sems)
 
 
 def own_kernel(own_ref, centered_ref, blocks_ref, enc_ref, sums_ref, grad_ref):
@@ -304,11 +310,17 @@
             pltpu.VMEM(residual.shape[::-1], BF16),
             pltpu.SemaphoreType.DMA((2,)),
         ],
+        limit=PICK,
     )(picked, residual.T)
     tensor_blocks = shape((count_t, piece, wide), BF16)
-    local_rows, copies = call(join_kernel, (small, tensor_blocks), [VMEM] * 2, (1 << 12, 1 << 19))(
-        own_rows, swap(other_rows)
-    )
+    local_rows, copies = call(
+        join_kernel,
+        (small, tensor_blocks),
+        [VMEM] * 2,
+        (1 << 12, 1 << 19),
+        [pltpu.SemaphoreType.DMA((count_t,))],
+        (VMEM, ANY),
+    )(own_rows, swap(other_rows))
     sampled = exchange(copies, TENSOR)
     bias_all = jnp.concatenate([dec_bias[None], swap(dec_bias)[None]], axis=1)
     enc_other = swap(enc_weight)
@@ -326,7 +338,12 @@
     blocks = exchange(pre_blocks, "y")
     enc_bias = enc_bias.reshape(blocks_n, LANES)
     copies = call(
-        act_kernel, shape((count_y, size, LANES), BF16), [VMEM] * 2, (1 << 20, 1 << 20)
+        act_kernel,
+        shape((count_y, size, LANES), BF16),
+        [VMEM] * 2,
+        (1 << 20, 1 << 20),
+        [pltpu.VMEM((size, LANES), BF16), pltpu.SemaphoreType.DMA((count_y,))],
+        ANY,
     )(blocks, enc_bias)
     unit = call(unit_kernel, shape((wide, latents), BF16), [VMEM] * 3, (1 << 20, moved))(
         blocks, dec_own, dec_other
@@ -364,6 +381,8 @@
             shape((count_y, size + extra, LANES), BF16),
             [VMEM] * 3,
             (1 << 20, 1 << 20),
+            [pltpu.VMEM((size + extra, LANES), BF16), pltpu.SemaphoreType.DMA((count_y,))],
+            ANY,
         )(exchange(raw_blocks, "y"), blocks, enc_bias),
         "y",
     )

time: 157 us -> 158 us (level)
  no operation moved by 1% of the time
where the time goes in v8:
time: 158 us; the launch traced here: 157 us
  blocking collectives  73.7 us (47%)
  starting transfers between devices  52 us (33%)
  waiting for transfers between devices  15.6 us (10%)
  Pallas kernels  11.3 us (7%)
  local copies, waits for them, and re-layouts  2.64 us (2%)
    all_to_all x4, blocking collectives, exchange(): return lax.all_to_all(blocks, axis, 0, 0, tiled=False)  73.7 us
    ppermute x8, starting transfers between devices, swap(): return lax.ppermute(block, 'core', [(0, 1), (1, 0)])  36.3 us
    all_to_all x3, starting transfers between devices, exchange(): return lax.all_to_all(blocks, axis, 0, 0, tiled=False)  15.7 us
    all_to_all x3, waiting for transfers between devices, exchange(): return lax.all_to_all(blocks, axis, 0, 0, tiled=False)  13.3 us
  transfers between devices with their start and end apart: 11, of which 6 were waited for; matrix products, arithmetic and copies ran while one was open for 1% of the time, Pallas kernels for 1%

profile of v8, /device:TPU:1, one launch (start us, length us, event | category | flops | bytes accessed | tf_op | source)
XLA Modules:
  0.0 157.3 jit_solution(8658655648358064192)
XLA Ops:
  0.6 1.8 %shard_map.85 = (bf16[8,576]{1,0:T(8,128)(2,1)}, bf16[8,576]{1,0:T(8,128)(2,1)}) custom-call(s32[16]{0:T(128)} %picked_hbm.1, bf16[288,128]{1,0:T(8,128)(2,1)} %bitcast.21), custom_call_target="tpu_custom_call" | custom-call | flops 1048576 | bytes 131072 | tf_op jit(solution)/shard_map/pallas_call | solution.py:303
  2.4 8.8 %collective-permute-start = (bf16[8,576]{1,0:T(8,128)(2,1)}, bf16[8,576]{1,0:T(8,128)(2,1)S(1)}, u32[]{:S(2)}, u32[]{:S(2)}) collective-permute-start(bf16[8,576]{1,0:T(8,128)(2,1)} %get-tuple-element.15), channel_id=1, source_target_pairs={{0,32},{32,0},{1,33},{33,1},{2,34},{34,2},{3,35},{35,3},{4,36},{36... | collective-permute-start | bytes 27656 | tf_op jit(solution)/shard_map/ppermute | solution.py:26
  11.2 1.0 collective-permute-done.got_ref
  12.2 0.7 copy-done.5
  12.9 1.0 shard_map.86
  13.9 7.7 %all-to-all-start = ((bf16[32,8,576]{2,1,0:T(8,128)(2,1)}), bf16[32,8,576]{2,1,0:T(8,128)(2,1)S(1)}, u32[]{:S(2)}, u32[]{:S(2)}) async-start(bf16[32,8,576]{2,1,0:T(8,128)(2,1)} %get-tuple-element.16), calls=%async_computation | async-start | bytes 655360 | tf_op jit(solution)/shard_map/all_to_all | solution.py:22
  21.6 2.5 %collective-permute-start.3 = (bf16[288,1024]{1,0:T(8,128)(2,1)}, bf16[288,1024]{1,0:T(8,128)(2,1)S(1)}, u32[]{:S(2)}, u32[]{:S(2)}) collective-permute-start(bf16[288,1024]{1,0:T(8,128)(2,1)} %bitcast.16), channel_id=1, source_target_pairs={{0,32},{32,0},{1,33},{33,1},{2,34},{34,2},{3,35},{35,3},{4,36},{36... | collective-permute-start | bytes 1769480 | tf_op jit(solution)/shard_map/ppermute | solution.py:26
  24.1 1.9 %collective-permute-start.2 = (bf16[288,1024]{1,0:T(8,128)(2,1)}, bf16[288,1024]{1,0:T(8,128)(2,1)S(1)}, u32[]{:S(2)}, u32[]{:S(2)}) collective-permute-start(bf16[288,1024]{1,0:T(8,128)(2,1)} %enc_own.1), channel_id=1, source_target_pairs={{0,32},{32,0},{1,33},{33,1},{2,34},{34,2},{3,35},{35,3},{4,36},{36... | collective-permute-start | bytes 1769480 | tf_op jit(solution)/shard_map/ppermute | solution.py:26
  26.1 2.4 %collective-permute-start.1 = (f32[288]{0:T(512)}, f32[288]{0:T(512)S(1)}, u32[]{:S(2)}, u32[]{:S(2)}) collective-permute-start(f32[288]{0:T(512)} %param.11), channel_id=1, source_target_pairs={{0,32},{32,0},{1,33},{33,1},{2,34},{34,2},{3,35},{35,3},{4,36},{36... | collective-permute-start | bytes 3464 | tf_op jit(solution)/shard_map/ppermute | solution.py:26
  28.5 0.7 broadcast_in_dim.6
  29.6 2.5 %all-to-all-done = bf16[32,8,576]{2,1,0:T(8,128)(2,1)S(1)} async-done(((bf16[32,8,576]{2,1,0:T(8,128)(2,1)}), bf16[32,8,576]{2,1,0:T(8,128)(2,1)S(1)}, u32[]{:S(2)}, u32[]{:S(2)}) %all-to-all-start) | async-done | bytes 294944 | tf_op jit(solution)/shard_map/all_to_all | solution.py:22
  32.5 0.6 shard_map.87
  33.1 20.0 %all_to_all.35.blocks_ref.pre_ref = bf16[8,272,128]{2,1,0:T(8,128)(2,1)S(1)} all-to-all(bf16[8,272,128]{2,1,0:T(8,128)(2,1)S(1)} %shard_map.87), channel_id=1, replica_groups=mesh['y'=8,'core'=2,'x'=4,'z'=8] {'y'}, dimensions={0} | all-to-all | bytes 1114112 | tf_op jit(solution)/shard_map/all_to_all | solution.py:22
  53.0 1.0 shard_map.88
  54.1 3.8 %all-to-all-start.2 = ((bf16[8,256,128]{2,1,0:T(8,128)(2,1)}), bf16[8,256,128]{2,1,0:T(8,128)(2,1)S(1)}, u32[]{:S(2)}, u32[]{:S(2)}) async-start(bf16[8,256,128]{2,1,0:T(8,128)(2,1)} %shard_map.88), calls=%async_computation.2 | async-start | bytes 1048576 | tf_op jit(solution)/shard_map/all_to_all | solution.py:22
  57.9 1.1 copy-done.2
  58.9 0.4 shard_map.89.unit_ref
  59.4 10.8 %all-to-all-done.2.copies_ref = bf16[8,256,128]{2,1,0:T(8,128)(2,1)S(1)} async-done(((bf16[8,256,128]{2,1,0:T(8,128)(2,1)}), bf16[8,256,128]{2,1,0:T(8,128)(2,1)S(1)}, u32[]{:S(2)}, u32[]{:S(2)}) %all-to-all-start.2) | async-done | bytes 524320 | tf_op jit(solution)/shard_map/all_to_all | solution.py:22
  70.1 0.6 shard_map.90
  70.8 23.5 %all_to_all.36.blocks_ref = bf16[32,8,576]{2,1,0:T(8,128)(2,1)S(1)} all-to-all(bf16[32,8,576]{2,1,0:T(8,128)(2,1)S(1)} %shard_map.90), channel_id=1, replica_groups=mesh['y'=8,'core'=2,'x'=4,'z'=8] {'x','z'}, dimensions={0} | all-to-all | bytes 589824 | tf_op jit(solution)/shard_map/all_to_all | solution.py:22
  94.4 14.7 %all_to_all.37.error_ref = bf16[32,8,576]{2,1,0:T(8,128)(2,1)S(1)} all-to-all(bf16[32,8,576]{2,1,0:T(8,128)(2,1)S(1)} %shard_map.91), channel_id=1, replica_groups=mesh['y'=8,'core'=2,'x'=4,'z'=8] {'x','z'}, dimensions={0} | all-to-all | bytes 589824 | tf_op jit(solution)/shard_map/all_to_all | solution.py:22
  109.1 0.6 shard_map.92
  109.7 15.5 %all_to_all.38.blocks_ref = bf16[8,256,128]{2,1,0:T(8,128)(2,1)S(1)} all-to-all(bf16[8,256,128]{2,1,0:T(8,128)(2,1)S(1)} %shard_map.92), channel_id=1, replica_groups=mesh['y'=8,'core'=2,'x'=4,'z'=8] {'y'}, dimensions={0} | all-to-all | bytes 1048576 | tf_op jit(solution)/shard_map/all_to_all | solution.py:22
  125.2 1.1 shard_map.93
  126.3 4.2 %all-to-all-start.6 = ((bf16[8,272,128]{2,1,0:T(8,128)(2,1)}), bf16[8,272,128]{2,1,0:T(8,128)(2,1)}, u32[]{:S(2)}, u32[]{:S(2)}) async-start(bf16[8,272,128]{2,1,0:T(8,128)(2,1)} %shard_map.93), calls=%async_computation.6 | async-start | bytes 1114112 | tf_op jit(solution)/shard_map/all_to_all | solution.py:22
  130.7 8.9 %collective-permute-start.7 = (bf16[256,1024]{1,0:T(8,128)(2,1)S(1)}, bf16[256,1024]{1,0:T(8,128)(2,1)S(1)}, u32[]{:S(2)}, u32[]{:S(2)}) collective-permute-start(bf16[256,1024]{1,0:T(8,128)(2,1)S(1)} %shard_map.96), channel_id=1, source_target_pairs={{0,32},{32,0},{1,33},{33,1},{2,34},{34,2},{3,35},{35,3},{4,36},{36... | collective-permute-start | bytes 1572872 | tf_op jit(solution)/shard_map/ppermute | solution.py:26
  139.8 1.9 %collective-permute-start.5 = (bf16[288,256]{1,0:T(8,128)(2,1)S(1)}, bf16[288,256]{1,0:T(8,128)(2,1)S(1)}, u32[]{:S(2)}, u32[]{:S(2)}) collective-permute-start(bf16[288,256]{1,0:T(8,128)(2,1)S(1)} %get-tuple-element.21), channel_id=1, source_target_pairs={{0,32},{32,0},{1,33},{33,1},{2,34},{34,2},{3,35},{35,3},{4,36},{36... | collective-permute-start | bytes 442376 | tf_op jit(solution)/shard_map/ppermute | solution.py:26
  141.9 2.4 %collective-permute-start.6 = (bf16[256,288]{1,0:T(8,128)(2,1)S(1)}, bf16[256,288]{1,0:T(8,128)(2,1)S(1)}, u32[]{:S(2)}, u32[]{:S(2)}) collective-permute-start(bf16[256,288]{1,0:T(8,128)(2,1)S(1)} %slice.13), channel_id=1, source_target_pairs={{0,32},{32,0},{1,33},{33,1},{2,34},{34,2},{3,35},{35,3},{4,36},{36... | collective-permute-start | bytes 442376 | tf_op jit(solution)/shard_map/ppermute | solution.py:26
  144.6 0.7 collective-permute-done.6
  145.7 7.4 %collective-permute-start.4 = (bf16[8,272,128]{2,1,0:T(8,128)(2,1)}, bf16[8,272,128]{2,1,0:T(8,128)(2,1)S(1)}, u32[]{:S(2)}, u32[]{:S(2)}) collective-permute-start(bf16[8,272,128]{2,1,0:T(8,128)(2,1)} %all-to-all-done.6.own_ref), channel_id=1, source_target_pairs={{0,32},{32,0},{1,33},{33,1},{2,34},{34,2},{3,35},{35,3},{4,36},{36... | collective-permute-start | bytes 1671176 | tf_op jit(solution)/shard_map/ppermute | solution.py:26
  153.1 1.4 shard_map.95
  154.9 2.4 %shard_map.97 = (f32[288,1024]{1,0:T(8,128)}, f32[8,128]{1,0:T(8,128)}, f32[288,1024]{1,0:T(8,128)}) custom-call(bf16[8,272,128]{2,1,0:T(8,128)(2,1)S(1)} %collective-permute-done.4.its_ref, f32[288,1024]{1,0:T(8,128)S(1)} %get-tuple-element.19.part_ref, f32[24,128]{1,0:T(8,128)S(1)} %get-tuple-element.20.sums_ref, ...), custom_call_target="tpu_custom_call" | custom-call | flops 301989888 | bytes 6291456 | tf_op jit(solution)/shard_map/pallas_call | solution.py:398
  (28 shorter events, 2.3 us)
Async XLA Ops:
  0.6 31.5 %copy-start = (bf16[1024,288]{0,1:T(8,128)(2,1)S(1)}, bf16[1024,288]{0,1:T(8,128)(2,1)}, u32[]{:S(2)}) copy-start(bf16[1024,288]{0,1:T(8,128)(2,1)} %param.10) | copy-start | bytes 1769476
  2.4 9.8 %collective-permute-start = (bf16[8,576]{1,0:T(8,128)(2,1)}, bf16[8,576]{1,0:T(8,128)(2,1)S(1)}, u32[]{:S(2)}, u32[]{:S(2)}) collective-permute-start(bf16[8,576]{1,0:T(8,128)(2,1)} %get-tuple-element.15), channel_id=1, source_target_pairs={{0,32},{32,0},{1,33},{33,1},{2,34},{34,2},{3,35},{35,3},{4,36},{36... | collective-permute-start | bytes 27656 | tf_op jit(solution)/shard_map/ppermute | solution.py:26
  12.2 0.7 copy-start.5
  13.9 18.5 %copy-start.3 = (bf16[288,1024]{1,0:T(8,128)(2,1)S(1)}, bf16[288,1024]{1,0:T(8,128)(2,1)}, u32[]{:S(2)}) copy-start(bf16[288,1024]{1,0:T(8,128)(2,1)} %enc_own.1) | copy-start | bytes 1769476
  13.9 18.2 %all-to-all-start = ((bf16[32,8,576]{2,1,0:T(8,128)(2,1)}), bf16[32,8,576]{2,1,0:T(8,128)(2,1)S(1)}, u32[]{:S(2)}, u32[]{:S(2)}) async-start(bf16[32,8,576]{2,1,0:T(8,128)(2,1)} %get-tuple-element.16), calls=%async_computation | async-start | bytes 655360 | tf_op jit(solution)/shard_map/all_to_all | solution.py:22
  21.6 10.6 %collective-permute-start.3 = (bf16[288,1024]{1,0:T(8,128)(2,1)}, bf16[288,1024]{1,0:T(8,128)(2,1)S(1)}, u32[]{:S(2)}, u32[]{:S(2)}) collective-permute-start(bf16[288,1024]{1,0:T(8,128)(2,1)} %bitcast.16), channel_id=1, source_target_pairs={{0,32},{32,0},{1,33},{33,1},{2,34},{34,2},{3,35},{35,3},{4,36},{36... | collective-permute-start | bytes 1769480 | tf_op jit(solution)/shard_map/ppermute | solution.py:26
  24.1 8.3 %collective-permute-start.2 = (bf16[288,1024]{1,0:T(8,128)(2,1)}, bf16[288,1024]{1,0:T(8,128)(2,1)S(1)}, u32[]{:S(2)}, u32[]{:S(2)}) collective-permute-start(bf16[288,1024]{1,0:T(8,128)(2,1)} %enc_own.1), channel_id=1, source_target_pairs={{0,32},{32,0},{1,33},{33,1},{2,34},{34,2},{3,35},{35,3},{4,36},{36... | collective-permute-start | bytes 1769480 | tf_op jit(solution)/shard_map/ppermute | solution.py:26
  26.1 3.4 %collective-permute-start.1 = (f32[288]{0:T(512)}, f32[288]{0:T(512)S(1)}, u32[]{:S(2)}, u32[]{:S(2)}) collective-permute-start(f32[288]{0:T(512)} %param.11), channel_id=1, source_target_pairs={{0,32},{32,0},{1,33},{33,1},{2,34},{34,2},{3,35},{35,3},{4,36},{36... | collective-permute-start | bytes 3464 | tf_op jit(solution)/shard_map/ppermute | solution.py:26
  32.2 0.9 copy-start.1
  32.5 20.6 %copy-start.4 = (f32[1024]{0:T(1024)S(1)}, f32[1024]{0:T(1024)}, u32[]{:S(2)}) copy-start(f32[1024]{0:T(1024)} %param.9) | copy-start | bytes 12292
  54.1 16.1 %all-to-all-start.2 = ((bf16[8,256,128]{2,1,0:T(8,128)(2,1)}), bf16[8,256,128]{2,1,0:T(8,128)(2,1)S(1)}, u32[]{:S(2)}, u32[]{:S(2)}) async-start(bf16[8,256,128]{2,1,0:T(8,128)(2,1)} %shard_map.88), calls=%async_computation.2 | async-start | bytes 1048576 | tf_op jit(solution)/shard_map/all_to_all | solution.py:22
  57.9 1.1 copy-start.2
  126.3 19.4 %all-to-all-start.6 = ((bf16[8,272,128]{2,1,0:T(8,128)(2,1)}), bf16[8,272,128]{2,1,0:T(8,128)(2,1)}, u32[]{:S(2)}, u32[]{:S(2)}) async-start(bf16[8,272,128]{2,1,0:T(8,128)(2,1)} %shard_map.93), calls=%async_computation.6 | async-start | bytes 1114112 | tf_op jit(solution)/shard_map/all_to_all | solution.py:22
  130.7 14.0 %collective-permute-start.7 = (bf16[256,1024]{1,0:T(8,128)(2,1)S(1)}, bf16[256,1024]{1,0:T(8,128)(2,1)S(1)}, u32[]{:S(2)}, u32[]{:S(2)}) collective-permute-start(bf16[256,1024]{1,0:T(8,128)(2,1)S(1)} %shard_map.96), channel_id=1, source_target_pairs={{0,32},{32,0},{1,33},{33,1},{2,34},{34,2},{3,35},{35,3},{4,36},{36... | collective-permute-start | bytes 1572872 | tf_op jit(solution)/shard_map/ppermute | solution.py:26
  139.8 14.7 %collective-permute-start.5 = (bf16[288,256]{1,0:T(8,128)(2,1)S(1)}, bf16[288,256]{1,0:T(8,128)(2,1)S(1)}, u32[]{:S(2)}, u32[]{:S(2)}) collective-permute-start(bf16[288,256]{1,0:T(8,128)(2,1)S(1)} %get-tuple-element.21), channel_id=1, source_target_pairs={{0,32},{32,0},{1,33},{33,1},{2,34},{34,2},{3,35},{35,3},{4,36},{36... | collective-permute-start | bytes 442376 | tf_op jit(solution)/shard_map/ppermute | solution.py:26
  141.9 3.5 %collective-permute-start.6 = (bf16[256,288]{1,0:T(8,128)(2,1)S(1)}, bf16[256,288]{1,0:T(8,128)(2,1)S(1)}, u32[]{:S(2)}, u32[]{:S(2)}) collective-permute-start(bf16[256,288]{1,0:T(8,128)(2,1)S(1)} %slice.13), channel_id=1, source_target_pairs={{0,32},{32,0},{1,33},{33,1},{2,34},{34,2},{3,35},{35,3},{4,36},{36... | collective-permute-start | bytes 442376 | tf_op jit(solution)/shard_map/ppermute | solution.py:26
  145.7 9.2 %collective-permute-start.4 = (bf16[8,272,128]{2,1,0:T(8,128)(2,1)}, bf16[8,272,128]{2,1,0:T(8,128)(2,1)S(1)}, u32[]{:S(2)}, u32[]{:S(2)}) collective-permute-start(bf16[8,272,128]{2,1,0:T(8,128)(2,1)} %all-to-all-done.6.own_ref), channel_id=1, source_target_pairs={{0,32},{32,0},{1,33},{33,1},{2,34},{34,2},{3,35},{35,3},{4,36},{36... | collective-permute-start | bytes 1671176 | tf_op jit(solution)/shard_map/ppermute | solution.py:26

commit v9 on v7

--- a/solution.py
+++ b/solution.py
@@ -18,7 +18,14 @@
 
 
 def exchange(blocks, axis):
-    return lax.all_to_all(blocks, axis, 0, 0, tiled=False)
+    if axis == TENSOR:
+        return lax.all_to_all(blocks, axis, 0, 0, tiled=False)
+    count = lax.axis_size(axis)
+    even = [2 * i for i in range(count)]
+    odd = [2 * i + 1 for i in reversed(range(count))]
+    return lax.all_to_all(
+        blocks, (axis, "core"), 0, 0, tiled=False, axis_index_groups=[even, odd]
+    )
 
 
 def swap(block):

time: 157 us -> 158 us (level)
  starting transfers between devices: 51.9 us -> 57.7 us
  waiting for transfers between devices: 15.4 us -> 10.7 us
    all_to_all x4 -> x2, blocking collectives: 73.7 us -> 38.2 us  [exchange(): return lax.all_to_all(blocks, axis, 0, 0, tiled=False)]
    all_to_all x0 -> x2, blocking collectives: none -> 34.8 us  [exchange(): lax.all_to_all(blocks, (axis, 'core'), 0, 0, tiled=False, axis_index_grou...]
    all_to_all x0 -> x2, starting transfers between devices: none -> 14.9 us  [exchange(): lax.all_to_all(blocks, (axis, 'core'), 0, 0, tiled=False, axis_index_grou...]
    all_to_all x3 -> x1, waiting for transfers between devices: 13.3 us -> 2.5 us  [exchange(): return lax.all_to_all(blocks, axis, 0, 0, tiled=False)]
    all_to_all x3 -> x1, starting transfers between devices: 15.6 us -> 7.64 us  [exchange(): return lax.all_to_all(blocks, axis, 0, 0, tiled=False)]
    all_to_all x0 -> x2, waiting for transfers between devices: none -> 6.04 us  [exchange(): lax.all_to_all(blocks, (axis, 'core'), 0, 0, tiled=False, axis_index_grou...]
where the time goes in v9:
time: 158 us; the launch traced here: 157 us
  blocking collectives  73 us (46%)
  starting transfers between devices  57.7 us (37%)
  waiting for transfers between devices  10.7 us (7%)
  Pallas kernels  9.98 us (6%)
  local copies, waits for them, and re-layouts  3.53 us (2%)
    all_to_all x2, blocking collectives, exchange(): return lax.all_to_all(blocks, axis, 0, 0, tiled=False)  38.2 us
    ppermute x8, starting transfers between devices, swap(): return lax.ppermute(block, 'core', [(0, 1), (1, 0)])  35.1 us
    all_to_all x2, blocking collectives, exchange(): lax.all_to_all(blocks, (axis, 'core'), 0, 0, tiled=False, axis_index_grou...  34.8 us
    all_to_all x2, starting transfers between devices, exchange(): lax.all_to_all(blocks, (axis, 'core'), 0, 0, tiled=False, axis_index_grou...  14.9 us
    all_to_all x1, starting transfers between devices, exchange(): return lax.all_to_all(blocks, axis, 0, 0, tiled=False)  7.64 us
    all_to_all x2, waiting for transfers between devices, exchange(): lax.all_to_all(blocks, (axis, 'core'), 0, 0, tiled=False, axis_index_grou...  6.04 us
  transfers between devices with their start and end apart: 11, of which 6 were waited for; matrix products, arithmetic and copies ran while one was open for 1% of the time, Pallas kernels for 1%

profile of v9, /device:TPU:1, one launch (start us, length us, event | category | flops | bytes accessed | tf_op | source)
XLA Modules:
  0.0 156.8 jit_solution(5809382419817272923)
XLA Ops:
  0.7 0.9 copy-done.4
  1.6 0.7 copy-done.6
  2.2 0.8 shard_map.85
  3.0 8.8 %collective-permute-start = (bf16[8,576]{1,0:T(8,128)(2,1)S(1)}, bf16[8,576]{1,0:T(8,128)(2,1)S(1)}, u32[]{:S(2)}, u32[]{:S(2)}) collective-permute-start(bf16[8,576]{1,0:T(8,128)(2,1)S(1)} %get-tuple-element.15), channel_id=1, source_target_pairs={{0,32},{32,0},{1,33},{33,1},{2,34},{34,2},{3,35},{35,3},{4,36},{36... | collective-permute-start | bytes 27656 | tf_op jit(solution)/shard_map/ppermute | solution.py:32
  11.8 0.8 collective-permute-done.got_ref
  12.7 0.8 shard_map.86
  13.4 7.6 %all-to-all-start = ((bf16[32,8,576]{2,1,0:T(8,128)(2,1)}), bf16[32,8,576]{2,1,0:T(8,128)(2,1)S(1)}, u32[]{:S(2)}, u32[]{:S(2)}) async-start(bf16[32,8,576]{2,1,0:T(8,128)(2,1)} %get-tuple-element.16), calls=%async_computation | async-start | bytes 655360 | tf_op jit(solution)/shard_map/all_to_all | solution.py:22
  21.1 2.5 %collective-permute-start.3 = (bf16[288,1024]{1,0:T(8,128)(2,1)}, bf16[288,1024]{1,0:T(8,128)(2,1)S(1)}, u32[]{:S(2)}, u32[]{:S(2)}) collective-permute-start(bf16[288,1024]{1,0:T(8,128)(2,1)} %bitcast.16), channel_id=1, source_target_pairs={{0,32},{32,0},{1,33},{33,1},{2,34},{34,2},{3,35},{35,3},{4,36},{36... | collective-permute-start | bytes 1769480 | tf_op jit(solution)/shard_map/ppermute | solution.py:32
  23.6 1.9 %collective-permute-start.2 = (bf16[288,1024]{1,0:T(8,128)(2,1)}, bf16[288,1024]{1,0:T(8,128)(2,1)S(1)}, u32[]{:S(2)}, u32[]{:S(2)}) collective-permute-start(bf16[288,1024]{1,0:T(8,128)(2,1)} %enc_own.1), channel_id=1, source_target_pairs={{0,32},{32,0},{1,33},{33,1},{2,34},{34,2},{3,35},{35,3},{4,36},{36... | collective-permute-start | bytes 1769480 | tf_op jit(solution)/shard_map/ppermute | solution.py:32
  25.5 2.4 %collective-permute-start.1 = (f32[288]{0:T(512)}, f32[288]{0:T(512)S(1)}, u32[]{:S(2)}, u32[]{:S(2)}) collective-permute-start(f32[288]{0:T(512)} %param.11), channel_id=1, source_target_pairs={{0,32},{32,0},{1,33},{33,1},{2,34},{34,2},{3,35},{35,3},{4,36},{36... | collective-permute-start | bytes 3464 | tf_op jit(solution)/shard_map/ppermute | solution.py:32
  27.9 0.7 broadcast_in_dim.6
  29.1 2.5 %all-to-all-done = bf16[32,8,576]{2,1,0:T(8,128)(2,1)S(1)} async-done(((bf16[32,8,576]{2,1,0:T(8,128)(2,1)}), bf16[32,8,576]{2,1,0:T(8,128)(2,1)S(1)}, u32[]{:S(2)}, u32[]{:S(2)}) %all-to-all-start) | async-done | bytes 294944 | tf_op jit(solution)/shard_map/all_to_all | solution.py:22
  31.9 0.6 shard_map.87
  32.5 17.4 %all_to_all.35.blocks_ref.pre_ref = bf16[8,272,128]{2,1,0:T(8,128)(2,1)S(1)} all-to-all(bf16[8,272,128]{2,1,0:T(8,128)(2,1)S(1)} %shard_map.87), channel_id=1, replica_groups={{0,64,128,192,256,320,384,448},{480,416,352,288,224,160,96,32},{1,65,12..., dimensions={0} | all-to-all | bytes 1114112 | tf_op jit(solution)/shard_map/all_to_all | solution.py:26
  49.9 1.0 shard_map.88
  50.9 6.0 %all-to-all-start.2 = ((bf16[8,256,128]{2,1,0:T(8,128)(2,1)}), bf16[8,256,128]{2,1,0:T(8,128)(2,1)S(1)}, u32[]{:S(2)}, u32[]{:S(2)}) async-start(bf16[8,256,128]{2,1,0:T(8,128)(2,1)} %shard_map.88), calls=%async_computation.2 | async-start | bytes 1048576 | tf_op jit(solution)/shard_map/all_to_all | solution.py:26
  56.9 1.1 copy-done.2
  58.4 6.0 %all-to-all-done.2.copies_ref = bf16[8,256,128]{2,1,0:T(8,128)(2,1)S(1)} async-done(((bf16[8,256,128]{2,1,0:T(8,128)(2,1)}), bf16[8,256,128]{2,1,0:T(8,128)(2,1)S(1)}, u32[]{:S(2)}, u32[]{:S(2)}) %all-to-all-start.2) | async-done | bytes 524320 | tf_op jit(solution)/shard_map/all_to_all | solution.py:26
  64.5 0.6 shard_map.90
  65.1 23.6 %all_to_all.36.blocks_ref = bf16[32,8,576]{2,1,0:T(8,128)(2,1)S(1)} all-to-all(bf16[32,8,576]{2,1,0:T(8,128)(2,1)S(1)} %shard_map.90), channel_id=1, replica_groups=mesh['y'=8,'core'=2,'x'=4,'z'=8] {'x','z'}, dimensions={0} | all-to-all | bytes 589824 | tf_op jit(solution)/shard_map/all_to_all | solution.py:22
  88.8 14.6 %all_to_all.37.error_ref = bf16[32,8,576]{2,1,0:T(8,128)(2,1)S(1)} all-to-all(bf16[32,8,576]{2,1,0:T(8,128)(2,1)S(1)} %shard_map.91), channel_id=1, replica_groups=mesh['y'=8,'core'=2,'x'=4,'z'=8] {'x','z'}, dimensions={0} | all-to-all | bytes 589824 | tf_op jit(solution)/shard_map/all_to_all | solution.py:22
  103.4 0.6 shard_map.92
  104.0 17.3 %all_to_all.38.blocks_ref = bf16[8,256,128]{2,1,0:T(8,128)(2,1)S(1)} all-to-all(bf16[8,256,128]{2,1,0:T(8,128)(2,1)S(1)} %shard_map.92), channel_id=1, replica_groups={{0,64,128,192,256,320,384,448},{480,416,352,288,224,160,96,32},{1,65,12..., dimensions={0} | all-to-all | bytes 1048576 | tf_op jit(solution)/shard_map/all_to_all | solution.py:26
  121.3 1.1 shard_map.93
  122.4 8.9 %all-to-all-start.6 = ((bf16[8,272,128]{2,1,0:T(8,128)(2,1)}), bf16[8,272,128]{2,1,0:T(8,128)(2,1)}, u32[]{:S(2)}, u32[]{:S(2)}) async-start(bf16[8,272,128]{2,1,0:T(8,128)(2,1)} %shard_map.93), calls=%async_computation.6 | async-start | bytes 1114112 | tf_op jit(solution)/shard_map/all_to_all | solution.py:26
  131.4 7.3 %collective-permute-start.7 = (bf16[256,1024]{1,0:T(8,128)(2,1)S(1)}, bf16[256,1024]{1,0:T(8,128)(2,1)S(1)}, u32[]{:S(2)}, u32[]{:S(2)}) collective-permute-start(bf16[256,1024]{1,0:T(8,128)(2,1)S(1)} %shard_map.96), channel_id=1, source_target_pairs={{0,32},{32,0},{1,33},{33,1},{2,34},{34,2},{3,35},{35,3},{4,36},{36... | collective-permute-start | bytes 1572872 | tf_op jit(solution)/shard_map/ppermute | solution.py:32
  138.9 1.9 %collective-permute-start.5 = (bf16[288,256]{1,0:T(8,128)(2,1)S(1)}, bf16[288,256]{1,0:T(8,128)(2,1)S(1)}, u32[]{:S(2)}, u32[]{:S(2)}) collective-permute-start(bf16[288,256]{1,0:T(8,128)(2,1)S(1)} %get-tuple-element.21), channel_id=1, source_target_pairs={{0,32},{32,0},{1,33},{33,1},{2,34},{34,2},{3,35},{35,3},{4,36},{36... | collective-permute-start | bytes 442376 | tf_op jit(solution)/shard_map/ppermute | solution.py:32
  141.0 2.4 %collective-permute-start.6 = (bf16[256,288]{1,0:T(8,128)(2,1)S(1)}, bf16[256,288]{1,0:T(8,128)(2,1)S(1)}, u32[]{:S(2)}, u32[]{:S(2)}) collective-permute-start(bf16[256,288]{1,0:T(8,128)(2,1)S(1)} %slice.13), channel_id=1, source_target_pairs={{0,32},{32,0},{1,33},{33,1},{2,34},{34,2},{3,35},{35,3},{4,36},{36... | collective-permute-start | bytes 442376 | tf_op jit(solution)/shard_map/ppermute | solution.py:32
  143.8 0.7 collective-permute-done.6
  144.8 7.8 %collective-permute-start.4 = (bf16[8,272,128]{2,1,0:T(8,128)(2,1)}, bf16[8,272,128]{2,1,0:T(8,128)(2,1)S(1)}, u32[]{:S(2)}, u32[]{:S(2)}) collective-permute-start(bf16[8,272,128]{2,1,0:T(8,128)(2,1)} %all-to-all-done.6.own_ref), channel_id=1, source_target_pairs={{0,32},{32,0},{1,33},{33,1},{2,34},{34,2},{3,35},{35,3},{4,36},{36... | collective-permute-start | bytes 1671176 | tf_op jit(solution)/shard_map/ppermute | solution.py:32
  152.7 1.4 shard_map.95
  154.4 2.4 %shard_map.97 = (f32[288,1024]{1,0:T(8,128)}, f32[8,128]{1,0:T(8,128)}, f32[288,1024]{1,0:T(8,128)}) custom-call(bf16[8,272,128]{2,1,0:T(8,128)(2,1)S(1)} %collective-permute-done.4.its_ref, f32[288,1024]{1,0:T(8,128)S(1)} %get-tuple-element.19.part_ref, f32[24,128]{1,0:T(8,128)S(1)} %get-tuple-element.20.sums_ref, ...), custom_call_target="tpu_custom_call" | custom-call | flops 301989888 | bytes 6291456 | tf_op jit(solution)/shard_map/pallas_call | solution.py:386
  (30 shorter events, 2.7 us)
Async XLA Ops:
  0.6 31.0 %copy-start = (bf16[1024,288]{0,1:T(8,128)(2,1)S(1)}, bf16[1024,288]{0,1:T(8,128)(2,1)}, u32[]{:S(2)}) copy-start(bf16[1024,288]{0,1:T(8,128)(2,1)} %param.10) | copy-start | bytes 1769476
  0.6 0.9 copy-start.4
  1.6 0.7 copy-start.6
  3.0 9.6 %collective-permute-start = (bf16[8,576]{1,0:T(8,128)(2,1)S(1)}, bf16[8,576]{1,0:T(8,128)(2,1)S(1)}, u32[]{:S(2)}, u32[]{:S(2)}) collective-permute-start(bf16[8,576]{1,0:T(8,128)(2,1)S(1)} %get-tuple-element.15), channel_id=1, source_target_pairs={{0,32},{32,0},{1,33},{33,1},{2,34},{34,2},{3,35},{35,3},{4,36},{36... | collective-permute-start | bytes 27656 | tf_op jit(solution)/shard_map/ppermute | solution.py:32
  13.4 18.5 %copy-start.3 = (bf16[288,1024]{1,0:T(8,128)(2,1)S(1)}, bf16[288,1024]{1,0:T(8,128)(2,1)}, u32[]{:S(2)}) copy-start(bf16[288,1024]{1,0:T(8,128)(2,1)} %enc_own.1) | copy-start | bytes 1769476
  13.4 18.1 %all-to-all-start = ((bf16[32,8,576]{2,1,0:T(8,128)(2,1)}), bf16[32,8,576]{2,1,0:T(8,128)(2,1)S(1)}, u32[]{:S(2)}, u32[]{:S(2)}) async-start(bf16[32,8,576]{2,1,0:T(8,128)(2,1)} %get-tuple-element.16), calls=%async_computation | async-start | bytes 655360 | tf_op jit(solution)/shard_map/all_to_all | solution.py:22
  21.1 10.6 %collective-permute-start.3 = (bf16[288,1024]{1,0:T(8,128)(2,1)}, bf16[288,1024]{1,0:T(8,128)(2,1)S(1)}, u32[]{:S(2)}, u32[]{:S(2)}) collective-permute-start(bf16[288,1024]{1,0:T(8,128)(2,1)} %bitcast.16), channel_id=1, source_target_pairs={{0,32},{32,0},{1,33},{33,1},{2,34},{34,2},{3,35},{35,3},{4,36},{36... | collective-permute-start | bytes 1769480 | tf_op jit(solution)/shard_map/ppermute | solution.py:32
  23.6 8.3 %collective-permute-start.2 = (bf16[288,1024]{1,0:T(8,128)(2,1)}, bf16[288,1024]{1,0:T(8,128)(2,1)S(1)}, u32[]{:S(2)}, u32[]{:S(2)}) collective-permute-start(bf16[288,1024]{1,0:T(8,128)(2,1)} %enc_own.1), channel_id=1, source_target_pairs={{0,32},{32,0},{1,33},{33,1},{2,34},{34,2},{3,35},{35,3},{4,36},{36... | collective-permute-start | bytes 1769480 | tf_op jit(solution)/shard_map/ppermute | solution.py:32
  25.5 3.4 %collective-permute-start.1 = (f32[288]{0:T(512)}, f32[288]{0:T(512)S(1)}, u32[]{:S(2)}, u32[]{:S(2)}) collective-permute-start(f32[288]{0:T(512)} %param.11), channel_id=1, source_target_pairs={{0,32},{32,0},{1,33},{33,1},{2,34},{34,2},{3,35},{35,3},{4,36},{36... | collective-permute-start | bytes 3464 | tf_op jit(solution)/shard_map/ppermute | solution.py:32
  31.6 0.9 copy-start.1
  31.9 18.0 %copy-start.5 = (f32[1024]{0:T(1024)S(1)}, f32[1024]{0:T(1024)}, u32[]{:S(2)}) copy-start(f32[1024]{0:T(1024)} %param.9) | copy-start | bytes 12292
  50.9 13.6 %all-to-all-start.2 = ((bf16[8,256,128]{2,1,0:T(8,128)(2,1)}), bf16[8,256,128]{2,1,0:T(8,128)(2,1)S(1)}, u32[]{:S(2)}, u32[]{:S(2)}) async-start(bf16[8,256,128]{2,1,0:T(8,128)(2,1)} %shard_map.88), calls=%async_computation.2 | async-start | bytes 1048576 | tf_op jit(solution)/shard_map/all_to_all | solution.py:26
  56.9 1.1 copy-start.2
  122.4 22.4 %all-to-all-start.6 = ((bf16[8,272,128]{2,1,0:T(8,128)(2,1)}), bf16[8,272,128]{2,1,0:T(8,128)(2,1)}, u32[]{:S(2)}, u32[]{:S(2)}) async-start(bf16[8,272,128]{2,1,0:T(8,128)(2,1)} %shard_map.93), calls=%async_computation.6 | async-start | bytes 1114112 | tf_op jit(solution)/shard_map/all_to_all | solution.py:26
  131.4 12.3 %collective-permute-start.7 = (bf16[256,1024]{1,0:T(8,128)(2,1)S(1)}, bf16[256,1024]{1,0:T(8,128)(2,1)S(1)}, u32[]{:S(2)}, u32[]{:S(2)}) collective-permute-start(bf16[256,1024]{1,0:T(8,128)(2,1)S(1)} %shard_map.96), channel_id=1, source_target_pairs={{0,32},{32,0},{1,33},{33,1},{2,34},{34,2},{3,35},{35,3},{4,36},{36... | collective-permute-start | bytes 1572872 | tf_op jit(solution)/shard_map/ppermute | solution.py:32
  138.9 15.2 %collective-permute-start.5 = (bf16[288,256]{1,0:T(8,128)(2,1)S(1)}, bf16[288,256]{1,0:T(8,128)(2,1)S(1)}, u32[]{:S(2)}, u32[]{:S(2)}) collective-permute-start(bf16[288,256]{1,0:T(8,128)(2,1)S(1)} %get-tuple-element.21), channel_id=1, source_target_pairs={{0,32},{32,0},{1,33},{33,1},{2,34},{34,2},{3,35},{35,3},{4,36},{36... | collective-permute-start | bytes 442376 | tf_op jit(solution)/shard_map/ppermute | solution.py:32
  141.0 3.5 %collective-permute-start.6 = (bf16[256,288]{1,0:T(8,128)(2,1)S(1)}, bf16[256,288]{1,0:T(8,128)(2,1)S(1)}, u32[]{:S(2)}, u32[]{:S(2)}) collective-permute-start(bf16[256,288]{1,0:T(8,128)(2,1)S(1)} %slice.13), channel_id=1, source_target_pairs={{0,32},{32,0},{1,33},{33,1},{2,34},{34,2},{3,35},{35,3},{4,36},{36... | collective-permute-start | bytes 442376 | tf_op jit(solution)/shard_map/ppermute | solution.py:32
  144.8 9.6 %collective-permute-start.4 = (bf16[8,272,128]{2,1,0:T(8,128)(2,1)}, bf16[8,272,128]{2,1,0:T(8,128)(2,1)S(1)}, u32[]{:S(2)}, u32[]{:S(2)}) collective-permute-start(bf16[8,272,128]{2,1,0:T(8,128)(2,1)} %all-to-all-done.6.own_ref), channel_id=1, source_target_pairs={{0,32},{32,0},{1,33},{33,1},{2,34},{34,2},{3,35},{35,3},{4,36},{36... | collective-permute-start | bytes 1671176 | tf_op jit(solution)/shard_map/ppermute | solution.py:32

commit v10 on v7

--- a/solution.py
+++ b/solution.py
@@ -242,39 +242,45 @@
 
 def last_kernel(
     its_ref, part_ref, sums_ref, centered_ref, product_ref, unit_ref,
-    enc_out, bias_ref, dec_out,
-    grad_ref, enc_ref, dec_ref, sems,
+    enc_out, bias_out, dec_out,
+    grad_ref, enc_ref, dec_ref, bias_ref, sems,
 ):
     count = enc_ref.shape[1] // LANES
     size = its_ref.shape[1] - 2 * count
     share = size // count
     dots = sums_ref[count : 2 * count] + sum_parts(its_ref, size)
     step = 2 * LANES
+    pieces = count // 2
     copies = []
-    for n in range(count // 2):
+
+    def send(source, target, sem):
+        copies.append(pltpu.make_async_copy(source, target, sems.at[sem]))
+        copies[-1].start()
+
+    for n in range(pieces):
         lanes = pl.ds(n * step, step)
         for k in (2 * n, 2 * n + 1):
             cut = pl.ds(k * LANES, LANES)
-            lines = pl.ds(k * share, share)
             ratio = sums_ref[2 * count + k : 2 * count + k + 1]
             dec_ref[:, cut] = (
                 product_ref[:, cut] - unit_ref[:, cut].astype(F32) * dots[k : k + 1]
             ) * ratio
-            total = jnp.zeros((share, LANES), F32)
-            for y in range(its_ref.shape[0]):
-                value = its_ref[y, lines, :]
-                grad_ref[pl.ds(y * share, share), cut] = value
-                total = total + value.astype(F32)
-            bias_ref[k : k + 1, :] = sums_ref[k : k + 1, :] + jnp.sum(total, axis=0, keepdims=True)
-        copies.append(pltpu.make_async_copy(dec_ref.at[:, lanes], dec_out.at[:, lanes], sems.at[2 * n]))
-        copies[-1].start()
+        send(dec_ref.at[:, lanes], dec_out.at[:, lanes], n)
+    for k in range(count):
+        lines = pl.ds(k * share, share)
+        total = jnp.zeros((share, LANES), F32)
+        for y in range(its_ref.shape[0]):
+            value = its_ref[y, lines, :]
+            grad_ref[pl.ds(y * share, share), pl.ds(k * LANES, LANES)] = value
+            total = total + value.astype(F32)
+        bias_ref[k : k + 1, :] = sums_ref[k : k + 1, :] + jnp.sum(total, axis=0, keepdims=True)
+    send(bias_ref, bias_out, 2 * pieces)
+    for n in range(pieces):
+        lanes = pl.ds(n * step, step)
         enc_ref[:, lanes] = part_ref[:, lanes] + dot(
             centered_ref[...], grad_ref[:, lanes], ((1,), (0,))
         )
-        copies.append(
-            pltpu.make_async_copy(enc_ref.at[:, lanes], enc_out.at[:, lanes], sems.at[2 * n + 1])
-        )
-        copies[-1].start()
+        send(enc_ref.at[:, lanes], enc_out.at[:, lanes], pieces + n)
     for copy in copies:
         copy.wait()
 
@@ -385,9 +391,10 @@
             pltpu.VMEM((rows, latents), BF16),
             pltpu.VMEM((width, latents), F32),
             pltpu.VMEM((width, latents), F32),
-            pltpu.SemaphoreType.DMA((blocks_n,)),
+            pltpu.VMEM((blocks_n, LANES), F32),
+            pltpu.SemaphoreType.DMA((blocks_n + 1,)),
         ],
-        (ANY, VMEM, ANY),
+        (ANY, ANY, ANY),
     )(its, enc_part, sums, centered_its, product, unit[:width])
     return (enc_grad, bias_grad.reshape(latents), dec_grad.T)
 

time: 157 us -> 157 us (level)
  no operation moved by 1% of the time
where the time goes in v10:
time: 157 us; the launch traced here: 156 us
  blocking collectives  73.7 us (47%)
  starting transfers between devices  51.9 us (33%)
  waiting for transfers between devices  15.4 us (10%)
  Pallas kernels  9.4 us (6%)
  local copies, waits for them, and re-layouts  3.53 us (2%)
    all_to_all x4, blocking collectives, exchange(): return lax.all_to_all(blocks, axis, 0, 0, tiled=False)  73.7 us
    ppermute x8, starting transfers between devices, swap(): return lax.ppermute(block, 'core', [(0, 1), (1, 0)])  36.3 us
    all_to_all x3, starting transfers between devices, exchange(): return lax.all_to_all(blocks, axis, 0, 0, tiled=False)  15.6 us
    all_to_all x3, waiting for transfers between devices, exchange(): return lax.all_to_all(blocks, axis, 0, 0, tiled=False)  13.3 us
  transfers between devices with their start and end apart: 11, of which 6 were waited for; matrix products, arithmetic and copies ran while one was open for 1% of the time, Pallas kernels for 1%

profile of v10, /device:TPU:1, one launch (start us, length us, event | category | flops | bytes accessed | tf_op | source)
XLA Modules:
  0.0 156.0 jit_solution(3047959376946446302)
XLA Ops:
  0.7 0.9 copy-done.4
  1.6 0.7 copy-done.6
  2.2 0.8 shard_map.85
  3.0 8.8 %collective-permute-start = (bf16[8,576]{1,0:T(8,128)(2,1)S(1)}, bf16[8,576]{1,0:T(8,128)(2,1)S(1)}, u32[]{:S(2)}, u32[]{:S(2)}) collective-permute-start(bf16[8,576]{1,0:T(8,128)(2,1)S(1)} %get-tuple-element.15), channel_id=1, source_target_pairs={{0,32},{32,0},{1,33},{33,1},{2,34},{34,2},{3,35},{35,3},{4,36},{36... | collective-permute-start | bytes 27656 | tf_op jit(solution)/shard_map/ppermute | solution.py:25
  11.8 0.8 collective-permute-done.got_ref
  12.7 0.8 shard_map.86
  13.4 7.6 %all-to-all-start = ((bf16[32,8,576]{2,1,0:T(8,128)(2,1)}), bf16[32,8,576]{2,1,0:T(8,128)(2,1)S(1)}, u32[]{:S(2)}, u32[]{:S(2)}) async-start(bf16[32,8,576]{2,1,0:T(8,128)(2,1)} %get-tuple-element.16), calls=%async_computation | async-start | bytes 655360 | tf_op jit(solution)/shard_map/all_to_all | solution.py:21
  21.1 2.5 %collective-permute-start.3 = (bf16[288,1024]{1,0:T(8,128)(2,1)}, bf16[288,1024]{1,0:T(8,128)(2,1)S(1)}, u32[]{:S(2)}, u32[]{:S(2)}) collective-permute-start(bf16[288,1024]{1,0:T(8,128)(2,1)} %bitcast.16), channel_id=1, source_target_pairs={{0,32},{32,0},{1,33},{33,1},{2,34},{34,2},{3,35},{35,3},{4,36},{36... | collective-permute-start | bytes 1769480 | tf_op jit(solution)/shard_map/ppermute | solution.py:25
  23.6 1.9 %collective-permute-start.2 = (bf16[288,1024]{1,0:T(8,128)(2,1)}, bf16[288,1024]{1,0:T(8,128)(2,1)S(1)}, u32[]{:S(2)}, u32[]{:S(2)}) collective-permute-start(bf16[288,1024]{1,0:T(8,128)(2,1)} %enc_own.1), channel_id=1, source_target_pairs={{0,32},{32,0},{1,33},{33,1},{2,34},{34,2},{3,35},{35,3},{4,36},{36... | collective-permute-start | bytes 1769480 | tf_op jit(solution)/shard_map/ppermute | solution.py:25
  25.5 2.4 %collective-permute-start.1 = (f32[288]{0:T(512)}, f32[288]{0:T(512)S(1)}, u32[]{:S(2)}, u32[]{:S(2)}) collective-permute-start(f32[288]{0:T(512)} %param.11), channel_id=1, source_target_pairs={{0,32},{32,0},{1,33},{33,1},{2,34},{34,2},{3,35},{35,3},{4,36},{36... | collective-permute-start | bytes 3464 | tf_op jit(solution)/shard_map/ppermute | solution.py:25
  27.9 0.7 broadcast_in_dim.6
  29.1 2.5 %all-to-all-done = bf16[32,8,576]{2,1,0:T(8,128)(2,1)S(1)} async-done(((bf16[32,8,576]{2,1,0:T(8,128)(2,1)}), bf16[32,8,576]{2,1,0:T(8,128)(2,1)S(1)}, u32[]{:S(2)}, u32[]{:S(2)}) %all-to-all-start) | async-done | bytes 294944 | tf_op jit(solution)/shard_map/all_to_all | solution.py:21
  31.9 0.6 shard_map.87
  32.5 20.0 %all_to_all.35.blocks_ref.pre_ref = bf16[8,272,128]{2,1,0:T(8,128)(2,1)S(1)} all-to-all(bf16[8,272,128]{2,1,0:T(8,128)(2,1)S(1)} %shard_map.87), channel_id=1, replica_groups=mesh['y'=8,'core'=2,'x'=4,'z'=8] {'y'}, dimensions={0} | all-to-all | bytes 1114112 | tf_op jit(solution)/shard_map/all_to_all | solution.py:21
  52.5 1.0 shard_map.88
  53.5 3.8 %all-to-all-start.2 = ((bf16[8,256,128]{2,1,0:T(8,128)(2,1)}), bf16[8,256,128]{2,1,0:T(8,128)(2,1)S(1)}, u32[]{:S(2)}, u32[]{:S(2)}) async-start(bf16[8,256,128]{2,1,0:T(8,128)(2,1)} %shard_map.88), calls=%async_computation.2 | async-start | bytes 1048576 | tf_op jit(solution)/shard_map/all_to_all | solution.py:21
  57.3 1.1 copy-done.2
  58.8 10.8 %all-to-all-done.2.copies_ref = bf16[8,256,128]{2,1,0:T(8,128)(2,1)S(1)} async-done(((bf16[8,256,128]{2,1,0:T(8,128)(2,1)}), bf16[8,256,128]{2,1,0:T(8,128)(2,1)S(1)}, u32[]{:S(2)}, u32[]{:S(2)}) %all-to-all-start.2) | async-done | bytes 524320 | tf_op jit(solution)/shard_map/all_to_all | solution.py:21
  69.5 0.6 shard_map.90
  70.2 23.5 %all_to_all.36.blocks_ref = bf16[32,8,576]{2,1,0:T(8,128)(2,1)S(1)} all-to-all(bf16[32,8,576]{2,1,0:T(8,128)(2,1)S(1)} %shard_map.90), channel_id=1, replica_groups=mesh['y'=8,'core'=2,'x'=4,'z'=8] {'x','z'}, dimensions={0} | all-to-all | bytes 589824 | tf_op jit(solution)/shard_map/all_to_all | solution.py:21
  93.8 14.7 %all_to_all.37.error_ref = bf16[32,8,576]{2,1,0:T(8,128)(2,1)S(1)} all-to-all(bf16[32,8,576]{2,1,0:T(8,128)(2,1)S(1)} %shard_map.91), channel_id=1, replica_groups=mesh['y'=8,'core'=2,'x'=4,'z'=8] {'x','z'}, dimensions={0} | all-to-all | bytes 589824 | tf_op jit(solution)/shard_map/all_to_all | solution.py:21
  108.5 0.6 shard_map.92
  109.1 15.5 %all_to_all.38.blocks_ref = bf16[8,256,128]{2,1,0:T(8,128)(2,1)S(1)} all-to-all(bf16[8,256,128]{2,1,0:T(8,128)(2,1)S(1)} %shard_map.92), channel_id=1, replica_groups=mesh['y'=8,'core'=2,'x'=4,'z'=8] {'y'}, dimensions={0} | all-to-all | bytes 1048576 | tf_op jit(solution)/shard_map/all_to_all | solution.py:21
  124.6 1.1 shard_map.93
  125.6 4.2 %all-to-all-start.6 = ((bf16[8,272,128]{2,1,0:T(8,128)(2,1)}), bf16[8,272,128]{2,1,0:T(8,128)(2,1)}, u32[]{:S(2)}, u32[]{:S(2)}) async-start(bf16[8,272,128]{2,1,0:T(8,128)(2,1)} %shard_map.93), calls=%async_computation.6 | async-start | bytes 1114112 | tf_op jit(solution)/shard_map/all_to_all | solution.py:21
  130.0 8.9 %collective-permute-start.7 = (bf16[256,1024]{1,0:T(8,128)(2,1)S(1)}, bf16[256,1024]{1,0:T(8,128)(2,1)S(1)}, u32[]{:S(2)}, u32[]{:S(2)}) collective-permute-start(bf16[256,1024]{1,0:T(8,128)(2,1)S(1)} %shard_map.96), channel_id=1, source_target_pairs={{0,32},{32,0},{1,33},{33,1},{2,34},{34,2},{3,35},{35,3},{4,36},{36... | collective-permute-start | bytes 1572872 | tf_op jit(solution)/shard_map/ppermute | solution.py:25
  139.1 1.9 %collective-permute-start.5 = (bf16[288,256]{1,0:T(8,128)(2,1)S(1)}, bf16[288,256]{1,0:T(8,128)(2,1)S(1)}, u32[]{:S(2)}, u32[]{:S(2)}) collective-permute-start(bf16[288,256]{1,0:T(8,128)(2,1)S(1)} %get-tuple-element.21), channel_id=1, source_target_pairs={{0,32},{32,0},{1,33},{33,1},{2,34},{34,2},{3,35},{35,3},{4,36},{36... | collective-permute-start | bytes 442376 | tf_op jit(solution)/shard_map/ppermute | solution.py:25
  141.2 2.4 %collective-permute-start.6 = (bf16[256,288]{1,0:T(8,128)(2,1)S(1)}, bf16[256,288]{1,0:T(8,128)(2,1)S(1)}, u32[]{:S(2)}, u32[]{:S(2)}) collective-permute-start(bf16[256,288]{1,0:T(8,128)(2,1)S(1)} %slice.13), channel_id=1, source_target_pairs={{0,32},{32,0},{1,33},{33,1},{2,34},{34,2},{3,35},{35,3},{4,36},{36... | collective-permute-start | bytes 442376 | tf_op jit(solution)/shard_map/ppermute | solution.py:25
  144.0 0.7 collective-permute-done.6
  145.0 7.4 %collective-permute-start.4 = (bf16[8,272,128]{2,1,0:T(8,128)(2,1)}, bf16[8,272,128]{2,1,0:T(8,128)(2,1)S(1)}, u32[]{:S(2)}, u32[]{:S(2)}) collective-permute-start(bf16[8,272,128]{2,1,0:T(8,128)(2,1)} %all-to-all-done.6.own_ref), channel_id=1, source_target_pairs={{0,32},{32,0},{1,33},{33,1},{2,34},{34,2},{3,35},{35,3},{4,36},{36... | collective-permute-start | bytes 1671176 | tf_op jit(solution)/shard_map/ppermute | solution.py:25
  152.4 1.4 shard_map.95
  154.2 1.8 %shard_map.97 = (f32[288,1024]{1,0:T(8,128)}, f32[8,128]{1,0:T(8,128)}, f32[288,1024]{1,0:T(8,128)}) custom-call(bf16[8,272,128]{2,1,0:T(8,128)(2,1)S(1)} %collective-permute-done.4.its_ref, f32[288,1024]{1,0:T(8,128)S(1)} %get-tuple-element.19.part_ref, f32[24,128]{1,0:T(8,128)S(1)} %get-tuple-element.20.sums_ref, ...), custom_call_target="tpu_custom_call" | custom-call | flops 301989888 | bytes 6291456 | tf_op jit(solution)/shard_map/pallas_call | solution.py:385
  (30 shorter events, 2.7 us)
Async XLA Ops:
  0.6 31.0 %copy-start = (bf16[1024,288]{0,1:T(8,128)(2,1)S(1)}, bf16[1024,288]{0,1:T(8,128)(2,1)}, u32[]{:S(2)}) copy-start(bf16[1024,288]{0,1:T(8,128)(2,1)} %param.10) | copy-start | bytes 1769476
  0.6 0.9 copy-start.4
  1.6 0.7 copy-start.6
  3.0 9.6 %collective-permute-start = (bf16[8,576]{1,0:T(8,128)(2,1)S(1)}, bf16[8,576]{1,0:T(8,128)(2,1)S(1)}, u32[]{:S(2)}, u32[]{:S(2)}) collective-permute-start(bf16[8,576]{1,0:T(8,128)(2,1)S(1)} %get-tuple-element.15), channel_id=1, source_target_pairs={{0,32},{32,0},{1,33},{33,1},{2,34},{34,2},{3,35},{35,3},{4,36},{36... | collective-permute-start | bytes 27656 | tf_op jit(solution)/shard_map/ppermute | solution.py:25
  13.4 18.5 %copy-start.3 = (bf16[288,1024]{1,0:T(8,128)(2,1)S(1)}, bf16[288,1024]{1,0:T(8,128)(2,1)}, u32[]{:S(2)}) copy-start(bf16[288,1024]{1,0:T(8,128)(2,1)} %enc_own.1) | copy-start | bytes 1769476
  13.4 18.1 %all-to-all-start = ((bf16[32,8,576]{2,1,0:T(8,128)(2,1)}), bf16[32,8,576]{2,1,0:T(8,128)(2,1)S(1)}, u32[]{:S(2)}, u32[]{:S(2)}) async-start(bf16[32,8,576]{2,1,0:T(8,128)(2,1)} %get-tuple-element.16), calls=%async_computation | async-start | bytes 655360 | tf_op jit(solution)/shard_map/all_to_all | solution.py:21
  21.1 10.6 %collective-permute-start.3 = (bf16[288,1024]{1,0:T(8,128)(2,1)}, bf16[288,1024]{1,0:T(8,128)(2,1)S(1)}, u32[]{:S(2)}, u32[]{:S(2)}) collective-permute-start(bf16[288,1024]{1,0:T(8,128)(2,1)} %bitcast.16), channel_id=1, source_target_pairs={{0,32},{32,0},{1,33},{33,1},{2,34},{34,2},{3,35},{35,3},{4,36},{36... | collective-permute-start | bytes 1769480 | tf_op jit(solution)/shard_map/ppermute | solution.py:25
  23.6 8.3 %collective-permute-start.2 = (bf16[288,1024]{1,0:T(8,128)(2,1)}, bf16[288,1024]{1,0:T(8,128)(2,1)S(1)}, u32[]{:S(2)}, u32[]{:S(2)}) collective-permute-start(bf16[288,1024]{1,0:T(8,128)(2,1)} %enc_own.1), channel_id=1, source_target_pairs={{0,32},{32,0},{1,33},{33,1},{2,34},{34,2},{3,35},{35,3},{4,36},{36... | collective-permute-start | bytes 1769480 | tf_op jit(solution)/shard_map/ppermute | solution.py:25
  25.5 3.4 %collective-permute-start.1 = (f32[288]{0:T(512)}, f32[288]{0:T(512)S(1)}, u32[]{:S(2)}, u32[]{:S(2)}) collective-permute-start(f32[288]{0:T(512)} %param.11), channel_id=1, source_target_pairs={{0,32},{32,0},{1,33},{33,1},{2,34},{34,2},{3,35},{35,3},{4,36},{36... | collective-permute-start | bytes 3464 | tf_op jit(solution)/shard_map/ppermute | solution.py:25
  31.6 0.9 copy-start.1
  31.9 20.6 %copy-start.5 = (f32[1024]{0:T(1024)S(1)}, f32[1024]{0:T(1024)}, u32[]{:S(2)}) copy-start(f32[1024]{0:T(1024)} %param.9) | copy-start | bytes 12292
  53.5 16.1 %all-to-all-start.2 = ((bf16[8,256,128]{2,1,0:T(8,128)(2,1)}), bf16[8,256,128]{2,1,0:T(8,128)(2,1)S(1)}, u32[]{:S(2)}, u32[]{:S(2)}) async-start(bf16[8,256,128]{2,1,0:T(8,128)(2,1)} %shard_map.88), calls=%async_computation.2 | async-start | bytes 1048576 | tf_op jit(solution)/shard_map/all_to_all | solution.py:21
  57.3 1.1 copy-start.2
  125.6 19.4 %all-to-all-start.6 = ((bf16[8,272,128]{2,1,0:T(8,128)(2,1)}), bf16[8,272,128]{2,1,0:T(8,128)(2,1)}, u32[]{:S(2)}, u32[]{:S(2)}) async-start(bf16[8,272,128]{2,1,0:T(8,128)(2,1)} %shard_map.93), calls=%async_computation.6 | async-start | bytes 1114112 | tf_op jit(solution)/shard_map/all_to_all | solution.py:21
  130.0 14.0 %collective-permute-start.7 = (bf16[256,1024]{1,0:T(8,128)(2,1)S(1)}, bf16[256,1024]{1,0:T(8,128)(2,1)S(1)}, u32[]{:S(2)}, u32[]{:S(2)}) collective-permute-start(bf16[256,1024]{1,0:T(8,128)(2,1)S(1)} %shard_map.96), channel_id=1, source_target_pairs={{0,32},{32,0},{1,33},{33,1},{2,34},{34,2},{3,35},{35,3},{4,36},{36... | collective-permute-start | bytes 1572872 | tf_op jit(solution)/shard_map/ppermute | solution.py:25
  139.1 14.7 %collective-permute-start.5 = (bf16[288,256]{1,0:T(8,128)(2,1)S(1)}, bf16[288,256]{1,0:T(8,128)(2,1)S(1)}, u32[]{:S(2)}, u32[]{:S(2)}) collective-permute-start(bf16[288,256]{1,0:T(8,128)(2,1)S(1)} %get-tuple-element.21), channel_id=1, source_target_pairs={{0,32},{32,0},{1,33},{33,1},{2,34},{34,2},{3,35},{35,3},{4,36},{36... | collective-permute-start | bytes 442376 | tf_op jit(solution)/shard_map/ppermute | solution.py:25
  141.2 3.5 %collective-permute-start.6 = (bf16[256,288]{1,0:T(8,128)(2,1)S(1)}, bf16[256,288]{1,0:T(8,128)(2,1)S(1)}, u32[]{:S(2)}, u32[]{:S(2)}) collective-permute-start(bf16[256,288]{1,0:T(8,128)(2,1)S(1)} %slice.13), channel_id=1, source_target_pairs={{0,32},{32,0},{1,33},{33,1},{2,34},{34,2},{3,35},{35,3},{4,36},{36... | collective-permute-start | bytes 442376 | tf_op jit(solution)/shard_map/ppermute | solution.py:25
  145.0 9.2 %collective-permute-start.4 = (bf16[8,272,128]{2,1,0:T(8,128)(2,1)}, bf16[8,272,128]{2,1,0:T(8,128)(2,1)S(1)}, u32[]{:S(2)}, u32[]{:S(2)}) collective-permute-start(bf16[8,272,128]{2,1,0:T(8,128)(2,1)} %all-to-all-done.6.own_ref), channel_id=1, source_target_pairs={{0,32},{32,0},{1,33},{33,1},{2,34},{34,2},{3,35},{35,3},{4,36},{36... | collective-permute-start | bytes 1671176 | tf_op jit(solution)/shard_map/ppermute | solution.py:25

commit v11 on v10

--- a/solution.py
+++ b/solution.py
@@ -149,8 +149,16 @@
     return jnp.sqrt(sum_parts(blocks_ref, blocks_ref.shape[1] - 2 * count) + 1e-06)
 
 
-def unit_kernel(blocks_ref, dec_own, dec_other, unit_ref):
+def unit_kernel(blocks_ref, dec_own, dec_other, bias_ref, unit_ref, active_ref, gate_ref):
     width, latents = dec_own.shape
+    size = active_ref.shape[0]
+    share = size // bias_ref.shape[0]
+    total = sum_blocks(blocks_ref, size)
+    for k in range(bias_ref.shape[0]):
+        lines = slice(k * share, (k + 1) * share)
+        value, small, active = soft_parts(total[lines], bias_ref[k : k + 1, :])
+        active_ref[lines, :] = active
+        gate_ref[lines, :] = jnp.where(value >= 0.0, 1.0, small) / (1.0 + small)
     norms = norms_of(blocks_ref, latents // LANES)
     for k in range(latents // LANES):
         lanes = pl.ds(k * LANES, LANES)
@@ -199,22 +207,19 @@
         spread(part.astype(BF16), out_ref, 2 * n)
 
 
-def grad_kernel(blocks_ref, pre_ref, bias_ref, copies_ref):
+def grad_kernel(blocks_ref, active_ref, gate_ref, copies_ref):
     size = blocks_ref.shape[1]
-    count = bias_ref.shape[0]
+    count = (copies_ref.shape[1] - size) // 2
     share = size // count
     raw = sum_blocks(blocks_ref, size)
-    pre = sum_blocks(pre_ref, size)
     row = lax.broadcasted_iota(jnp.int32, (count, LANES), 0)
     dots = jnp.zeros((count, LANES), F32)
     for k in range(count):
         lines = slice(k * share, (k + 1) * share)
-        value, small, active = soft_parts(pre[lines], bias_ref[k : k + 1, :])
-        gate = jnp.where(value >= 0.0, 1.0, small) / (1.0 + small)
-        grad = ((raw[lines] + 1.0 / ROWS) * gate).astype(BF16)
+        grad = ((raw[lines] + 1.0 / ROWS) * gate_ref[lines, :]).astype(BF16)
         for y in range(copies_ref.shape[0]):
             copies_ref[y, lines, :] = grad
-        part = jnp.sum(active.astype(F32) * raw[lines], axis=0, keepdims=True)
+        part = jnp.sum(active_ref[lines, :].astype(F32) * raw[lines], axis=0, keepdims=True)
         dots = jnp.where(row == k, part, dots)
     high = dots.astype(BF16).astype(F32)
     parts = jnp.concatenate([high, dots - high], axis=0).astype(BF16)
@@ -334,9 +339,16 @@
     copies = call(
         act_kernel, shape((count_y, size, LANES), BF16), [VMEM] * 2, (1 << 20, 1 << 20)
     )(blocks, enc_bias)
-    unit = call(unit_kernel, shape((wide, latents), BF16), [VMEM] * 3, (1 << 20, moved))(
-        blocks, dec_own, dec_other
-    )
+    unit, active_share, gate = call(
+        unit_kernel,
+        (
+            shape((wide, latents), BF16),
+            shape((size, LANES), BF16),
+            shape((size, LANES), F32),
+        ),
+        [VMEM] * 4,
+        (1 << 20, moved),
+    )(blocks, dec_own, dec_other, enc_bias)
     copies = exchange(copies, "y")
     partial = call(
         rebuild_kernel,
@@ -370,7 +382,7 @@
             shape((count_y, size + extra, LANES), BF16),
             [VMEM] * 3,
             (1 << 20, 1 << 20),
-        )(exchange(raw_blocks, "y"), blocks, enc_bias),
+        )(exchange(raw_blocks, "y"), active_share, gate),
         "y",
     )
     its = swap(own)

time: 157 us -> 157 us (level)
    unnamed x14 -> x22, local copies, waits for them, and re-layouts: 2.68 us -> 3.96 us
where the time goes in v11:
time: 157 us; the launch traced here: 156 us
  blocking collectives  73.7 us (47%)
  starting transfers between devices  51.9 us (33%)
  waiting for transfers between devices  14 us (9%)
  Pallas kernels  9.34 us (6%)
  local copies, waits for them, and re-layouts  4.81 us (3%)
    all_to_all x4, blocking collectives, exchange(): return lax.all_to_all(blocks, axis, 0, 0, tiled=False)  73.7 us
    ppermute x8, starting transfers between devices, swap(): return lax.ppermute(block, 'core', [(0, 1), (1, 0)])  36.3 us
    all_to_all x3, starting transfers between devices, exchange(): return lax.all_to_all(blocks, axis, 0, 0, tiled=False)  15.6 us
    all_to_all x3, waiting for transfers between devices, exchange(): return lax.all_to_all(blocks, axis, 0, 0, tiled=False)  11.9 us
    unnamed x22, local copies, waits for them, and re-layouts  3.96 us
  transfers between devices with their start and end apart: 11, of which 6 were waited for; matrix products, arithmetic and copies ran while one was open for 1% of the time, Pallas kernels for 1%

profile of v11, /device:TPU:1, one launch (start us, length us, event | category | flops | bytes accessed | tf_op | source)
XLA Modules:
  0.0 155.8 jit_solution(8812660849404135241)
XLA Ops:
  0.7 0.9 copy-done.6
  1.6 0.7 copy-done.10
  2.2 0.8 shard_map.85
  3.0 8.8 %collective-permute-start = (bf16[8,576]{1,0:T(8,128)(2,1)S(1)}, bf16[8,576]{1,0:T(8,128)(2,1)S(1)}, u32[]{:S(2)}, u32[]{:S(2)}) collective-permute-start(bf16[8,576]{1,0:T(8,128)(2,1)S(1)} %get-tuple-element.18), channel_id=1, source_target_pairs={{0,32},{32,0},{1,33},{33,1},{2,34},{34,2},{3,35},{35,3},{4,36},{36... | collective-permute-start | bytes 27656 | tf_op jit(solution)/shard_map/ppermute | solution.py:25
  11.8 0.8 collective-permute-done.got_ref
  12.7 0.8 shard_map.86
  13.4 7.6 %all-to-all-start = ((bf16[32,8,576]{2,1,0:T(8,128)(2,1)}), bf16[32,8,576]{2,1,0:T(8,128)(2,1)S(1)}, u32[]{:S(2)}, u32[]{:S(2)}) async-start(bf16[32,8,576]{2,1,0:T(8,128)(2,1)} %get-tuple-element.19), calls=%async_computation | async-start | bytes 655360 | tf_op jit(solution)/shard_map/all_to_all | solution.py:21
  21.1 2.5 %collective-permute-start.3 = (bf16[288,1024]{1,0:T(8,128)(2,1)}, bf16[288,1024]{1,0:T(8,128)(2,1)S(1)}, u32[]{:S(2)}, u32[]{:S(2)}) collective-permute-start(bf16[288,1024]{1,0:T(8,128)(2,1)} %bitcast.16), channel_id=1, source_target_pairs={{0,32},{32,0},{1,33},{33,1},{2,34},{34,2},{3,35},{35,3},{4,36},{36... | collective-permute-start | bytes 1769480 | tf_op jit(solution)/shard_map/ppermute | solution.py:25
  23.6 1.9 %collective-permute-start.2 = (bf16[288,1024]{1,0:T(8,128)(2,1)}, bf16[288,1024]{1,0:T(8,128)(2,1)S(1)}, u32[]{:S(2)}, u32[]{:S(2)}) collective-permute-start(bf16[288,1024]{1,0:T(8,128)(2,1)} %enc_own.1), channel_id=1, source_target_pairs={{0,32},{32,0},{1,33},{33,1},{2,34},{34,2},{3,35},{35,3},{4,36},{36... | collective-permute-start | bytes 1769480 | tf_op jit(solution)/shard_map/ppermute | solution.py:25
  25.5 2.4 %collective-permute-start.1 = (f32[288]{0:T(512)}, f32[288]{0:T(512)S(1)}, u32[]{:S(2)}, u32[]{:S(2)}) collective-permute-start(f32[288]{0:T(512)} %param.11), channel_id=1, source_target_pairs={{0,32},{32,0},{1,33},{33,1},{2,34},{34,2},{3,35},{35,3},{4,36},{36... | collective-permute-start | bytes 3464 | tf_op jit(solution)/shard_map/ppermute | solution.py:25
  27.9 0.7 broadcast_in_dim.6
  29.1 2.5 %all-to-all-done = bf16[32,8,576]{2,1,0:T(8,128)(2,1)S(1)} async-done(((bf16[32,8,576]{2,1,0:T(8,128)(2,1)}), bf16[32,8,576]{2,1,0:T(8,128)(2,1)S(1)}, u32[]{:S(2)}, u32[]{:S(2)}) %all-to-all-start) | async-done | bytes 294944 | tf_op jit(solution)/shard_map/all_to_all | solution.py:21
  32.5 20.0 %all_to_all.35.blocks_ref = bf16[8,272,128]{2,1,0:T(8,128)(2,1)S(1)} all-to-all(bf16[8,272,128]{2,1,0:T(8,128)(2,1)S(1)} %shard_map.87), channel_id=1, replica_groups=mesh['y'=8,'core'=2,'x'=4,'z'=8] {'y'}, dimensions={0} | all-to-all | bytes 1114112 | tf_op jit(solution)/shard_map/all_to_all | solution.py:21
  52.5 1.0 shard_map.88
  53.5 3.8 %all-to-all-start.2 = ((bf16[8,256,128]{2,1,0:T(8,128)(2,1)}), bf16[8,256,128]{2,1,0:T(8,128)(2,1)S(1)}, u32[]{:S(2)}, u32[]{:S(2)}) async-start(bf16[8,256,128]{2,1,0:T(8,128)(2,1)} %shard_map.88), calls=%async_computation.2 | async-start | bytes 1048576 | tf_op jit(solution)/shard_map/all_to_all | solution.py:21
  57.3 1.1 copy-done.2
  58.9 0.6 copy-done.4
  59.5 0.6 copy-done.7
  60.2 9.4 %all-to-all-done.2.copies_ref = bf16[8,256,128]{2,1,0:T(8,128)(2,1)S(1)} async-done(((bf16[8,256,128]{2,1,0:T(8,128)(2,1)}), bf16[8,256,128]{2,1,0:T(8,128)(2,1)S(1)}, u32[]{:S(2)}, u32[]{:S(2)}) %all-to-all-start.2) | async-done | bytes 524320 | tf_op jit(solution)/shard_map/all_to_all | solution.py:21
  69.5 0.6 shard_map.90
  70.2 23.5 %all_to_all.36.blocks_ref = bf16[32,8,576]{2,1,0:T(8,128)(2,1)S(1)} all-to-all(bf16[32,8,576]{2,1,0:T(8,128)(2,1)S(1)} %shard_map.90), channel_id=1, replica_groups=mesh['y'=8,'core'=2,'x'=4,'z'=8] {'x','z'}, dimensions={0} | all-to-all | bytes 589824 | tf_op jit(solution)/shard_map/all_to_all | solution.py:21
  93.8 14.7 %all_to_all.37.error_ref = bf16[32,8,576]{2,1,0:T(8,128)(2,1)S(1)} all-to-all(bf16[32,8,576]{2,1,0:T(8,128)(2,1)S(1)} %shard_map.91), channel_id=1, replica_groups=mesh['y'=8,'core'=2,'x'=4,'z'=8] {'x','z'}, dimensions={0} | all-to-all | bytes 589824 | tf_op jit(solution)/shard_map/all_to_all | solution.py:21
  109.1 15.5 %all_to_all.38.blocks_ref = bf16[8,256,128]{2,1,0:T(8,128)(2,1)S(1)} all-to-all(bf16[8,256,128]{2,1,0:T(8,128)(2,1)S(1)} %shard_map.92), channel_id=1, replica_groups=mesh['y'=8,'core'=2,'x'=4,'z'=8] {'y'}, dimensions={0} | all-to-all | bytes 1048576 | tf_op jit(solution)/shard_map/all_to_all | solution.py:21
  124.6 0.9 shard_map.93
  125.5 4.2 %all-to-all-start.6 = ((bf16[8,272,128]{2,1,0:T(8,128)(2,1)}), bf16[8,272,128]{2,1,0:T(8,128)(2,1)}, u32[]{:S(2)}, u32[]{:S(2)}) async-start(bf16[8,272,128]{2,1,0:T(8,128)(2,1)} %shard_map.93), calls=%async_computation.6 | async-start | bytes 1114112 | tf_op jit(solution)/shard_map/all_to_all | solution.py:21
  129.8 8.9 %collective-permute-start.7 = (bf16[256,1024]{1,0:T(8,128)(2,1)S(1)}, bf16[256,1024]{1,0:T(8,128)(2,1)S(1)}, u32[]{:S(2)}, u32[]{:S(2)}) collective-permute-start(bf16[256,1024]{1,0:T(8,128)(2,1)S(1)} %shard_map.96), channel_id=1, source_target_pairs={{0,32},{32,0},{1,33},{33,1},{2,34},{34,2},{3,35},{35,3},{4,36},{36... | collective-permute-start | bytes 1572872 | tf_op jit(solution)/shard_map/ppermute | solution.py:25
  138.9 1.9 %collective-permute-start.5 = (bf16[288,256]{1,0:T(8,128)(2,1)S(1)}, bf16[288,256]{1,0:T(8,128)(2,1)S(1)}, u32[]{:S(2)}, u32[]{:S(2)}) collective-permute-start(bf16[288,256]{1,0:T(8,128)(2,1)S(1)} %get-tuple-element.27), channel_id=1, source_target_pairs={{0,32},{32,0},{1,33},{33,1},{2,34},{34,2},{3,35},{35,3},{4,36},{36... | collective-permute-start | bytes 442376 | tf_op jit(solution)/shard_map/ppermute | solution.py:25
  141.0 2.4 %collective-permute-start.6 = (bf16[256,288]{1,0:T(8,128)(2,1)S(1)}, bf16[256,288]{1,0:T(8,128)(2,1)S(1)}, u32[]{:S(2)}, u32[]{:S(2)}) collective-permute-start(bf16[256,288]{1,0:T(8,128)(2,1)S(1)} %slice.13), channel_id=1, source_target_pairs={{0,32},{32,0},{1,33},{33,1},{2,34},{34,2},{3,35},{35,3},{4,36},{36... | collective-permute-start | bytes 442376 | tf_op jit(solution)/shard_map/ppermute | solution.py:25
  143.8 0.7 collective-permute-done.6
  144.9 7.4 %collective-permute-start.4 = (bf16[8,272,128]{2,1,0:T(8,128)(2,1)}, bf16[8,272,128]{2,1,0:T(8,128)(2,1)S(1)}, u32[]{:S(2)}, u32[]{:S(2)}) collective-permute-start(bf16[8,272,128]{2,1,0:T(8,128)(2,1)} %all-to-all-done.6.own_ref), channel_id=1, source_target_pairs={{0,32},{32,0},{1,33},{33,1},{2,34},{34,2},{3,35},{35,3},{4,36},{36... | collective-permute-start | bytes 1671176 | tf_op jit(solution)/shard_map/ppermute | solution.py:25
  152.2 1.4 shard_map.95
  154.0 1.8 %shard_map.97 = (f32[288,1024]{1,0:T(8,128)}, f32[8,128]{1,0:T(8,128)}, f32[288,1024]{1,0:T(8,128)}) custom-call(bf16[8,272,128]{2,1,0:T(8,128)(2,1)S(1)} %collective-permute-done.4.its_ref, f32[288,1024]{1,0:T(8,128)S(1)} %get-tuple-element.25.part_ref, f32[24,128]{1,0:T(8,128)S(1)} %get-tuple-element.26.sums_ref, ...), custom_call_target="tpu_custom_call" | custom-call | flops 301989888 | bytes 6291456 | tf_op jit(solution)/shard_map/pallas_call | solution.py:397
  (38 shorter events, 4.0 us)
Async XLA Ops:
  0.6 31.0 %copy-start = (bf16[1024,288]{0,1:T(8,128)(2,1)S(1)}, bf16[1024,288]{0,1:T(8,128)(2,1)}, u32[]{:S(2)}) copy-start(bf16[1024,288]{0,1:T(8,128)(2,1)} %param.10) | copy-start | bytes 1769476
  0.6 0.9 copy-start.6
  1.6 0.7 copy-start.10
  3.0 9.6 %collective-permute-start = (bf16[8,576]{1,0:T(8,128)(2,1)S(1)}, bf16[8,576]{1,0:T(8,128)(2,1)S(1)}, u32[]{:S(2)}, u32[]{:S(2)}) collective-permute-start(bf16[8,576]{1,0:T(8,128)(2,1)S(1)} %get-tuple-element.18), channel_id=1, source_target_pairs={{0,32},{32,0},{1,33},{33,1},{2,34},{34,2},{3,35},{35,3},{4,36},{36... | collective-permute-start | bytes 27656 | tf_op jit(solution)/shard_map/ppermute | solution.py:25
  13.4 18.5 %copy-start.3 = (bf16[288,1024]{1,0:T(8,128)(2,1)S(1)}, bf16[288,1024]{1,0:T(8,128)(2,1)}, u32[]{:S(2)}) copy-start(bf16[288,1024]{1,0:T(8,128)(2,1)} %enc_own.1) | copy-start | bytes 1769476
  13.4 18.1 %all-to-all-start = ((bf16[32,8,576]{2,1,0:T(8,128)(2,1)}), bf16[32,8,576]{2,1,0:T(8,128)(2,1)S(1)}, u32[]{:S(2)}, u32[]{:S(2)}) async-start(bf16[32,8,576]{2,1,0:T(8,128)(2,1)} %get-tuple-element.19), calls=%async_computation | async-start | bytes 655360 | tf_op jit(solution)/shard_map/all_to_all | solution.py:21
  21.1 10.6 %collective-permute-start.3 = (bf16[288,1024]{1,0:T(8,128)(2,1)}, bf16[288,1024]{1,0:T(8,128)(2,1)S(1)}, u32[]{:S(2)}, u32[]{:S(2)}) collective-permute-start(bf16[288,1024]{1,0:T(8,128)(2,1)} %bitcast.16), channel_id=1, source_target_pairs={{0,32},{32,0},{1,33},{33,1},{2,34},{34,2},{3,35},{35,3},{4,36},{36... | collective-permute-start | bytes 1769480 | tf_op jit(solution)/shard_map/ppermute | solution.py:25
  23.6 8.3 %collective-permute-start.2 = (bf16[288,1024]{1,0:T(8,128)(2,1)}, bf16[288,1024]{1,0:T(8,128)(2,1)S(1)}, u32[]{:S(2)}, u32[]{:S(2)}) collective-permute-start(bf16[288,1024]{1,0:T(8,128)(2,1)} %enc_own.1), channel_id=1, source_target_pairs={{0,32},{32,0},{1,33},{33,1},{2,34},{34,2},{3,35},{35,3},{4,36},{36... | collective-permute-start | bytes 1769480 | tf_op jit(solution)/shard_map/ppermute | solution.py:25
  25.5 3.4 %collective-permute-start.1 = (f32[288]{0:T(512)}, f32[288]{0:T(512)S(1)}, u32[]{:S(2)}, u32[]{:S(2)}) collective-permute-start(f32[288]{0:T(512)} %param.11), channel_id=1, source_target_pairs={{0,32},{32,0},{1,33},{33,1},{2,34},{34,2},{3,35},{35,3},{4,36},{36... | collective-permute-start | bytes 3464 | tf_op jit(solution)/shard_map/ppermute | solution.py:25
  31.6 0.9 copy-start.1
  31.9 20.6 %copy-start.9 = (f32[1024]{0:T(1024)S(1)}, f32[1024]{0:T(1024)}, u32[]{:S(2)}) copy-start(f32[1024]{0:T(1024)} %param.9) | copy-start | bytes 12292
  53.5 16.1 %all-to-all-start.2 = ((bf16[8,256,128]{2,1,0:T(8,128)(2,1)}), bf16[8,256,128]{2,1,0:T(8,128)(2,1)S(1)}, u32[]{:S(2)}, u32[]{:S(2)}) async-start(bf16[8,256,128]{2,1,0:T(8,128)(2,1)} %shard_map.88), calls=%async_computation.2 | async-start | bytes 1048576 | tf_op jit(solution)/shard_map/all_to_all | solution.py:21
  57.3 1.1 copy-start.2
  58.9 0.7 copy-start.4
  59.5 0.6 copy-start.7
  108.5 16.1 %copy-start.5 = (f32[256,128]{1,0:T(8,128)S(1)}, f32[256,128]{1,0:T(8,128)}, u32[]{:S(2)}) copy-start(f32[256,128]{1,0:T(8,128)} %copy-done.4) | copy-start | bytes 393220
  108.5 16.1 %copy-start.8 = (bf16[256,128]{1,0:T(8,128)(2,1)S(1)}, bf16[256,128]{1,0:T(8,128)(2,1)}, u32[]{:S(2)}) copy-start(bf16[256,128]{1,0:T(8,128)(2,1)} %copy-done.7) | copy-start | bytes 196612
  125.5 19.4 %all-to-all-start.6 = ((bf16[8,272,128]{2,1,0:T(8,128)(2,1)}), bf16[8,272,128]{2,1,0:T(8,128)(2,1)}, u32[]{:S(2)}, u32[]{:S(2)}) async-start(bf16[8,272,128]{2,1,0:T(8,128)(2,1)} %shard_map.93), calls=%async_computation.6 | async-start | bytes 1114112 | tf_op jit(solution)/shard_map/all_to_all | solution.py:21
  129.8 14.0 %collective-permute-start.7 = (bf16[256,1024]{1,0:T(8,128)(2,1)S(1)}, bf16[256,1024]{1,0:T(8,128)(2,1)S(1)}, u32[]{:S(2)}, u32[]{:S(2)}) collective-permute-start(bf16[256,1024]{1,0:T(8,128)(2,1)S(1)} %shard_map.96), channel_id=1, source_target_pairs={{0,32},{32,0},{1,33},{33,1},{2,34},{34,2},{3,35},{35,3},{4,36},{36... | collective-permute-start | bytes 1572872 | tf_op jit(solution)/shard_map/ppermute | solution.py:25
  138.9 14.7 %collective-permute-start.5 = (bf16[288,256]{1,0:T(8,128)(2,1)S(1)}, bf16[288,256]{1,0:T(8,128)(2,1)S(1)}, u32[]{:S(2)}, u32[]{:S(2)}) collective-permute-start(bf16[288,256]{1,0:T(8,128)(2,1)S(1)} %get-tuple-element.27), channel_id=1, source_target_pairs={{0,32},{32,0},{1,33},{33,1},{2,34},{34,2},{3,35},{35,3},{4,36},{36... | collective-permute-start | bytes 442376 | tf_op jit(solution)/shard_map/ppermute | solution.py:25
  141.0 3.5 %collective-permute-start.6 = (bf16[256,288]{1,0:T(8,128)(2,1)S(1)}, bf16[256,288]{1,0:T(8,128)(2,1)S(1)}, u32[]{:S(2)}, u32[]{:S(2)}) collective-permute-start(bf16[256,288]{1,0:T(8,128)(2,1)S(1)} %slice.13), channel_id=1, source_target_pairs={{0,32},{32,0},{1,33},{33,1},{2,34},{34,2},{3,35},{35,3},{4,36},{36... | collective-permute-start | bytes 442376 | tf_op jit(solution)/shard_map/ppermute | solution.py:25
  144.9 9.2 %collective-permute-start.4 = (bf16[8,272,128]{2,1,0:T(8,128)(2,1)}, bf16[8,272,128]{2,1,0:T(8,128)(2,1)S(1)}, u32[]{:S(2)}, u32[]{:S(2)}) collective-permute-start(bf16[8,272,128]{2,1,0:T(8,128)(2,1)} %all-to-all-done.6.own_ref), channel_id=1, source_target_pairs={{0,32},{32,0},{1,33},{33,1},{2,34},{34,2},{3,35},{35,3},{4,36},{36... | collective-permute-start | bytes 1671176 | tf_op jit(solution)/shard_map/ppermute | solution.py:25

commit v12 on v10

--- a/solution.py
+++ b/solution.py
@@ -46,15 +46,9 @@
     return jax.ShapeDtypeStruct(dims, kind)
 
 
-def pick_kernel(picked_hbm, residual_hbm, own_ref, other_ref, picked, table, sems):
+def pick_kernel(picked, table, own_ref, other_ref):
     width, tokens = table.shape
     piece = own_ref.shape[0]
-    pairs = ((residual_hbm, table), (picked_hbm, picked))
-    copies = [pltpu.make_async_copy(a, b, sems.at[i]) for i, (a, b) in enumerate(pairs)]
-    for copy in copies:
-        copy.start()
-    for copy in copies:
-        copy.wait()
     core = lax.axis_index("core")
     place = lax.axis_index("x") * lax.axis_size("z") + lax.axis_index("z")
     row = lax.broadcasted_iota(jnp.int32, (piece, tokens), 0)
@@ -303,13 +297,8 @@
     own_rows, other_rows = call(
         pick_kernel,
         (small, small),
-        [HBM] * 2,
+        [pl.BlockSpec(memory_space=pltpu.SMEM), VMEM],
         (1 << 20, 1 << 17),
-        [
-            pltpu.SMEM(picked.shape, jnp.int32),
-            pltpu.VMEM(residual.shape[::-1], BF16),
-            pltpu.SemaphoreType.DMA((2,)),
-        ],
     )(picked, residual.T)
     tensor_blocks = shape((count_t, piece, wide), BF16)
     local_rows, copies = call(join_kernel, (small, tensor_blocks), [VMEM] * 2, (1 << 12, 1 << 19))(

time: 157 us -> 157 us (level)
  no operation moved by 1% of the time
where the time goes in v12:
time: 157 us; the launch traced here: 156 us
  blocking collectives  73.7 us (47%)
  starting transfers between devices  52 us (33%)
  waiting for transfers between devices  15.4 us (10%)
  Pallas kernels  9.3 us (6%)
  local copies, waits for them, and re-layouts  3.53 us (2%)
    all_to_all x4, blocking collectives, exchange(): return lax.all_to_all(blocks, axis, 0, 0, tiled=False)  73.7 us
    ppermute x8, starting transfers between devices, swap(): return lax.ppermute(block, 'core', [(0, 1), (1, 0)])  36.3 us
    all_to_all x3, starting transfers between devices, exchange(): return lax.all_to_all(blocks, axis, 0, 0, tiled=False)  15.6 us
    all_to_all x3, waiting for transfers between devices, exchange(): return lax.all_to_all(blocks, axis, 0, 0, tiled=False)  13.3 us
  transfers between devices with their start and end apart: 11, of which 6 were waited for; matrix products, arithmetic and copies ran while one was open for 1% of the time, Pallas kernels for 1%

profile of v12, /device:TPU:1, one launch (start us, length us, event | category | flops | bytes accessed | tf_op | source)
XLA Modules:
  0.0 155.9 jit_solution(927099570297333455)
XLA Ops:
  0.7 0.9 copy-done.4
  1.6 0.7 copy-done.6
  2.2 0.7 shard_map.85
  2.9 8.8 %collective-permute-start = (bf16[8,576]{1,0:T(8,128)(2,1)S(1)}, bf16[8,576]{1,0:T(8,128)(2,1)S(1)}, u32[]{:S(2)}, u32[]{:S(2)}) collective-permute-start(bf16[8,576]{1,0:T(8,128)(2,1)S(1)} %get-tuple-element.15), channel_id=1, source_target_pairs={{0,32},{32,0},{1,33},{33,1},{2,34},{34,2},{3,35},{35,3},{4,36},{36... | collective-permute-start | bytes 27656 | tf_op jit(solution)/shard_map/ppermute | solution.py:25
  11.7 0.8 collective-permute-done.got_ref
  12.6 0.8 shard_map.86
  13.3 7.6 %all-to-all-start = ((bf16[32,8,576]{2,1,0:T(8,128)(2,1)}), bf16[32,8,576]{2,1,0:T(8,128)(2,1)S(1)}, u32[]{:S(2)}, u32[]{:S(2)}) async-start(bf16[32,8,576]{2,1,0:T(8,128)(2,1)} %get-tuple-element.16), calls=%async_computation | async-start | bytes 655360 | tf_op jit(solution)/shard_map/all_to_all | solution.py:21
  21.0 2.5 %collective-permute-start.3 = (bf16[288,1024]{1,0:T(8,128)(2,1)}, bf16[288,1024]{1,0:T(8,128)(2,1)S(1)}, u32[]{:S(2)}, u32[]{:S(2)}) collective-permute-start(bf16[288,1024]{1,0:T(8,128)(2,1)} %bitcast.16), channel_id=1, source_target_pairs={{0,32},{32,0},{1,33},{33,1},{2,34},{34,2},{3,35},{35,3},{4,36},{36... | collective-permute-start | bytes 1769480 | tf_op jit(solution)/shard_map/ppermute | solution.py:25
  23.5 1.9 %collective-permute-start.2 = (bf16[288,1024]{1,0:T(8,128)(2,1)}, bf16[288,1024]{1,0:T(8,128)(2,1)S(1)}, u32[]{:S(2)}, u32[]{:S(2)}) collective-permute-start(bf16[288,1024]{1,0:T(8,128)(2,1)} %enc_own.1), channel_id=1, source_target_pairs={{0,32},{32,0},{1,33},{33,1},{2,34},{34,2},{3,35},{35,3},{4,36},{36... | collective-permute-start | bytes 1769480 | tf_op jit(solution)/shard_map/ppermute | solution.py:25
  25.4 2.4 %collective-permute-start.1 = (f32[288]{0:T(512)}, f32[288]{0:T(512)S(1)}, u32[]{:S(2)}, u32[]{:S(2)}) collective-permute-start(f32[288]{0:T(512)} %param.11), channel_id=1, source_target_pairs={{0,32},{32,0},{1,33},{33,1},{2,34},{34,2},{3,35},{35,3},{4,36},{36... | collective-permute-start | bytes 3464 | tf_op jit(solution)/shard_map/ppermute | solution.py:25
  27.9 0.7 broadcast_in_dim.6
  29.0 2.5 %all-to-all-done = bf16[32,8,576]{2,1,0:T(8,128)(2,1)S(1)} async-done(((bf16[32,8,576]{2,1,0:T(8,128)(2,1)}), bf16[32,8,576]{2,1,0:T(8,128)(2,1)S(1)}, u32[]{:S(2)}, u32[]{:S(2)}) %all-to-all-start) | async-done | bytes 294944 | tf_op jit(solution)/shard_map/all_to_all | solution.py:21
  31.8 0.6 shard_map.87
  32.4 20.0 %all_to_all.35.blocks_ref.pre_ref = bf16[8,272,128]{2,1,0:T(8,128)(2,1)S(1)} all-to-all(bf16[8,272,128]{2,1,0:T(8,128)(2,1)S(1)} %shard_map.87), channel_id=1, replica_groups=mesh['y'=8,'core'=2,'x'=4,'z'=8] {'y'}, dimensions={0} | all-to-all | bytes 1114112 | tf_op jit(solution)/shard_map/all_to_all | solution.py:21
  52.4 1.0 shard_map.88
  53.4 3.8 %all-to-all-start.2 = ((bf16[8,256,128]{2,1,0:T(8,128)(2,1)}), bf16[8,256,128]{2,1,0:T(8,128)(2,1)S(1)}, u32[]{:S(2)}, u32[]{:S(2)}) async-start(bf16[8,256,128]{2,1,0:T(8,128)(2,1)} %shard_map.88), calls=%async_computation.2 | async-start | bytes 1048576 | tf_op jit(solution)/shard_map/all_to_all | solution.py:21
  57.2 1.1 copy-done.2
  58.7 10.8 %all-to-all-done.2.copies_ref = bf16[8,256,128]{2,1,0:T(8,128)(2,1)S(1)} async-done(((bf16[8,256,128]{2,1,0:T(8,128)(2,1)}), bf16[8,256,128]{2,1,0:T(8,128)(2,1)S(1)}, u32[]{:S(2)}, u32[]{:S(2)}) %all-to-all-start.2) | async-done | bytes 524320 | tf_op jit(solution)/shard_map/all_to_all | solution.py:21
  69.4 0.6 shard_map.90
  70.1 23.5 %all_to_all.36.blocks_ref = bf16[32,8,576]{2,1,0:T(8,128)(2,1)S(1)} all-to-all(bf16[32,8,576]{2,1,0:T(8,128)(2,1)S(1)} %shard_map.90), channel_id=1, replica_groups=mesh['y'=8,'core'=2,'x'=4,'z'=8] {'x','z'}, dimensions={0} | all-to-all | bytes 589824 | tf_op jit(solution)/shard_map/all_to_all | solution.py:21
  93.7 14.7 %all_to_all.37.error_ref = bf16[32,8,576]{2,1,0:T(8,128)(2,1)S(1)} all-to-all(bf16[32,8,576]{2,1,0:T(8,128)(2,1)S(1)} %shard_map.91), channel_id=1, replica_groups=mesh['y'=8,'core'=2,'x'=4,'z'=8] {'x','z'}, dimensions={0} | all-to-all | bytes 589824 | tf_op jit(solution)/shard_map/all_to_all | solution.py:21
  108.4 0.6 shard_map.92
  109.0 15.5 %all_to_all.38.blocks_ref = bf16[8,256,128]{2,1,0:T(8,128)(2,1)S(1)} all-to-all(bf16[8,256,128]{2,1,0:T(8,128)(2,1)S(1)} %shard_map.92), channel_id=1, replica_groups=mesh['y'=8,'core'=2,'x'=4,'z'=8] {'y'}, dimensions={0} | all-to-all | bytes 1048576 | tf_op jit(solution)/shard_map/all_to_all | solution.py:21
  124.5 1.1 shard_map.93
  125.5 4.2 %all-to-all-start.6 = ((bf16[8,272,128]{2,1,0:T(8,128)(2,1)}), bf16[8,272,128]{2,1,0:T(8,128)(2,1)}, u32[]{:S(2)}, u32[]{:S(2)}) async-start(bf16[8,272,128]{2,1,0:T(8,128)(2,1)} %shard_map.93), calls=%async_computation.6 | async-start | bytes 1114112 | tf_op jit(solution)/shard_map/all_to_all | solution.py:21
  129.9 8.9 %collective-permute-start.7 = (bf16[256,1024]{1,0:T(8,128)(2,1)S(1)}, bf16[256,1024]{1,0:T(8,128)(2,1)S(1)}, u32[]{:S(2)}, u32[]{:S(2)}) collective-permute-start(bf16[256,1024]{1,0:T(8,128)(2,1)S(1)} %shard_map.96), channel_id=1, source_target_pairs={{0,32},{32,0},{1,33},{33,1},{2,34},{34,2},{3,35},{35,3},{4,36},{36... | collective-permute-start | bytes 1572872 | tf_op jit(solution)/shard_map/ppermute | solution.py:25
  139.0 1.9 %collective-permute-start.5 = (bf16[288,256]{1,0:T(8,128)(2,1)S(1)}, bf16[288,256]{1,0:T(8,128)(2,1)S(1)}, u32[]{:S(2)}, u32[]{:S(2)}) collective-permute-start(bf16[288,256]{1,0:T(8,128)(2,1)S(1)} %get-tuple-element.21), channel_id=1, source_target_pairs={{0,32},{32,0},{1,33},{33,1},{2,34},{34,2},{3,35},{35,3},{4,36},{36... | collective-permute-start | bytes 442376 | tf_op jit(solution)/shard_map/ppermute | solution.py:25
  141.1 2.4 %collective-permute-start.6 = (bf16[256,288]{1,0:T(8,128)(2,1)S(1)}, bf16[256,288]{1,0:T(8,128)(2,1)S(1)}, u32[]{:S(2)}, u32[]{:S(2)}) collective-permute-start(bf16[256,288]{1,0:T(8,128)(2,1)S(1)} %slice.13), channel_id=1, source_target_pairs={{0,32},{32,0},{1,33},{33,1},{2,34},{34,2},{3,35},{35,3},{4,36},{36... | collective-permute-start | bytes 442376 | tf_op jit(solution)/shard_map/ppermute | solution.py:25
  143.9 0.7 collective-permute-done.6
  144.9 7.4 %collective-permute-start.4 = (bf16[8,272,128]{2,1,0:T(8,128)(2,1)}, bf16[8,272,128]{2,1,0:T(8,128)(2,1)S(1)}, u32[]{:S(2)}, u32[]{:S(2)}) collective-permute-start(bf16[8,272,128]{2,1,0:T(8,128)(2,1)} %all-to-all-done.6.own_ref), channel_id=1, source_target_pairs={{0,32},{32,0},{1,33},{33,1},{2,34},{34,2},{3,35},{35,3},{4,36},{36... | collective-permute-start | bytes 1671176 | tf_op jit(solution)/shard_map/ppermute | solution.py:25
  152.3 1.4 shard_map.95
  154.1 1.8 %shard_map.97 = (f32[288,1024]{1,0:T(8,128)}, f32[8,128]{1,0:T(8,128)}, f32[288,1024]{1,0:T(8,128)}) custom-call(bf16[8,272,128]{2,1,0:T(8,128)(2,1)S(1)} %collective-permute-done.4.its_ref, f32[288,1024]{1,0:T(8,128)S(1)} %get-tuple-element.19.part_ref, f32[24,128]{1,0:T(8,128)S(1)} %get-tuple-element.20.sums_ref, ...), custom_call_target="tpu_custom_call" | custom-call | flops 301989888 | bytes 6291456 | tf_op jit(solution)/shard_map/pallas_call | solution.py:374
  (30 shorter events, 2.7 us)
Async XLA Ops:
  0.6 30.9 %copy-start = (bf16[1024,288]{0,1:T(8,128)(2,1)S(1)}, bf16[1024,288]{0,1:T(8,128)(2,1)}, u32[]{:S(2)}) copy-start(bf16[1024,288]{0,1:T(8,128)(2,1)} %param.10) | copy-start | bytes 1769476
  0.6 0.9 copy-start.4
  1.6 0.7 copy-start.6
  2.9 9.6 %collective-permute-start = (bf16[8,576]{1,0:T(8,128)(2,1)S(1)}, bf16[8,576]{1,0:T(8,128)(2,1)S(1)}, u32[]{:S(2)}, u32[]{:S(2)}) collective-permute-start(bf16[8,576]{1,0:T(8,128)(2,1)S(1)} %get-tuple-element.15), channel_id=1, source_target_pairs={{0,32},{32,0},{1,33},{33,1},{2,34},{34,2},{3,35},{35,3},{4,36},{36... | collective-permute-start | bytes 27656 | tf_op jit(solution)/shard_map/ppermute | solution.py:25
  13.3 18.5 %copy-start.3 = (bf16[288,1024]{1,0:T(8,128)(2,1)S(1)}, bf16[288,1024]{1,0:T(8,128)(2,1)}, u32[]{:S(2)}) copy-start(bf16[288,1024]{1,0:T(8,128)(2,1)} %enc_own.1) | copy-start | bytes 1769476
  13.3 18.1 %all-to-all-start = ((bf16[32,8,576]{2,1,0:T(8,128)(2,1)}), bf16[32,8,576]{2,1,0:T(8,128)(2,1)S(1)}, u32[]{:S(2)}, u32[]{:S(2)}) async-start(bf16[32,8,576]{2,1,0:T(8,128)(2,1)} %get-tuple-element.16), calls=%async_computation | async-start | bytes 655360 | tf_op jit(solution)/shard_map/all_to_all | solution.py:21
  21.0 10.6 %collective-permute-start.3 = (bf16[288,1024]{1,0:T(8,128)(2,1)}, bf16[288,1024]{1,0:T(8,128)(2,1)S(1)}, u32[]{:S(2)}, u32[]{:S(2)}) collective-permute-start(bf16[288,1024]{1,0:T(8,128)(2,1)} %bitcast.16), channel_id=1, source_target_pairs={{0,32},{32,0},{1,33},{33,1},{2,34},{34,2},{3,35},{35,3},{4,36},{36... | collective-permute-start | bytes 1769480 | tf_op jit(solution)/shard_map/ppermute | solution.py:25
  23.5 8.3 %collective-permute-start.2 = (bf16[288,1024]{1,0:T(8,128)(2,1)}, bf16[288,1024]{1,0:T(8,128)(2,1)S(1)}, u32[]{:S(2)}, u32[]{:S(2)}) collective-permute-start(bf16[288,1024]{1,0:T(8,128)(2,1)} %enc_own.1), channel_id=1, source_target_pairs={{0,32},{32,0},{1,33},{33,1},{2,34},{34,2},{3,35},{35,3},{4,36},{36... | collective-permute-start | bytes 1769480 | tf_op jit(solution)/shard_map/ppermute | solution.py:25
  25.4 3.4 %collective-permute-start.1 = (f32[288]{0:T(512)}, f32[288]{0:T(512)S(1)}, u32[]{:S(2)}, u32[]{:S(2)}) collective-permute-start(f32[288]{0:T(512)} %param.11), channel_id=1, source_target_pairs={{0,32},{32,0},{1,33},{33,1},{2,34},{34,2},{3,35},{35,3},{4,36},{36... | collective-permute-start | bytes 3464 | tf_op jit(solution)/shard_map/ppermute | solution.py:25
  31.5 0.9 copy-start.1
  31.8 20.6 %copy-start.5 = (f32[1024]{0:T(1024)S(1)}, f32[1024]{0:T(1024)}, u32[]{:S(2)}) copy-start(f32[1024]{0:T(1024)} %param.9) | copy-start | bytes 12292
  53.4 16.1 %all-to-all-start.2 = ((bf16[8,256,128]{2,1,0:T(8,128)(2,1)}), bf16[8,256,128]{2,1,0:T(8,128)(2,1)S(1)}, u32[]{:S(2)}, u32[]{:S(2)}) async-start(bf16[8,256,128]{2,1,0:T(8,128)(2,1)} %shard_map.88), calls=%async_computation.2 | async-start | bytes 1048576 | tf_op jit(solution)/shard_map/all_to_all | solution.py:21
  57.2 1.1 copy-start.2
  125.5 19.4 %all-to-all-start.6 = ((bf16[8,272,128]{2,1,0:T(8,128)(2,1)}), bf16[8,272,128]{2,1,0:T(8,128)(2,1)}, u32[]{:S(2)}, u32[]{:S(2)}) async-start(bf16[8,272,128]{2,1,0:T(8,128)(2,1)} %shard_map.93), calls=%async_computation.6 | async-start | bytes 1114112 | tf_op jit(solution)/shard_map/all_to_all | solution.py:21
  129.9 14.0 %collective-permute-start.7 = (bf16[256,1024]{1,0:T(8,128)(2,1)S(1)}, bf16[256,1024]{1,0:T(8,128)(2,1)S(1)}, u32[]{:S(2)}, u32[]{:S(2)}) collective-permute-start(bf16[256,1024]{1,0:T(8,128)(2,1)S(1)} %shard_map.96), channel_id=1, source_target_pairs={{0,32},{32,0},{1,33},{33,1},{2,34},{34,2},{3,35},{35,3},{4,36},{36... | collective-permute-start | bytes 1572872 | tf_op jit(solution)/shard_map/ppermute | solution.py:25
  139.0 14.7 %collective-permute-start.5 = (bf16[288,256]{1,0:T(8,128)(2,1)S(1)}, bf16[288,256]{1,0:T(8,128)(2,1)S(1)}, u32[]{:S(2)}, u32[]{:S(2)}) collective-permute-start(bf16[288,256]{1,0:T(8,128)(2,1)S(1)} %get-tuple-element.21), channel_id=1, source_target_pairs={{0,32},{32,0},{1,33},{33,1},{2,34},{34,2},{3,35},{35,3},{4,36},{36... | collective-permute-start | bytes 442376 | tf_op jit(solution)/shard_map/ppermute | solution.py:25
  141.1 3.5 %collective-permute-start.6 = (bf16[256,288]{1,0:T(8,128)(2,1)S(1)}, bf16[256,288]{1,0:T(8,128)(2,1)S(1)}, u32[]{:S(2)}, u32[]{:S(2)}) collective-permute-start(bf16[256,288]{1,0:T(8,128)(2,1)S(1)} %slice.13), channel_id=1, source_target_pairs={{0,32},{32,0},{1,33},{33,1},{2,34},{34,2},{3,35},{35,3},{4,36},{36... | collective-permute-start | bytes 442376 | tf_op jit(solution)/shard_map/ppermute | solution.py:25
  144.9 9.2 %collective-permute-start.4 = (bf16[8,272,128]{2,1,0:T(8,128)(2,1)}, bf16[8,272,128]{2,1,0:T(8,128)(2,1)S(1)}, u32[]{:S(2)}, u32[]{:S(2)}) collective-permute-start(bf16[8,272,128]{2,1,0:T(8,128)(2,1)} %all-to-all-done.6.own_ref), channel_id=1, source_target_pairs={{0,32},{32,0},{1,33},{33,1},{2,34},{34,2},{3,35},{35,3},{4,36},{36... | collective-permute-start | bytes 1671176 | tf_op jit(solution)/shard_map/ppermute | solution.py:25

commit v13 on v10

--- a/solution.py
+++ b/solution.py
@@ -96,7 +96,7 @@
             ]
 
 
-def pre_kernel(centered_ref, enc_own, enc_other, squares_ref, out_ref, enc_ref):
+def pre_kernel(centered_ref, enc_own, enc_other, squares_ref, out_ref):
     width, latents = enc_own.shape
     step = 2 * LANES
     squares = squares_ref[...]
@@ -106,9 +106,9 @@
         out_ref[y, pl.ds(out_ref.shape[1] - parts.shape[0], parts.shape[0]), :] = parts
     for n in range(latents // step):
         lanes = pl.ds(n * step, step)
-        enc_ref[:width, lanes] = enc_own[:, lanes]
-        enc_ref[width:, lanes] = enc_other[:, lanes]
-        part = dot(centered_ref[...], enc_ref[:, lanes], ((1,), (0,)))
+        part = dot(centered_ref[:, :width], enc_own[:, lanes], ((1,), (0,))) + dot(
+            centered_ref[:, width:], enc_other[:, lanes], ((1,), (0,))
+        )
         spread(part.astype(BF16), out_ref, 2 * n)
 
 
@@ -327,7 +327,6 @@
         shape((count_y, size + extra, LANES), BF16),
         [VMEM] * 4,
         (matmul, moved),
-        [pltpu.VMEM((wide, latents), BF16)],
     )(centered, enc_weight, enc_other, squares.reshape(blocks_n, LANES))
     blocks = exchange(pre_blocks, "y")
     enc_bias = enc_bias.reshape(blocks_n, LANES)

time: 157 us -> 157 us (level)
  no operation moved by 1% of the time
where the time goes in v13:
time: 157 us
  blocking collectives  75 us (48%)
  starting transfers between devices  51 us (32%)
  waiting for transfers between devices  15.4 us (10%)
  Pallas kernels  9.61 us (6%)
  local copies, waits for them, and re-layouts  3.53 us (2%)
    all_to_all x4, blocking collectives, exchange(): return lax.all_to_all(blocks, axis, 0, 0, tiled=False)  75 us
    ppermute x8, starting transfers between devices, swap(): return lax.ppermute(block, 'core', [(0, 1), (1, 0)])  35.3 us
    all_to_all x3, starting transfers between devices, exchange(): return lax.all_to_all(blocks, axis, 0, 0, tiled=False)  15.7 us
    all_to_all x3, waiting for transfers between devices, exchange(): return lax.all_to_all(blocks, axis, 0, 0, tiled=False)  13.3 us
  transfers between devices with their start and end apart: 11, of which 6 were waited for; matrix products, arithmetic and copies ran while one was open for 1% of the time, Pallas kernels for 1%

profile of v13, /device:TPU:1, one launch (start us, length us, event | category | flops | bytes accessed | tf_op | source)
XLA Modules:
  0.0 156.5 jit_solution(14246916997370610602)
XLA Ops:
  0.7 0.9 copy-done.4
  1.6 0.7 copy-done.6
  2.2 0.8 shard_map.85
  3.0 8.8 %collective-permute-start = (bf16[8,576]{1,0:T(8,128)(2,1)S(1)}, bf16[8,576]{1,0:T(8,128)(2,1)S(1)}, u32[]{:S(2)}, u32[]{:S(2)}) collective-permute-start(bf16[8,576]{1,0:T(8,128)(2,1)S(1)} %get-tuple-element.15), channel_id=1, source_target_pairs={{0,32},{32,0},{1,33},{33,1},{2,34},{34,2},{3,35},{35,3},{4,36},{36... | collective-permute-start | bytes 27656 | tf_op jit(solution)/shard_map/ppermute | solution.py:25
  11.8 0.8 collective-permute-done.got_ref
  12.7 0.8 shard_map.86
  13.4 7.6 %all-to-all-start = ((bf16[32,8,576]{2,1,0:T(8,128)(2,1)}), bf16[32,8,576]{2,1,0:T(8,128)(2,1)S(1)}, u32[]{:S(2)}, u32[]{:S(2)}) async-start(bf16[32,8,576]{2,1,0:T(8,128)(2,1)} %get-tuple-element.16), calls=%async_computation | async-start | bytes 655360 | tf_op jit(solution)/shard_map/all_to_all | solution.py:21
  21.1 2.5 %collective-permute-start.3 = (bf16[288,1024]{1,0:T(8,128)(2,1)}, bf16[288,1024]{1,0:T(8,128)(2,1)S(1)}, u32[]{:S(2)}, u32[]{:S(2)}) collective-permute-start(bf16[288,1024]{1,0:T(8,128)(2,1)} %bitcast.16), channel_id=1, source_target_pairs={{0,32},{32,0},{1,33},{33,1},{2,34},{34,2},{3,35},{35,3},{4,36},{36... | collective-permute-start | bytes 1769480 | tf_op jit(solution)/shard_map/ppermute | solution.py:25
  23.6 1.9 %collective-permute-start.2 = (bf16[288,1024]{1,0:T(8,128)(2,1)}, bf16[288,1024]{1,0:T(8,128)(2,1)S(1)}, u32[]{:S(2)}, u32[]{:S(2)}) collective-permute-start(bf16[288,1024]{1,0:T(8,128)(2,1)} %enc_own.1), channel_id=1, source_target_pairs={{0,32},{32,0},{1,33},{33,1},{2,34},{34,2},{3,35},{35,3},{4,36},{36... | collective-permute-start | bytes 1769480 | tf_op jit(solution)/shard_map/ppermute | solution.py:25
  25.5 2.4 %collective-permute-start.1 = (f32[288]{0:T(512)}, f32[288]{0:T(512)S(1)}, u32[]{:S(2)}, u32[]{:S(2)}) collective-permute-start(f32[288]{0:T(512)} %param.11), channel_id=1, source_target_pairs={{0,32},{32,0},{1,33},{33,1},{2,34},{34,2},{3,35},{35,3},{4,36},{36... | collective-permute-start | bytes 3464 | tf_op jit(solution)/shard_map/ppermute | solution.py:25
  27.9 0.7 broadcast_in_dim.6
  29.1 2.5 %all-to-all-done = bf16[32,8,576]{2,1,0:T(8,128)(2,1)S(1)} async-done(((bf16[32,8,576]{2,1,0:T(8,128)(2,1)}), bf16[32,8,576]{2,1,0:T(8,128)(2,1)S(1)}, u32[]{:S(2)}, u32[]{:S(2)}) %all-to-all-start) | async-done | bytes 294944 | tf_op jit(solution)/shard_map/all_to_all | solution.py:21
  31.9 0.8 shard_map.87
  32.7 20.0 %all_to_all.35.blocks_ref.pre_ref = bf16[8,272,128]{2,1,0:T(8,128)(2,1)S(1)} all-to-all(bf16[8,272,128]{2,1,0:T(8,128)(2,1)S(1)} %shard_map.87), channel_id=1, replica_groups=mesh['y'=8,'core'=2,'x'=4,'z'=8] {'y'}, dimensions={0} | all-to-all | bytes 1114112 | tf_op jit(solution)/shard_map/all_to_all | solution.py:21
  52.7 1.0 shard_map.88
  53.7 3.8 %all-to-all-start.2 = ((bf16[8,256,128]{2,1,0:T(8,128)(2,1)}), bf16[8,256,128]{2,1,0:T(8,128)(2,1)S(1)}, u32[]{:S(2)}, u32[]{:S(2)}) async-start(bf16[8,256,128]{2,1,0:T(8,128)(2,1)} %shard_map.88), calls=%async_computation.2 | async-start | bytes 1048576 | tf_op jit(solution)/shard_map/all_to_all | solution.py:21
  57.5 1.1 copy-done.2
  59.0 10.8 %all-to-all-done.2.copies_ref = bf16[8,256,128]{2,1,0:T(8,128)(2,1)S(1)} async-done(((bf16[8,256,128]{2,1,0:T(8,128)(2,1)}), bf16[8,256,128]{2,1,0:T(8,128)(2,1)S(1)}, u32[]{:S(2)}, u32[]{:S(2)}) %all-to-all-start.2) | async-done | bytes 524320 | tf_op jit(solution)/shard_map/all_to_all | solution.py:21
  69.8 0.6 shard_map.90
  70.4 24.1 %all_to_all.36.blocks_ref = bf16[32,8,576]{2,1,0:T(8,128)(2,1)S(1)} all-to-all(bf16[32,8,576]{2,1,0:T(8,128)(2,1)S(1)} %shard_map.90), channel_id=1, replica_groups=mesh['y'=8,'core'=2,'x'=4,'z'=8] {'x','z'}, dimensions={0} | all-to-all | bytes 589824 | tf_op jit(solution)/shard_map/all_to_all | solution.py:21
  94.6 14.8 %all_to_all.37.error_ref = bf16[32,8,576]{2,1,0:T(8,128)(2,1)S(1)} all-to-all(bf16[32,8,576]{2,1,0:T(8,128)(2,1)S(1)} %shard_map.91), channel_id=1, replica_groups=mesh['y'=8,'core'=2,'x'=4,'z'=8] {'x','z'}, dimensions={0} | all-to-all | bytes 589824 | tf_op jit(solution)/shard_map/all_to_all | solution.py:21
  109.4 0.6 shard_map.92
  110.0 16.1 %all_to_all.38.blocks_ref = bf16[8,256,128]{2,1,0:T(8,128)(2,1)S(1)} all-to-all(bf16[8,256,128]{2,1,0:T(8,128)(2,1)S(1)} %shard_map.92), channel_id=1, replica_groups=mesh['y'=8,'core'=2,'x'=4,'z'=8] {'y'}, dimensions={0} | all-to-all | bytes 1048576 | tf_op jit(solution)/shard_map/all_to_all | solution.py:21
  126.1 1.1 shard_map.93
  127.2 4.2 %all-to-all-start.6 = ((bf16[8,272,128]{2,1,0:T(8,128)(2,1)}), bf16[8,272,128]{2,1,0:T(8,128)(2,1)}, u32[]{:S(2)}, u32[]{:S(2)}) async-start(bf16[8,272,128]{2,1,0:T(8,128)(2,1)} %shard_map.93), calls=%async_computation.6 | async-start | bytes 1114112 | tf_op jit(solution)/shard_map/all_to_all | solution.py:21
  131.5 7.9 %collective-permute-start.7 = (bf16[256,1024]{1,0:T(8,128)(2,1)S(1)}, bf16[256,1024]{1,0:T(8,128)(2,1)S(1)}, u32[]{:S(2)}, u32[]{:S(2)}) collective-permute-start(bf16[256,1024]{1,0:T(8,128)(2,1)S(1)} %shard_map.96), channel_id=1, source_target_pairs={{0,32},{32,0},{1,33},{33,1},{2,34},{34,2},{3,35},{35,3},{4,36},{36... | collective-permute-start | bytes 1572872 | tf_op jit(solution)/shard_map/ppermute | solution.py:25
  139.6 1.9 %collective-permute-start.5 = (bf16[288,256]{1,0:T(8,128)(2,1)S(1)}, bf16[288,256]{1,0:T(8,128)(2,1)S(1)}, u32[]{:S(2)}, u32[]{:S(2)}) collective-permute-start(bf16[288,256]{1,0:T(8,128)(2,1)S(1)} %get-tuple-element.21), channel_id=1, source_target_pairs={{0,32},{32,0},{1,33},{33,1},{2,34},{34,2},{3,35},{35,3},{4,36},{36... | collective-permute-start | bytes 442376 | tf_op jit(solution)/shard_map/ppermute | solution.py:25
  141.8 2.4 %collective-permute-start.6 = (bf16[256,288]{1,0:T(8,128)(2,1)S(1)}, bf16[256,288]{1,0:T(8,128)(2,1)S(1)}, u32[]{:S(2)}, u32[]{:S(2)}) collective-permute-start(bf16[256,288]{1,0:T(8,128)(2,1)S(1)} %slice.13), channel_id=1, source_target_pairs={{0,32},{32,0},{1,33},{33,1},{2,34},{34,2},{3,35},{35,3},{4,36},{36... | collective-permute-start | bytes 442376 | tf_op jit(solution)/shard_map/ppermute | solution.py:25
  144.5 0.7 collective-permute-done.6
  145.6 7.4 %collective-permute-start.4 = (bf16[8,272,128]{2,1,0:T(8,128)(2,1)}, bf16[8,272,128]{2,1,0:T(8,128)(2,1)S(1)}, u32[]{:S(2)}, u32[]{:S(2)}) collective-permute-start(bf16[8,272,128]{2,1,0:T(8,128)(2,1)} %all-to-all-done.6.own_ref), channel_id=1, source_target_pairs={{0,32},{32,0},{1,33},{33,1},{2,34},{34,2},{3,35},{35,3},{4,36},{36... | collective-permute-start | bytes 1671176 | tf_op jit(solution)/shard_map/ppermute | solution.py:25
  153.0 1.4 shard_map.95
  154.7 1.8 %shard_map.97 = (f32[288,1024]{1,0:T(8,128)}, f32[8,128]{1,0:T(8,128)}, f32[288,1024]{1,0:T(8,128)}) custom-call(bf16[8,272,128]{2,1,0:T(8,128)(2,1)S(1)} %collective-permute-done.4.its_ref, f32[288,1024]{1,0:T(8,128)S(1)} %get-tuple-element.19.part_ref, f32[24,128]{1,0:T(8,128)S(1)} %get-tuple-element.20.sums_ref, ...), custom_call_target="tpu_custom_call" | custom-call | flops 301989888 | bytes 6291456 | tf_op jit(solution)/shard_map/pallas_call | solution.py:384
  (30 shorter events, 2.7 us)
Async XLA Ops:
  0.6 31.0 %copy-start = (bf16[1024,288]{0,1:T(8,128)(2,1)S(1)}, bf16[1024,288]{0,1:T(8,128)(2,1)}, u32[]{:S(2)}) copy-start(bf16[1024,288]{0,1:T(8,128)(2,1)} %param.10) | copy-start | bytes 1769476
  0.6 0.9 copy-start.4
  1.6 0.7 copy-start.6
  3.0 9.6 %collective-permute-start = (bf16[8,576]{1,0:T(8,128)(2,1)S(1)}, bf16[8,576]{1,0:T(8,128)(2,1)S(1)}, u32[]{:S(2)}, u32[]{:S(2)}) collective-permute-start(bf16[8,576]{1,0:T(8,128)(2,1)S(1)} %get-tuple-element.15), channel_id=1, source_target_pairs={{0,32},{32,0},{1,33},{33,1},{2,34},{34,2},{3,35},{35,3},{4,36},{36... | collective-permute-start | bytes 27656 | tf_op jit(solution)/shard_map/ppermute | solution.py:25
  13.4 18.5 %copy-start.3 = (bf16[288,1024]{1,0:T(8,128)(2,1)S(1)}, bf16[288,1024]{1,0:T(8,128)(2,1)}, u32[]{:S(2)}) copy-start(bf16[288,1024]{1,0:T(8,128)(2,1)} %enc_own.1) | copy-start | bytes 1769476
  13.4 18.1 %all-to-all-start = ((bf16[32,8,576]{2,1,0:T(8,128)(2,1)}), bf16[32,8,576]{2,1,0:T(8,128)(2,1)S(1)}, u32[]{:S(2)}, u32[]{:S(2)}) async-start(bf16[32,8,576]{2,1,0:T(8,128)(2,1)} %get-tuple-element.16), calls=%async_computation | async-start | bytes 655360 | tf_op jit(solution)/shard_map/all_to_all | solution.py:21
  21.1 10.6 %collective-permute-start.3 = (bf16[288,1024]{1,0:T(8,128)(2,1)}, bf16[288,1024]{1,0:T(8,128)(2,1)S(1)}, u32[]{:S(2)}, u32[]{:S(2)}) collective-permute-start(bf16[288,1024]{1,0:T(8,128)(2,1)} %bitcast.16), channel_id=1, source_target_pairs={{0,32},{32,0},{1,33},{33,1},{2,34},{34,2},{3,35},{35,3},{4,36},{36... | collective-permute-start | bytes 1769480 | tf_op jit(solution)/shard_map/ppermute | solution.py:25
  23.6 8.3 %collective-permute-start.2 = (bf16[288,1024]{1,0:T(8,128)(2,1)}, bf16[288,1024]{1,0:T(8,128)(2,1)S(1)}, u32[]{:S(2)}, u32[]{:S(2)}) collective-permute-start(bf16[288,1024]{1,0:T(8,128)(2,1)} %enc_own.1), channel_id=1, source_target_pairs={{0,32},{32,0},{1,33},{33,1},{2,34},{34,2},{3,35},{35,3},{4,36},{36... | collective-permute-start | bytes 1769480 | tf_op jit(solution)/shard_map/ppermute | solution.py:25
  25.5 3.4 %collective-permute-start.1 = (f32[288]{0:T(512)}, f32[288]{0:T(512)S(1)}, u32[]{:S(2)}, u32[]{:S(2)}) collective-permute-start(f32[288]{0:T(512)} %param.11), channel_id=1, source_target_pairs={{0,32},{32,0},{1,33},{33,1},{2,34},{34,2},{3,35},{35,3},{4,36},{36... | collective-permute-start | bytes 3464 | tf_op jit(solution)/shard_map/ppermute | solution.py:25
  31.6 1.1 copy-start.1
  31.9 20.8 %copy-start.5 = (f32[1024]{0:T(1024)S(1)}, f32[1024]{0:T(1024)}, u32[]{:S(2)}) copy-start(f32[1024]{0:T(1024)} %param.9) | copy-start | bytes 12292
  53.7 16.1 %all-to-all-start.2 = ((bf16[8,256,128]{2,1,0:T(8,128)(2,1)}), bf16[8,256,128]{2,1,0:T(8,128)(2,1)S(1)}, u32[]{:S(2)}, u32[]{:S(2)}) async-start(bf16[8,256,128]{2,1,0:T(8,128)(2,1)} %shard_map.88), calls=%async_computation.2 | async-start | bytes 1048576 | tf_op jit(solution)/shard_map/all_to_all | solution.py:21
  57.5 1.1 copy-start.2
  127.2 18.4 %all-to-all-start.6 = ((bf16[8,272,128]{2,1,0:T(8,128)(2,1)}), bf16[8,272,128]{2,1,0:T(8,128)(2,1)}, u32[]{:S(2)}, u32[]{:S(2)}) async-start(bf16[8,272,128]{2,1,0:T(8,128)(2,1)} %shard_map.93), calls=%async_computation.6 | async-start | bytes 1114112 | tf_op jit(solution)/shard_map/all_to_all | solution.py:21
  131.5 13.0 %collective-permute-start.7 = (bf16[256,1024]{1,0:T(8,128)(2,1)S(1)}, bf16[256,1024]{1,0:T(8,128)(2,1)S(1)}, u32[]{:S(2)}, u32[]{:S(2)}) collective-permute-start(bf16[256,1024]{1,0:T(8,128)(2,1)S(1)} %shard_map.96), channel_id=1, source_target_pairs={{0,32},{32,0},{1,33},{33,1},{2,34},{34,2},{3,35},{35,3},{4,36},{36... | collective-permute-start | bytes 1572872 | tf_op jit(solution)/shard_map/ppermute | solution.py:25
  139.6 14.7 %collective-permute-start.5 = (bf16[288,256]{1,0:T(8,128)(2,1)S(1)}, bf16[288,256]{1,0:T(8,128)(2,1)S(1)}, u32[]{:S(2)}, u32[]{:S(2)}) collective-permute-start(bf16[288,256]{1,0:T(8,128)(2,1)S(1)} %get-tuple-element.21), channel_id=1, source_target_pairs={{0,32},{32,0},{1,33},{33,1},{2,34},{34,2},{3,35},{35,3},{4,36},{36... | collective-permute-start | bytes 442376 | tf_op jit(solution)/shard_map/ppermute | solution.py:25
  141.8 3.5 %collective-permute-start.6 = (bf16[256,288]{1,0:T(8,128)(2,1)S(1)}, bf16[256,288]{1,0:T(8,128)(2,1)S(1)}, u32[]{:S(2)}, u32[]{:S(2)}) collective-permute-start(bf16[256,288]{1,0:T(8,128)(2,1)S(1)} %slice.13), channel_id=1, source_target_pairs={{0,32},{32,0},{1,33},{33,1},{2,34},{34,2},{3,35},{35,3},{4,36},{36... | collective-permute-start | bytes 442376 | tf_op jit(solution)/shard_map/ppermute | solution.py:25
  145.6 9.2 %collective-permute-start.4 = (bf16[8,272,128]{2,1,0:T(8,128)(2,1)}, bf16[8,272,128]{2,1,0:T(8,128)(2,1)S(1)}, u32[]{:S(2)}, u32[]{:S(2)}) collective-permute-start(bf16[8,272,128]{2,1,0:T(8,128)(2,1)} %all-to-all-done.6.own_ref), channel_id=1, source_target_pairs={{0,32},{32,0},{1,33},{33,1},{2,34},{34,2},{3,35},{35,3},{4,36},{36... | collective-permute-start | bytes 1671176 | tf_op jit(solution)/shard_map/ppermute | solution.py:25
